TPU v7x, 512 devices: a whole 4x8x8 slice. The times are simulated.
512 devices in a mesh: dp: 64 (over x, z, core), tensor: 8 (over y).
Axes of the slice: x: 4, y: 8, z: 8, core: 2. Of those that a mesh axis runs over, the one named last changes fastest.
Arguments:
- tokens: bfloat16 [2, 4096, 8192], P(None, 'dp'), may hold values from -6 to 6
- value_matrix: bfloat16 [8192, 1024], P(None, 'tensor'), may hold values from -0.0625 to 0.0625
- adapter_down_weight: bfloat16 [256, 8192, 64], P('dp', 'tensor'), may hold values from -0.0625 to 0.0625
- adapter_up_weight: bfloat16 [256, 64, 1024], P('dp', None, 'tensor'), may hold values from -0.75 to 0.75
- adapter_index: int32 [2, 4096], P(None, 'dp'), may hold values from 0 to 255, as said below
Outputs:
- values: bfloat16 [2, 4096, 1024], P(None, 'dp', 'tensor')
Inputs may be any that keep to these rules, and one draw needn't show every extreme that they name: `adapter_index`: adapter a is owned by dp shard a // 4. Of the 64 rows of one dp shard in one group, at most 2 use adapters of one owner, and in each group one owner takes exactly 2 rows from every dp shard.
All inputs are finite; a program needn't handle non-finite values.
Results may differ from a plain program's by a relative error of at most 0.0038.
Values may be sent and summed in bfloat16 or wider, within the bound.
No kernel may reach another device: no remote copies, remote signals or barrier semaphores. Data moves between devices by JAX's collectives and lax.ppermute only.
A program may use at most 64 MiB of HBM per device.

v0:
```python
import jax
import jax.numpy as jnp
from jax import lax
from jax.sharding import PartitionSpec as P


def route_rows(chosen, sliced_rows, adapters_per_owner, group_list, slot_capacity):
    owners = chosen // adapters_per_owner
    owner_hits = (owners[:, None] == jnp.arange(group_list, dtype=jnp.int32)[None, :]).astype(
        jnp.int32
    )
    before = jnp.cumsum(owner_hits, axis=0) - owner_hits
    position = jnp.sum(owner_hits * before, axis=1)
    target_slot = owners * slot_capacity + position
    select = (
        target_slot[None, :] == jnp.arange(group_list * slot_capacity, dtype=jnp.int32)[:, None]
    )
    outgoing = jnp.dot(
        select.astype(jnp.bfloat16), sliced_rows, preferred_element_type=jnp.float32
    ).astype(jnp.bfloat16)
    local_plus = chosen % adapters_per_owner + 1
    slot_labels = jnp.sum(jnp.where(select, local_plus[None, :], 0), axis=1) - 1
    return (
        outgoing.reshape(group_list, slot_capacity, -1),
        slot_labels.reshape(group_list, slot_capacity),
        target_slot,
    )


def shrink_slot_rows(received_rows, slot_labels, adapter_down_weight):
    flattened_rows = received_rows.reshape(-1, received_rows.shape[-1])
    flattened_labels = slot_labels.reshape(-1)
    adapter_matches = (
        flattened_labels[None, :]
        == jnp.arange(adapter_down_weight.shape[0], dtype=jnp.int32)[:, None]
    ).astype(jnp.float32)
    partial_all = jnp.einsum(
        "px,qxg->qpg", flattened_rows, adapter_down_weight, preferred_element_type=jnp.float32
    )
    return (jnp.sum(partial_all * adapter_matches[:, :, None], axis=0), adapter_matches)


def expand_slot_rows(shrunk_output, adapter_matches, adapter_up_weight):
    expanded_output = jnp.einsum(
        "yh,rho->ryo", shrunk_output, adapter_up_weight, preferred_element_type=jnp.float32
    )
    return jnp.sum(expanded_output * adapter_matches[:, :, None], axis=0)


def on_device(tokens, value_matrix, adapter_down_weight, adapter_up_weight, adapter_index):
    micro_count, rows_local, features = tokens.shape
    group_list = lax.axis_size("dp")
    slot_capacity = 2 * ((rows_local + group_list - 1) // group_list)
    adapters_per_owner, column_slice_width, rank_width = adapter_down_weight.shape
    slice_start = lax.axis_index("tensor") * column_slice_width
    sliced = lax.dynamic_slice_in_dim(tokens, slice_start, column_slice_width, 2)
    base_output = jnp.einsum(
        "mrd,dc->mrc", tokens, value_matrix, preferred_element_type=jnp.float32
    )
    routed = [
        route_rows(
            adapter_index[member], sliced[member], adapters_per_owner, group_list, slot_capacity
        )
        for member in range(micro_count)
    ]
    arrivals = []
    for member in range(micro_count):
        received_rows, slot_labels = (
            lax.all_to_all(routed[member][0], "dp", split_axis=0, concat_axis=0, tiled=True),
            lax.all_to_all(routed[member][1], "dp", split_axis=0, concat_axis=0, tiled=True),
        )
        partial_value_sum, adapter_matches = shrink_slot_rows(
            received_rows, slot_labels, adapter_down_weight
        )
        shrunk_output = lax.psum(partial_value_sum, "tensor").astype(jnp.bfloat16)
        returned_rows = expand_slot_rows(shrunk_output, adapter_matches, adapter_up_weight).reshape(
            group_list, slot_capacity, -1
        )
        arrived = lax.all_to_all(returned_rows, "dp", split_axis=0, concat_axis=0, tiled=True)
        arrivals.append(arrived.reshape(group_list * slot_capacity, -1))
    adapter_rows = jnp.stack(
        [jnp.take(arrivals[member], routed[member][2], axis=0) for member in range(micro_count)]
    )
    return (base_output + adapter_rows).astype(jnp.bfloat16)


def solution(mesh):
    in_specs = (
        P(None, "dp", None),
        P(None, "tensor"),
        P("dp", "tensor", None),
        P("dp", None, "tensor"),
        P(None, "dp"),
    )
    out_specs = P(None, "dp", "tensor")
    return jax.shard_map(
        on_device, mesh=mesh, in_specs=in_specs, out_specs=out_specs, check_vma=False
    )
```

profile of v0, /device:TPU:1, one launch (start us, length us, event | category | flops | bytes accessed | tf_op | source)
XLA Modules:
  0.0 142.7 jit_solution(12712249678464949549)
XLA Ops:
  0.0 0.0 copy-start
  0.0 0.0 copy-start.1
  0.0 0.9 and_select_fusion.4
  0.9 0.7 fusion.23
  1.6 0.1 fusion.13
  1.6 0.1 fusion.12
  1.7 0.1 reduce_window_sum.17
  1.8 0.1 reduce_window_sum.18
  1.9 0.2 select_reduce_fusion.1
  2.1 0.8 fusion.26
  2.9 0.1 select_reduce_fusion
  3.0 0.8 sub.39
  3.7 14.8 %all-to-all-start.4 = ((s32[64,1,2]{2,1,0:T(1,128)}), s32[64,1,2]{2,1,0:T(1,128)S(1)}, u32[]{:S(2)}, u32[]{:S(2)}) async-start(s32[64,1,2]{2,1,0:T(1,128)} %bitcast.25), calls=%async_computation.4 | async-start | bytes 65536 | tf_op jit(solution)/shard_map/all_to_all | solution.py:70
  18.6 0.1 select_reduce_fusion.2
  18.7 0.0 copy-done
  18.7 0.3 convolution_convert_fusion.1
  19.0 0.7 sub.34
  19.8 8.0 %all-to-all-done.4 = s32[64,1,2]{2,1,0:T(1,128)S(1)} async-done(((s32[64,1,2]{2,1,0:T(1,128)}), s32[64,1,2]{2,1,0:T(1,128)S(1)}, u32[]{:S(2)}, u32[]{:S(2)}) %all-to-all-start.4) | async-done | bytes 544 | tf_op jit(solution)/shard_map/all_to_all | solution.py:70
  27.8 4.7 %all-to-all-start.1 = ((s32[64,1,2]{2,1,0:T(1,128)}), s32[64,1,2]{2,1,0:T(1,128)S(1)}, u32[]{:S(2)}, u32[]{:S(2)}) async-start(s32[64,1,2]{2,1,0:T(1,128)} %bitcast.10), calls=%async_computation.1 | async-start | bytes 65536 | tf_op jit(solution)/shard_map/all_to_all | solution.py:70
  32.5 0.3 convolution_convert_fusion
  32.9 0.8 reshape.169
  33.7 0.8 reshape.165
  34.5 7.5 %all-to-all-done.1 = s32[64,1,2]{2,1,0:T(1,128)S(1)} async-done(((s32[64,1,2]{2,1,0:T(1,128)}), s32[64,1,2]{2,1,0:T(1,128)S(1)}, u32[]{:S(2)}, u32[]{:S(2)}) %all-to-all-start.1) | async-done | bytes 544 | tf_op jit(solution)/shard_map/all_to_all | solution.py:70
  41.9 4.7 %all-to-all-start.3 = ((bf16[64,2,1024]{2,1,0:T(2,128)(2,1)}), bf16[64,2,1024]{2,1,0:T(2,128)(2,1)S(1)}, u32[]{:S(2)}, u32[]{:S(2)}) async-start(bf16[64,2,1024]{2,1,0:T(2,128)(2,1)} %reshape.169), calls=%async_computation.3 | async-start | bytes 524288 | tf_op jit(solution)/shard_map/all_to_all | solution.py:69
  46.6 0.0 copy-start.2
  46.7 0.5 broadcast.202
  47.2 0.7 reduce.6
  47.9 0.1 eq.115
  48.1 10.6 %all-to-all-done.3 = bf16[64,2,1024]{2,1,0:T(2,128)(2,1)S(1)} async-done(((bf16[64,2,1024]{2,1,0:T(2,128)(2,1)}), bf16[64,2,1024]{2,1,0:T(2,128)(2,1)S(1)}, u32[]{:S(2)}, u32[]{:S(2)}) %all-to-all-start.3) | async-done | bytes 262176 | tf_op jit(solution)/shard_map/all_to_all | solution.py:69
  58.7 6.1 %all-to-all-start = ((bf16[64,2,1024]{2,1,0:T(2,128)(2,1)}), bf16[64,2,1024]{2,1,0:T(2,128)(2,1)S(1)}, u32[]{:S(2)}, u32[]{:S(2)}) async-start(bf16[64,2,1024]{2,1,0:T(2,128)(2,1)} %reshape.165), calls=%async_computation | async-start | bytes 524288 | tf_op jit(solution)/shard_map/all_to_all | solution.py:69
  64.8 0.7 reduce.7
  65.5 0.1 eq.104
  65.7 0.1 reshape.170
  65.8 0.0 copy-done.1
  65.8 0.3 fusion.31
  66.1 10.7 %all-to-all-done = bf16[64,2,1024]{2,1,0:T(2,128)(2,1)S(1)} async-done(((bf16[64,2,1024]{2,1,0:T(2,128)(2,1)}), bf16[64,2,1024]{2,1,0:T(2,128)(2,1)S(1)}, u32[]{:S(2)}, u32[]{:S(2)}) %all-to-all-start) | async-done | bytes 262176 | tf_op jit(solution)/shard_map/all_to_all | solution.py:69
  76.8 0.1 reshape.166
  76.9 0.3 fusion.30
  77.2 24.0 %all-reduce = (bf16[128,64]{0,1:T(8,128)(2,1)S(1)}, bf16[128,64]{0,1:T(8,128)(2,1)S(1)}) all-reduce(f32[128,64]{0,1:T(8,128)S(1)} %multiply_reduce_fusion, f32[128,64]{0,1:T(8,128)S(1)} %multiply_reduce_fusion.1), channel_id=1, replica_groups=mesh['dp'=64,'tensor'=8] {'tensor'}, use_global_device_ids=true, to_apply=%region_10.12 | all-reduce | flops 16384 | bytes 98304 | tf_op jit(solution)/shard_map/psum | solution.py:75
  101.2 0.0 copy-done.2
  101.2 0.8 fusion.4
  102.0 13.0 %all-to-all-start.2 = ((f32[64,2,128]{2,1,0:T(2,128)}), f32[64,2,128]{2,1,0:T(2,128)S(1)}, u32[]{:S(2)}, u32[]{:S(2)}) async-start(f32[64,2,128]{2,1,0:T(2,128)} %bitcast.13), calls=%async_computation.2 | async-start | bytes 131072 | tf_op jit(solution)/shard_map/all_to_all | solution.py:79
  115.0 0.8 fusion.5
  115.9 8.9 %all-to-all-done.2 = f32[64,2,128]{2,1,0:T(2,128)S(1)} async-done(((f32[64,2,128]{2,1,0:T(2,128)}), f32[64,2,128]{2,1,0:T(2,128)S(1)}, u32[]{:S(2)}, u32[]{:S(2)}) %all-to-all-start.2) | async-done | bytes 65568 | tf_op jit(solution)/shard_map/all_to_all | solution.py:79
  124.8 4.4 %all-to-all-start.5 = ((f32[64,2,128]{2,1,0:T(2,128)}), f32[64,2,128]{2,1,0:T(2,128)S(1)}, u32[]{:S(2)}, u32[]{:S(2)}) async-start(f32[64,2,128]{2,1,0:T(2,128)} %bitcast.28), calls=%async_computation.5 | async-start | bytes 131072 | tf_op jit(solution)/shard_map/all_to_all | solution.py:79
  129.3 0.6 gather_fusion
  129.9 0.1 select_bitcast_fusion.1
  129.9 9.2 %all-to-all-done.5 = f32[64,2,128]{2,1,0:T(2,128)S(1)} async-done(((f32[64,2,128]{2,1,0:T(2,128)}), f32[64,2,128]{2,1,0:T(2,128)S(1)}, u32[]{:S(2)}, u32[]{:S(2)}) %all-to-all-start.5) | async-done | bytes 65568 | tf_op jit(solution)/shard_map/all_to_all | solution.py:79
  139.2 0.6 gather_fusion.1
  139.7 0.1 select_bitcast_fusion
  139.8 2.9 %fusion.9 = bf16[2,64,128]{2,1,0:T(8,128)(2,1)} fusion(bf16[2,64,8192]{2,1,0:T(8,128)(2,1)S(1)} %copy-done, bf16[8192,128]{1,0:T(8,128)(2,1)} %param.8, f32[1,64,128]{2,1,0:T(8,128)S(1)} %select_bitcast_fusion, f32[1,64,128]{2,1,0:T(8,128)S(1)} %select_bitcast_fusion.1), kind=kOutput, calls=%fused_computation.13 | convolution fusion | flops 268484608 | bytes 4292608 | tf_op jit(solution)/shard_map/mrd,dc->mrc/dot_general | solution.py:57
  (11 shorter events, 0.1 us)
Async XLA Ops:
  0.0 18.7 %copy-start = (bf16[2,64,8192]{2,1,0:T(8,128)(2,1)S(1)}, bf16[2,64,8192]{2,1,0:T(8,128)(2,1)}, u32[]{:S(2)}) copy-start(bf16[2,64,8192]{2,1,0:T(8,128)(2,1)} %param.7) | copy-start | bytes 6291460
  0.0 65.8 %copy-start.1 = (bf16[4,1024,64]{1,2,0:T(8,128)(2,1)S(1)}, bf16[4,1024,64]{1,2,0:T(8,128)(2,1)}, u32[]{:S(2)}) copy-start(bf16[4,1024,64]{1,2,0:T(8,128)(2,1)} %param.9) | copy-start | bytes 1572868
  3.7 24.1 %all-to-all-start.4 = ((s32[64,1,2]{2,1,0:T(1,128)}), s32[64,1,2]{2,1,0:T(1,128)S(1)}, u32[]{:S(2)}, u32[]{:S(2)}) async-start(s32[64,1,2]{2,1,0:T(1,128)} %bitcast.25), calls=%async_computation.4 | async-start | bytes 65536 | tf_op jit(solution)/shard_map/all_to_all | solution.py:70
  27.8 14.1 %all-to-all-start.1 = ((s32[64,1,2]{2,1,0:T(1,128)}), s32[64,1,2]{2,1,0:T(1,128)S(1)}, u32[]{:S(2)}, u32[]{:S(2)}) async-start(s32[64,1,2]{2,1,0:T(1,128)} %bitcast.10), calls=%async_computation.1 | async-start | bytes 65536 | tf_op jit(solution)/shard_map/all_to_all | solution.py:70
  41.9 16.7 %all-to-all-start.3 = ((bf16[64,2,1024]{2,1,0:T(2,128)(2,1)}), bf16[64,2,1024]{2,1,0:T(2,128)(2,1)S(1)}, u32[]{:S(2)}, u32[]{:S(2)}) async-start(bf16[64,2,1024]{2,1,0:T(2,128)(2,1)} %reshape.169), calls=%async_computation.3 | async-start | bytes 524288 | tf_op jit(solution)/shard_map/all_to_all | solution.py:69
  46.6 54.6 %copy-start.2 = (bf16[4,64,128]{2,1,0:T(8,128)(2,1)S(1)}, bf16[4,64,128]{2,1,0:T(8,128)(2,1)}, u32[]{:S(2)}) copy-start(bf16[4,64,128]{2,1,0:T(8,128)(2,1)} %param.10) | copy-start | bytes 196612
  58.7 18.1 %all-to-all-start = ((bf16[64,2,1024]{2,1,0:T(2,128)(2,1)}), bf16[64,2,1024]{2,1,0:T(2,128)(2,1)S(1)}, u32[]{:S(2)}, u32[]{:S(2)}) async-start(bf16[64,2,1024]{2,1,0:T(2,128)(2,1)} %reshape.165), calls=%async_computation | async-start | bytes 524288 | tf_op jit(solution)/shard_map/all_to_all | solution.py:69
  102.0 22.8 %all-to-all-start.2 = ((f32[64,2,128]{2,1,0:T(2,128)}), f32[64,2,128]{2,1,0:T(2,128)S(1)}, u32[]{:S(2)}, u32[]{:S(2)}) async-start(f32[64,2,128]{2,1,0:T(2,128)} %bitcast.13), calls=%async_computation.2 | async-start | bytes 131072 | tf_op jit(solution)/shard_map/all_to_all | solution.py:79
  124.8 14.3 %all-to-all-start.5 = ((f32[64,2,128]{2,1,0:T(2,128)}), f32[64,2,128]{2,1,0:T(2,128)S(1)}, u32[]{:S(2)}, u32[]{:S(2)}) async-start(f32[64,2,128]{2,1,0:T(2,128)} %bitcast.28), calls=%async_computation.5 | async-start | bytes 131072 | tf_op jit(solution)/shard_map/all_to_all | solution.py:79
where the time goes:
time: 143 us
  waiting for transfers between devices  54.9 us (38%)
  starting transfers between devices  47.8 us (33%)
  blocking collectives  24 us (17%)
  matrix products  5.85 us (4%)
  local copies, waits for them, and re-layouts  5.29 us (4%)
  other arithmetic  4.72 us (3%)
    psum x1, blocking collectives, on_device(): shrunk_output = lax.psum(partial_value_sum, 'tensor').astype(jnp.bfloat16)  24 us
    all_to_all x2, waiting for transfers between devices, on_device(): lax.all_to_all(routed[member][0], 'dp', split_axis=0, concat_axis=0, tile...  21.3 us
    all_to_all x2, starting transfers between devices, on_device(): lax.all_to_all(routed[member][1], 'dp', split_axis=0, concat_axis=0, tile...  19.6 us
    all_to_all x2, waiting for transfers between devices, on_device(): lax.all_to_all(returned_rows, 'dp', split_axis=0, concat_axis=0, tiled=True)  18.2 us
    all_to_all x2, starting transfers between devices, on_device(): lax.all_to_all(returned_rows, 'dp', split_axis=0, concat_axis=0, tiled=True)  17.4 us
    all_to_all x2, waiting for transfers between devices, on_device(): lax.all_to_all(routed[member][1], 'dp', split_axis=0, concat_axis=0, tile...  15.5 us
    all_to_all x2, starting transfers between devices, on_device(): lax.all_to_all(routed[member][0], 'dp', split_axis=0, concat_axis=0, tile...  10.8 us
    dot_general x1, matrix products, on_device(): jnp.einsum('mrd,dc->mrc', tokens, value_matrix, preferred_element_type=jn...  2.91 us
  transfers between devices with their start and end apart: 6, of which 6 were waited for; matrix products, arithmetic and copies ran while one was open for 5% of the time, Pallas kernels for 0%

commit v1 on v0

v1 whole, which is shorter than its diff:
```python
import functools

import jax
import jax.numpy as jnp
from jax import lax
from jax.experimental import pallas as pl
from jax.experimental.pallas import tpu as pltpu
from jax.sharding import PartitionSpec as P

BF16, F32, I32 = jnp.bfloat16, jnp.float32, jnp.int32
VMEM_LIMIT = 40 * 1024 * 1024


def iota(shape, dim):
    return lax.broadcasted_iota(I32, shape, dim)


def slots_of(index_row, owned, slots):
    rows = index_row.shape[1]
    wide = jnp.broadcast_to(index_row, (rows, rows))
    line, column = iota((rows, rows), 0), iota((rows, rows), 1)
    index_col = jnp.sum(jnp.where(line == column, wide, 0), axis=1, keepdims=True)
    half = rows // 2
    same_group = (line >= half) == (column >= half)
    same = (wide // owned == index_col // owned) & same_group
    before = jnp.sum(jnp.where(same & (line < column), 1, 0), axis=0, keepdims=True)
    before_col = jnp.sum(jnp.where(same & (column < line), 1, 0), axis=1, keepdims=True)
    group_row = jnp.where(iota((1, rows), 1) >= half, 2, 0)
    group_col = jnp.where(iota((rows, 1), 0) >= half, 2, 0)
    return group_row + before, group_col + before_col, index_col


def pack_kernel(owned, owners, index_ref, tokens_ref, out_ref, held, sem):
    width = held.shape[2]
    start = pl.multiple_of(lax.axis_index("tensor") * width, width)
    copy = pltpu.make_async_copy(tokens_ref.at[:, :, pl.ds(start, width)], held, sem)
    copy.start()
    index_row = index_ref[...]
    rows = index_row.shape[1]
    slot, _, index_col = slots_of(index_row, owned, 4)
    target = index_row // owned * 8 + slot
    both = jnp.concatenate([target, target + 4], axis=1)
    lines = owners * 8
    select = jnp.where(iota((lines, 2 * rows), 0) == both, 1.0, 0.0).astype(BF16)
    label = jnp.broadcast_to((index_col % owned + 1).astype(F32), (rows, 128)).astype(BF16)
    labels = jnp.concatenate([label, label], axis=0)
    half = width // 2
    out_ref[:, half:] = jnp.dot(select, labels, preferred_element_type=F32).astype(BF16)
    copy.wait()
    tokens = held[...].reshape(rows, width)
    halves = jnp.concatenate([tokens[:, :half], tokens[:, half:]], axis=0)
    out_ref[:, :half] = jnp.dot(select, halves, preferred_element_type=F32).astype(BF16)


def pair_up(lines):
    by_shard = lines.reshape(2, lines.shape[0] // 32, 2, 8, 128)
    low = iota((lines.shape[0] // 32, 8, 128), 1) < 4
    return [
        jnp.where(low, by_shard[e, :, 0], by_shard[e, :, 1]).reshape(lines.shape[0] // 4, 128)
        for e in range(2)
    ]


def shrink_kernel(received_ref, down_ref, partial_ref, label_ref):
    lines = received_ref.shape[0]
    half = down_ref.shape[0]
    product = jnp.dot(received_ref[:, :half], down_ref[...], preferred_element_type=F32)
    label = received_ref[:, half:].astype(F32)
    second = iota((lines, 128), 0) % 8 >= 4
    upper = iota((lines, 128), 1) >= 64
    left = jnp.where(second, product[:, 256:384], product[:, :128])
    right = jnp.where(second, product[:, 384:], product[:, 128:256])
    total = jnp.where(label == jnp.where(upper, 2.0, 1.0), left, 0.0) + jnp.where(
        label == jnp.where(upper, 4.0, 3.0), right, 0.0
    )
    total = total + pltpu.roll(total, 64, 1)
    by_shard = total.reshape(lines // 8, 8, 128)
    total = (by_shard + pltpu.roll(by_shard, 4, 1)).reshape(lines, 128)
    first, last = pair_up(total)
    packed = jnp.where(iota(first.shape, 1) < 64, first, last).astype(BF16)
    for peer in range(partial_ref.shape[0]):
        partial_ref[peer] = packed
    labels = pair_up(label)
    for e in range(2):
        label_ref[e] = labels[e].astype(BF16)


def expand_kernel(partial_ref, label_ref, up_ref, out_ref):
    total = partial_ref[0].astype(F32)
    for peer in range(1, partial_ref.shape[0]):
        total = total + partial_ref[peer].astype(F32)
    turned = pltpu.roll(total, 64, 1)
    upper = iota(total.shape, 1) >= 64
    lines = total.shape[0]
    for e in range(2):
        row = jnp.where(upper, turned, total) if e == 0 else jnp.where(upper, total, turned)
        label = label_ref[e].astype(F32)
        left = jnp.where(label == jnp.where(upper, 2.0, 1.0), row, 0.0)
        right = jnp.where(label == jnp.where(upper, 4.0, 3.0), row, 0.0)
        wide = jnp.concatenate([left, right], axis=1).astype(BF16)
        out_ref[e * lines : (e + 1) * lines] = jnp.dot(
            wide, up_ref[...], preferred_element_type=F32
        )


def place_kernel(owned, owners, index_ref, out_ref):
    index_row = index_ref[...]
    rows = index_row.shape[1]
    _, slot, index_col = slots_of(index_row, owned, 4)
    target = index_col // owned * 4 + slot
    out_ref[...] = jnp.where(iota((rows, owners * 4), 1) == target, 1.0, 0.0).astype(BF16)


def add_kernel(place_ref, arrived_ref, base_ref, out_ref):
    arrived = arrived_ref[...]
    high = arrived.astype(BF16)
    low = (arrived - high.astype(F32)).astype(BF16)
    place = place_ref[...]
    terms = jnp.dot(place, high, preferred_element_type=F32) + jnp.dot(
        place, low, preferred_element_type=F32
    )
    out_ref[...] = (base_ref[...] + terms).astype(BF16)


def call(kernel, shapes, ins, scratch=(), flops=0, any_at=()):
    nbytes = sum(v.size * v.dtype.itemsize for v in ins)
    return pl.pallas_call(
        kernel,
        out_shape=shapes,
        in_specs=[
            pl.BlockSpec(memory_space=pl.ANY if i in any_at else pltpu.VMEM)
            for i in range(len(ins))
        ],
        out_specs=jax.tree.map(lambda _: pl.BlockSpec(memory_space=pltpu.VMEM), shapes),
        scratch_shapes=scratch,
        compiler_params=pltpu.CompilerParams(vmem_limit_bytes=VMEM_LIMIT),
        cost_estimate=pl.CostEstimate(flops=flops, bytes_accessed=nbytes, transcendentals=0),
    )(*ins)


def on_device(tokens, value_matrix, down, up, index):
    groups, rows_local, features = tokens.shape
    owners = lax.axis_size("dp")
    planes = lax.axis_size("tensor")
    owned, width, rank = down.shape
    columns = up.shape[2]
    rows = groups * rows_local
    half = width // 2
    lines = owners * 8
    shape = jax.ShapeDtypeStruct
    index_row = index.reshape(1, rows)

    packed = call(
        functools.partial(pack_kernel, owned, owners),
        shape((lines, half + 128), BF16),
        (index_row, tokens),
        [pltpu.VMEM((groups, rows_local, width), BF16), pltpu.SemaphoreType.DMA],
        any_at=(1,),
    )
    received = lax.all_to_all(
        packed.reshape(owners, 8, half + 128), "dp", split_axis=0, concat_axis=0, tiled=True
    ).reshape(lines, half + 128)

    base = jnp.dot(
        tokens.reshape(rows, features), value_matrix, preferred_element_type=F32
    )
    place = call(
        functools.partial(place_kernel, owned, owners),
        shape((rows, owners * 4), BF16),
        (index_row,),
    )
    down_wide = down.reshape(owned, 2, half, rank).transpose(2, 1, 0, 3).reshape(half, -1)

    partial, label = call(
        shrink_kernel,
        (shape((planes, lines // 4, 128), BF16), shape((2, lines // 4, 128), BF16)),
        (received, down_wide),
    )
    partials = lax.all_to_all(partial, "tensor", split_axis=0, concat_axis=0, tiled=True)
    terms = call(
        expand_kernel,
        shape((owners * 4, columns), F32),
        (partials, label, up.reshape(owned * rank, columns)),
    )
    arrived = lax.all_to_all(
        terms.reshape(owners, 4, columns), "dp", split_axis=0, concat_axis=0, tiled=True
    ).reshape(owners * 4, columns)
    out = call(add_kernel, shape((rows, columns), BF16), (place, arrived, base))
    return out.reshape(groups, rows_local, columns)


def solution(mesh):
    in_specs = (
        P(None, "dp", None),
        P(None, "tensor"),
        P("dp", "tensor", None),
        P("dp", None, "tensor"),
        P(None, "dp"),
    )
    out_specs = P(None, "dp", "tensor")
    return jax.shard_map(
        on_device, mesh=mesh, in_specs=in_specs, out_specs=out_specs, check_vma=False
    )
```

time: 143 us -> 78.1 us (0.55)
  blocking collectives: 24 us -> 0 us
  starting transfers between devices: 47.8 us -> 28.4 us
  waiting for transfers between devices: 54.9 us -> 36.1 us
  other arithmetic: 4.72 us -> 0 us
  Pallas kernels: 0 us -> 4.67 us
  matrix products: 5.85 us -> 2.29 us
    psum x1 -> x0, blocking collectives: 24 us -> none  [on_device(): shrunk_output = lax.psum(partial_value_sum, 'tensor').astype(jnp.bfloat16)]
    all_to_all x6 -> x3, starting transfers between devices: 47.8 us -> 28.4 us  [the longest x1 14.9 us: on_device(): lax.all_to_all(packed.reshape(owners, 8, half + 128), 'dp', split_axis=0,...]
    all_to_all x6 -> x3, waiting for transfers between devices: 54.9 us -> 36.1 us  [the longest x1 16.6 us: on_device(): lax.all_to_all(packed.reshape(owners, 8, half + 128), 'dp', split_axis=0,...]
    pallas_call x0 -> x5, Pallas kernels: none -> 4.67 us  [call(): pl.pallas_call(kernel, out_shape=shapes, in_specs=[pl.BlockSpec(memory_sp...]
    dot_general x5 -> x1, matrix products: 5.25 us -> 2.29 us  [on_device(): jnp.dot(tokens.reshape(rows, features), value_matrix, preferred_element_t...]
    reshape x4 -> x3, local copies, waits for them, and re-layouts: 1.79 us -> 3.59 us  [the longest x2 2.68 us: on_device(): down.reshape(owned, 2, half, rank).transpose(2, 1, 0, 3).reshape(half, -1)]
    unnamed x6, local copies, waits for them, and re-layouts: 0.01 us -> 1.6 us
    sub x2 -> x0, local copies, waits for them, and re-layouts: 1.5 us -> none  [route_rows(): slot_labels = jnp.sum(jnp.where(select, local_plus[None, :], 0), axis=1) - 1]
  transfers between devices with their start and end apart: 6 -> 3, of which waited for: 6 -> 3; matrix products, arithmetic and copies ran while one was open for 5% -> 8% of each run, Pallas kernels for 0% -> 0%
where the time goes in v1:
time: 78.1 us; the launch traced here: 77.6 us
  waiting for transfers between devices  36.1 us (46%)
  starting transfers between devices  28.4 us (36%)
  local copies, waits for them, and re-layouts  6.06 us (8%)
  Pallas kernels  4.67 us (6%)
  matrix products  2.29 us (3%)
    all_to_all x1, waiting for transfers between devices, on_device(): lax.all_to_all(packed.reshape(owners, 8, half + 128), 'dp', split_axis=0,...  16.6 us
    all_to_all x1, starting transfers between devices, on_device(): lax.all_to_all(packed.reshape(owners, 8, half + 128), 'dp', split_axis=0,...  14.9 us
    all_to_all x1, waiting for transfers between devices, on_device(): lax.all_to_all(partial, 'tensor', split_axis=0, concat_axis=0, tiled=True)  11.5 us
    all_to_all x1, waiting for transfers between devices, on_device(): lax.all_to_all(terms.reshape(owners, 4, columns), 'dp', split_axis=0, con...  8.06 us
    all_to_all x1, starting transfers between devices, on_device(): lax.all_to_all(partial, 'tensor', split_axis=0, concat_axis=0, tiled=True)  6.82 us
    all_to_all x1, starting transfers between devices, on_device(): lax.all_to_all(terms.reshape(owners, 4, columns), 'dp', split_axis=0, con...  6.72 us
    pallas_call x5, Pallas kernels, call(): pl.pallas_call(kernel, out_shape=shapes, in_specs=[pl.BlockSpec(memory_sp...  4.67 us
    reshape x2, local copies, waits for them, and re-layouts, on_device(): down.reshape(owned, 2, half, rank).transpose(2, 1, 0, 3).reshape(half, -1)  2.68 us
  transfers between devices with their start and end apart: 3, of which 3 were waited for; matrix products, arithmetic and copies ran while one was open for 8% of the time, Pallas kernels for 0%

profile of v1, /device:TPU:1, one launch (start us, length us, event | category | flops | bytes accessed | tf_op | source)
XLA Modules:
  0.0 77.6 jit_solution(15599798978798742538)
XLA Ops:
  0.0 0.0 copy-start
  0.0 0.9 %reshape.30.index_ref = s32[1,128]{1,0:T(1,128)S(1)} reshape(s32[2,64]{1,0:T(2,128)} %param.9) | data formatting | bytes 1024 | tf_op jit(solution)/shard_map/reshape | solution.py:151
  0.9 0.0 copy-start.1
  0.9 1.6 %copy-done.1 = bf16[2,64,8192]{2,1,0:T(8,128)(2,1)S(1)} copy-done((bf16[2,64,8192]{2,1,0:T(8,128)(2,1)S(1)}, bf16[2,64,8192]{2,1,0:T(8,128)(2,1)}, u32[]{:S(2)}) %copy-start.1) | copy-done | bytes 2097176
  2.5 1.5 %shard_map.56 = bf16[512,640]{1,0:T(8,128)(2,1)} custom-call(s32[1,128]{1,0:T(1,128)S(1)} %reshape.30.index_ref, bf16[2,64,8192]{2,1,0:T(8,128)(2,1)S(1)} %copy-done.1), custom_call_target="tpu_custom_call" | custom-call | bytes 2097664 | tf_op jit(solution)/shard_map/pallas_call | solution.py:127
  4.0 14.9 %all-to-all-start = ((bf16[64,8,640]{2,1,0:T(8,128)(2,1)}), bf16[64,8,640]{2,1,0:T(8,128)(2,1)S(1)}, u32[]{:S(2)}, u32[]{:S(2)}) async-start(bf16[64,8,640]{2,1,0:T(8,128)(2,1)} %bitcast), calls=%async_computation | async-start | bytes 1310720 | tf_op jit(solution)/shard_map/all_to_all | solution.py:160
  18.9 1.4 %reshape.33 = bf16[4,2,512,64]{2,1,3,0:T(2,128)(2,1)S(1)} reshape(bf16[4,1024,64]{1,2,0:T(8,128)(2,1)} %param.7) | data formatting | bytes 1048576 | tf_op jit(solution)/shard_map/reshape | solution.py:172
  20.3 0.0 copy-start.2
  20.4 0.9 %copy.8 = bf16[512,2,4,64]{0,3,2,1:T(8,128)(2,1)} copy(bf16[512,2,4,64]{0,1,3,2:T(2,128)(2,1)S(1)} %bitcast.18) | data formatting | bytes 1048576 | tf_op jit(solution)/shard_map/transpose | solution.py:172
  21.2 1.3 %copy.9.down_ref = bf16[512,512]{1,0:T(8,128)(2,1)S(1)} copy(bf16[512,512]{0,1:T(8,128)(2,1)} %bitcast.17) | data formatting | bytes 1048576 | tf_op jit(solution)/shard_map/reshape | solution.py:172
  22.5 16.6 %all-to-all-done = bf16[64,8,640]{2,1,0:T(8,128)(2,1)S(1)} async-done(((bf16[64,8,640]{2,1,0:T(8,128)(2,1)}), bf16[64,8,640]{2,1,0:T(8,128)(2,1)S(1)}, u32[]{:S(2)}, u32[]{:S(2)}) %all-to-all-start) | async-done | bytes 655392 | tf_op jit(solution)/shard_map/all_to_all | solution.py:160
  39.0 1.2 %shard_map.57 = (bf16[8,128,128]{2,1,0:T(8,128)(2,1)}, bf16[2,128,128]{2,1,0:T(8,128)(2,1)S(1)}) custom-call(bf16[512,640]{1,0:T(8,128)(2,1)S(1)} %bitcast.14, bf16[512,512]{1,0:T(8,128)(2,1)S(1)} %copy.9.down_ref), custom_call_target="tpu_custom_call" | custom-call | bytes 1179648 | tf_op jit(solution)/shard_map/pallas_call | solution.py:127
  40.2 6.8 %all-to-all-start.1 = ((bf16[8,128,128]{2,1,0:T(8,128)(2,1)}), bf16[8,128,128]{2,1,0:T(8,128)(2,1)S(1)}, u32[]{:S(2)}, u32[]{:S(2)}) async-start(bf16[8,128,128]{2,1,0:T(8,128)(2,1)} %get-tuple-element.7), calls=%async_computation.1 | async-start | bytes 524288 | tf_op jit(solution)/shard_map/all_to_all | solution.py:179
  47.1 0.3 shard_map.55.place_ref
  47.3 11.5 %all-to-all-done.1.partial_ref = bf16[8,128,128]{2,1,0:T(8,128)(2,1)S(1)} async-done(((bf16[8,128,128]{2,1,0:T(8,128)(2,1)}), bf16[8,128,128]{2,1,0:T(8,128)(2,1)S(1)}, u32[]{:S(2)}, u32[]{:S(2)}) %all-to-all-start.1) | async-done | bytes 262176 | tf_op jit(solution)/shard_map/all_to_all | solution.py:179
  58.8 0.0 copy-done.2
  58.8 0.9 %shard_map.58 = f32[256,128]{1,0:T(8,128)} custom-call(bf16[8,128,128]{2,1,0:T(8,128)(2,1)S(1)} %all-to-all-done.1.partial_ref, bf16[2,128,128]{2,1,0:T(8,128)(2,1)S(1)} %get-tuple-element.8.label_ref, bf16[256,128]{1,0:T(8,128)(2,1)S(1)} %bitcast.16), custom_call_target="tpu_custom_call" | custom-call | bytes 393216 | tf_op jit(solution)/shard_map/pallas_call | solution.py:127
  59.7 6.7 %all-to-all-start.2 = ((f32[64,4,128]{2,1,0:T(4,128)}), f32[64,4,128]{2,1,0:T(4,128)S(1)}, u32[]{:S(2)}, u32[]{:S(2)}) async-start(f32[64,4,128]{2,1,0:T(4,128)} %bitcast.5), calls=%async_computation.2 | async-start | bytes 262144 | tf_op jit(solution)/shard_map/all_to_all | solution.py:185
  66.4 0.0 copy-done
  66.4 2.3 %fusion.base_ref = f32[128,128]{1,0:T(8,128)S(1)} fusion(bf16[128,8192]{1,0:T(8,128)(2,1)} %bitcast.13, bf16[8192,128]{1,0:T(8,128)(2,1)S(1)} %copy-done), kind=kOutput, calls=%fused_computation | convolution fusion | flops 268435456 | bytes 4259840 | tf_op jit(solution)/shard_map/dot_general | solution.py:164
  68.7 8.1 %all-to-all-done.2 = f32[64,4,128]{2,1,0:T(4,128)S(1)} async-done(((f32[64,4,128]{2,1,0:T(4,128)}), f32[64,4,128]{2,1,0:T(4,128)S(1)}, u32[]{:S(2)}, u32[]{:S(2)}) %all-to-all-start.2) | async-done | bytes 131104 | tf_op jit(solution)/shard_map/all_to_all | solution.py:185
  76.8 0.8 %shard_map.59 = bf16[128,128]{1,0:T(8,128)(2,1)} custom-call(bf16[128,256]{1,0:T(8,128)(2,1)S(1)} %shard_map.55.place_ref, f32[256,128]{1,0:T(8,128)S(1)} %bitcast.15, f32[128,128]{1,0:T(8,128)S(1)} %fusion.base_ref), custom_call_target="tpu_custom_call" | custom-call | bytes 262144 | tf_op jit(solution)/shard_map/pallas_call | solution.py:127
Async XLA Ops:
  0.0 66.4 %copy-start = (bf16[8192,128]{1,0:T(8,128)(2,1)S(1)}, bf16[8192,128]{1,0:T(8,128)(2,1)}, u32[]{:S(2)}) copy-start(bf16[8192,128]{1,0:T(8,128)(2,1)} %param.6) | copy-start | bytes 6291460
  0.9 1.6 %copy-start.1 = (bf16[2,64,8192]{2,1,0:T(8,128)(2,1)S(1)}, bf16[2,64,8192]{2,1,0:T(8,128)(2,1)}, u32[]{:S(2)}) copy-start(bf16[2,64,8192]{2,1,0:T(8,128)(2,1)} %tokens_ref.1) | copy-start | bytes 6291460
  4.0 35.0 %all-to-all-start = ((bf16[64,8,640]{2,1,0:T(8,128)(2,1)}), bf16[64,8,640]{2,1,0:T(8,128)(2,1)S(1)}, u32[]{:S(2)}, u32[]{:S(2)}) async-start(bf16[64,8,640]{2,1,0:T(8,128)(2,1)} %bitcast), calls=%async_computation | async-start | bytes 1310720 | tf_op jit(solution)/shard_map/all_to_all | solution.py:160
  20.3 38.5 %copy-start.2 = (bf16[4,64,128]{2,1,0:T(8,128)(2,1)S(1)}, bf16[4,64,128]{2,1,0:T(8,128)(2,1)}, u32[]{:S(2)}) copy-start(bf16[4,64,128]{2,1,0:T(8,128)(2,1)} %param.8) | copy-start | bytes 196612
  40.2 18.6 %all-to-all-start.1 = ((bf16[8,128,128]{2,1,0:T(8,128)(2,1)}), bf16[8,128,128]{2,1,0:T(8,128)(2,1)S(1)}, u32[]{:S(2)}, u32[]{:S(2)}) async-start(bf16[8,128,128]{2,1,0:T(8,128)(2,1)} %get-tuple-element.7), calls=%async_computation.1 | async-start | bytes 524288 | tf_op jit(solution)/shard_map/all_to_all | solution.py:179
  59.7 17.1 %all-to-all-start.2 = ((f32[64,4,128]{2,1,0:T(4,128)}), f32[64,4,128]{2,1,0:T(4,128)S(1)}, u32[]{:S(2)}, u32[]{:S(2)}) async-start(f32[64,4,128]{2,1,0:T(4,128)} %bitcast.5), calls=%async_computation.2 | async-start | bytes 262144 | tf_op jit(solution)/shard_map/all_to_all | solution.py:185

commit v2 on v1

v2 whole, which is shorter than its diff:
```python
import functools

import jax
import jax.numpy as jnp
from jax import lax
from jax.experimental import pallas as pl
from jax.experimental.pallas import tpu as pltpu
from jax.sharding import PartitionSpec as P

BF16, F32, I32 = jnp.bfloat16, jnp.float32, jnp.int32
MIB = 1024 * 1024


def iota(shape, dim):
    return lax.broadcasted_iota(I32, shape, dim)


def read_index(index_ref, owned):
    along = jnp.concatenate([index_ref[0:1, :], index_ref[1:2, :]], axis=1)
    rows = along.shape[1]
    wide = jnp.broadcast_to(along, (rows, rows))
    line, column = iota((rows, rows), 0), iota((rows, rows), 1)
    down = jnp.sum(jnp.where(line == column, wide, 0), axis=1, keepdims=True)
    half = rows // 2
    same = (wide // owned == down // owned) & ((line >= half) == (column >= half))
    place = jnp.sum(jnp.where(same & (line < column), 1, 0), axis=0, keepdims=True)
    place_down = jnp.sum(jnp.where(same & (column < line), 1, 0), axis=1, keepdims=True)
    group = jnp.where(iota((1, rows), 1) >= half, 1, 0)
    group_down = jnp.where(iota((rows, 1), 0) >= half, 1, 0)
    return (along, place, group), (down, place_down, group_down)


def pack_kernel(owned, owners, index_ref, tokens_ref, out_ref, held, sems):
    quarter = held.shape[3]
    plane = lax.axis_index("tensor")
    parity = plane % 2
    copies = []
    for e in range(4):
        from_plane = plane if e < 2 else plane + 1 - 2 * parity
        start = pl.multiple_of(from_plane * (2 * quarter) + (e % 2) * quarter, quarter)
        copies.append(
            pltpu.make_async_copy(
                tokens_ref.at[:, :, pl.ds(start, quarter)], held.at[e], sems.at[e]
            )
        )
        copies[-1].start()
    (along, place, group), (down, _, _) = read_index(index_ref, owned)
    rows = along.shape[1]
    lines = owners * 8
    owner = along // owned
    first = jnp.where(place == parity, owner * 8 + group, -1)
    target = jnp.concatenate([jnp.where(first >= 0, first + 2 * e, -1) for e in range(4)], axis=1)
    select = jnp.where(iota((lines, 4 * rows), 0) == target, 1.0, 0.0).astype(BF16)
    wanted = owner * 2 + group
    wanted = jnp.concatenate([jnp.where(place == p, wanted, -1) for p in range(2)], axis=1)
    line = iota((lines, 2 * rows), 0)
    choose = jnp.where(line // 8 * 2 + line % 2 == wanted, 1.0, 0.0).astype(BF16)
    label = jnp.broadcast_to((down % owned + 1).astype(F32), (rows, 128))
    upper = iota((rows, 128), 1) >= 64
    labels = jnp.concatenate(
        [jnp.where(upper, 0.0, label), jnp.where(upper, label, 0.0)], axis=0
    ).astype(BF16)
    out_ref[:, quarter:] = jnp.dot(choose, labels, preferred_element_type=F32).astype(BF16)
    for copy in copies:
        copy.wait()
    tokens = held[...].reshape(4 * rows, quarter)
    out_ref[:, :quarter] = jnp.dot(select, tokens, preferred_element_type=F32).astype(BF16)


def shrink_kernel(received_ref, own_ref, other_ref, partial_ref, label_ref):
    lines = received_ref.shape[0]
    quarter = received_ref.shape[1] - 128
    shards = lines // 8
    parity = lax.axis_index("tensor") % 2
    rows = received_ref[:, :quarter]
    part = iota((lines, 256), 0) % 8 // 2
    product = None
    for e in range(4):
        held = own_ref if e < 2 else other_ref
        weight = held[:, :, (e % 2) * quarter : (e % 2 + 1) * quarter].reshape(256, quarter)
        mine = lax.dot_general(
            rows, weight, (((1,), (1,)), ((), ())), preferred_element_type=F32
        )
        product = mine if e == 0 else jnp.where(part == e, mine, product)
    label = received_ref[:, quarter:].astype(F32)
    turned = pltpu.roll(label, 64, 1)
    upper = iota((lines, 128), 1) // 64
    here = jnp.where(upper == parity, label, turned)
    total = jnp.where(here == upper.astype(F32) + 1.0, product[:, :128], 0.0)
    total = total + jnp.where(here == upper.astype(F32) + 3.0, product[:, 128:], 0.0)
    total = (total + pltpu.roll(total, 64, 1)).reshape(shards, 8, 128)
    total = total + pltpu.roll(total, 4, 1)
    total = total + pltpu.roll(total, 2, 1)
    by_shard = total.reshape(2, shards // 8, 4, 8, 128)
    pair = iota((shards // 8, 8, 128), 1) // 2
    halves = []
    for e in range(2):
        chosen = by_shard[e, :, 0]
        for d in range(1, 4):
            chosen = jnp.where(pair == d, by_shard[e, :, d], chosen)
        halves.append(chosen)
    packed = jnp.where(iota((shards // 8, 8, 128), 2) < 64, halves[0], halves[1])
    packed = packed.reshape(shards, 128).astype(BF16)
    for peer in range(partial_ref.shape[0]):
        partial_ref[peer] = packed
    low = jnp.where(upper == 0, label, turned)
    high = jnp.where(upper == 0, turned, label)
    place = iota((lines, 128), 0) // 2 % 2
    both = jnp.where(place == 0, low, high).reshape(2, shards // 4, 2, 8, 128)
    even = iota((shards // 4, 8, 128), 1) < 4
    for e in range(2):
        chosen = jnp.where(even, both[e, :, 0], both[e, :, 1])
        label_ref[e] = chosen.reshape(shards * 2, 128).astype(BF16)


def expand_kernel(partial_ref, label_ref, up_ref, out_ref):
    planes, shards, _ = partial_ref.shape
    sums = []
    for p in range(2):
        total = partial_ref[p].astype(F32)
        for peer in range(p + 2, planes, 2):
            total = total + partial_ref[peer].astype(F32)
        sums.append(total.reshape(shards // 8, 8, 128))
    first, second = sums
    pair = iota(first.shape, 1) // 2

    def spread(pieces):
        out = pieces[0]
        for d in range(1, 4):
            out = jnp.where(pair == d, pieces[d], out)
        return out

    def turn(total, by):
        return pltpu.roll(total, by, 1)

    even = spread([first, turn(second, 2), turn(first, 2), turn(second, 4)])
    odd = spread([turn(first, 4), turn(second, 6), turn(first, 6), second])
    total = jnp.stack([even, odd], axis=1).reshape(shards * 2, 128)
    turned = pltpu.roll(total, 64, 1)
    upper = iota(total.shape, 1) // 64
    lines = total.shape[0]
    for e in range(2):
        row = jnp.where(upper == e, total, turned)
        label = label_ref[e].astype(F32)
        left = jnp.where(label == upper.astype(F32) + 1.0, row, 0.0)
        right = jnp.where(label == upper.astype(F32) + 3.0, row, 0.0)
        wide = jnp.concatenate([left, right], axis=1).astype(BF16)
        out_ref[e * lines : (e + 1) * lines] = jnp.dot(
            wide, up_ref[...], preferred_element_type=F32
        )


def place_kernel(owned, owners, index_ref, out_ref):
    _, (down, place, group) = read_index(index_ref, owned)
    target = down // owned * 4 + place * 2 + group
    out_ref[...] = jnp.where(iota(out_ref.shape, 1) == target, 1.0, 0.0).astype(BF16)


def add_kernel(place_ref, arrived_ref, base_ref, out_ref):
    arrived = arrived_ref[...]
    high = arrived.astype(BF16)
    low = (arrived - high.astype(F32)).astype(BF16)
    place = place_ref[...]
    terms = jnp.dot(place, high, preferred_element_type=F32) + jnp.dot(
        place, low, preferred_element_type=F32
    )
    out_ref[...] = (base_ref[...] + terms).astype(BF16)


def call(kernel, shapes, ins, scratch=(), flops=0, in_hbm=(), vmem=40):
    nbytes = sum(v.size * v.dtype.itemsize for v in ins)
    return pl.pallas_call(
        kernel,
        out_shape=shapes,
        in_specs=[
            pl.BlockSpec(memory_space=pltpu.HBM if i in in_hbm else pltpu.VMEM)
            for i in range(len(ins))
        ],
        out_specs=jax.tree.map(lambda _: pl.BlockSpec(memory_space=pltpu.VMEM), shapes),
        scratch_shapes=scratch,
        compiler_params=pltpu.CompilerParams(vmem_limit_bytes=vmem * MIB),
        cost_estimate=pl.CostEstimate(flops=flops, bytes_accessed=nbytes, transcendentals=0),
    )(*ins)


def on_device(tokens, value_matrix, down, up, index):
    groups, rows_local, features = tokens.shape
    owners = lax.axis_size("dp")
    planes = lax.axis_size("tensor")
    owned, width, rank = down.shape
    columns = up.shape[2]
    rows = groups * rows_local
    quarter = width // 2
    lines = owners * 8
    shape = jax.ShapeDtypeStruct

    packed = call(
        functools.partial(pack_kernel, owned, owners),
        shape((lines, quarter + 128), BF16),
        (index, tokens),
        [pltpu.VMEM((4, groups, rows_local, quarter), BF16), pltpu.SemaphoreType.DMA((4,))],
        in_hbm=(1,),
        vmem=62,
    )
    received = lax.all_to_all(
        packed.reshape(owners, 8, quarter + 128), "dp", split_axis=0, concat_axis=0, tiled=True
    ).reshape(lines, quarter + 128)

    down_own = down.transpose(0, 2, 1)
    sent_first, _ = lax.optimization_barrier((down_own, packed))
    down_other = lax.ppermute(sent_first, "tensor", [(i, i ^ 1) for i in range(planes)])
    base = jnp.dot(tokens.reshape(rows, features), value_matrix, preferred_element_type=F32)
    place = call(
        functools.partial(place_kernel, owned, owners), shape((rows, owners * 4), BF16), (index,)
    )

    partial, label = call(
        shrink_kernel,
        (shape((planes, owners, 128), BF16), shape((2, owners * 2, 128), BF16)),
        (received, down_own, down_other),
    )
    partials = lax.all_to_all(partial, "tensor", split_axis=0, concat_axis=0, tiled=True)
    terms = call(
        expand_kernel,
        shape((owners * 4, columns), F32),
        (partials, label, up.reshape(owned * rank, columns)),
    )
    arrived = lax.all_to_all(
        terms.reshape(owners, 4, columns), "dp", split_axis=0, concat_axis=0, tiled=True
    ).reshape(owners * 4, columns)
    out = call(add_kernel, shape((rows, columns), BF16), (place, arrived, base))
    return out.reshape(groups, rows_local, columns)


def solution(mesh):
    in_specs = (
        P(None, "dp", None),
        P(None, "tensor"),
        P("dp", "tensor", None),
        P("dp", None, "tensor"),
        P(None, "dp"),
    )
    out_specs = P(None, "dp", "tensor")
    return jax.shard_map(
        on_device, mesh=mesh, in_specs=in_specs, out_specs=out_specs, check_vma=False
    )
```

time: 78.1 us -> 74.7 us (0.956)
  local copies, waits for them, and re-layouts: 6.06 us -> 0.02 us
  starting transfers between devices: 28.4 us -> 32.6 us
  waiting for transfers between devices: 36.1 us -> 32 us
  Pallas kernels: 4.67 us -> 6.65 us
    ppermute x0 -> x1, waiting for transfers between devices: none -> 11.7 us  [on_device(): lax.ppermute(sent_first, 'tensor', [(i, i ^ 1) for i in range(planes)])]
    all_to_all x1, waiting for transfers between devices: 16.6 us -> 5.18 us  [on_device(): lax.all_to_all(packed.reshape(owners, 8, quarter + 128), 'dp', split_axis...]
    all_to_all x1, waiting for transfers between devices: 11.5 us -> 7.69 us  [on_device(): lax.all_to_all(partial, 'tensor', split_axis=0, concat_axis=0, tiled=True)]
    reshape x3 -> x0, local copies, waits for them, and re-layouts: 3.59 us -> none  [the longest x2 2.68 us: on_device(): down.reshape(owned, 2, half, rank).transpose(2, 1, 0, 3).reshape(half, -1)]
    ppermute x0 -> x1, starting transfers between devices: none -> 3.2 us  [on_device(): lax.ppermute(sent_first, 'tensor', [(i, i ^ 1) for i in range(planes)])]
    pallas_call x5, Pallas kernels: 4.67 us -> 6.65 us  [call(): pl.pallas_call(kernel, out_shape=shapes, in_specs=[pl.BlockSpec(memory_sp...]
    unnamed x6, local copies, waits for them, and re-layouts: 1.6 us -> 0.02 us
    all_to_all x1, starting transfers between devices: 6.72 us -> 7.63 us  [on_device(): lax.all_to_all(terms.reshape(owners, 4, columns), 'dp', split_axis=0, con...]
  transfers between devices with their start and end apart: 3 -> 4, of which waited for: 3 -> 4; matrix products, arithmetic and copies ran while one was open for 8% -> 4% of each run, Pallas kernels for 0% -> 0%
where the time goes in v2:
time: 74.7 us; the launch traced here: 74.3 us
  starting transfers between devices  32.6 us (44%)
  waiting for transfers between devices  32 us (43%)
  Pallas kernels  6.65 us (9%)
  matrix products  2.92 us (4%)
    all_to_all x1, starting transfers between devices, on_device(): lax.all_to_all(packed.reshape(owners, 8, quarter + 128), 'dp', split_axis...  15 us
    ppermute x1, waiting for transfers between devices, on_device(): lax.ppermute(sent_first, 'tensor', [(i, i ^ 1) for i in range(planes)])  11.7 us
    all_to_all x1, waiting for transfers between devices, on_device(): lax.all_to_all(partial, 'tensor', split_axis=0, concat_axis=0, tiled=True)  7.69 us
    all_to_all x1, starting transfers between devices, on_device(): lax.all_to_all(terms.reshape(owners, 4, columns), 'dp', split_axis=0, con...  7.63 us
    all_to_all x1, waiting for transfers between devices, on_device(): lax.all_to_all(terms.reshape(owners, 4, columns), 'dp', split_axis=0, con...  7.44 us
    all_to_all x1, starting transfers between devices, on_device(): lax.all_to_all(partial, 'tensor', split_axis=0, concat_axis=0, tiled=True)  6.82 us
    pallas_call x5, Pallas kernels, call(): pl.pallas_call(kernel, out_shape=shapes, in_specs=[pl.BlockSpec(memory_sp...  6.65 us
    all_to_all x1, waiting for transfers between devices, on_device(): lax.all_to_all(packed.reshape(owners, 8, quarter + 128), 'dp', split_axis...  5.18 us
  transfers between devices with their start and end apart: 4, of which 4 were waited for; matrix products, arithmetic and copies ran while one was open for 4% of the time, Pallas kernels for 0%

profile of v2, /device:TPU:1, one launch (start us, length us, event | category | flops | bytes accessed | tf_op | source)
XLA Modules:
  0.0 74.3 jit_solution(9214887478999128008)
XLA Ops:
  0.0 0.0 copy-start
  0.0 3.2 %shard_map.56 = bf16[512,640]{1,0:T(8,128)(2,1)} custom-call(s32[2,64]{1,0:T(2,128)} %index_ref.3, bf16[2,64,8192]{2,1,0:T(8,128)(2,1)} %tokens_ref.1), custom_call_target="tpu_custom_call" | custom-call | bytes 2097664 | tf_op jit(solution)/shard_map/pallas_call | solution.py:172
  3.2 0.0 copy-start.2
  3.2 0.0 copy-start.1
  3.2 15.0 %all-to-all-start = ((bf16[64,8,640]{2,1,0:T(8,128)(2,1)}), bf16[64,8,640]{2,1,0:T(8,128)(2,1)S(1)}, u32[]{:S(2)}, u32[]{:S(2)}) async-start(bf16[64,8,640]{2,1,0:T(8,128)(2,1)} %bitcast.16), calls=%async_computation | async-start | bytes 1310720 | tf_op jit(solution)/shard_map/all_to_all | solution.py:205
  18.2 0.0 copy-done
  18.2 3.2 %collective-permute-start = (bf16[4,64,1024]{2,1,0:T(8,128)(2,1)S(1)}, bf16[4,64,1024]{2,1,0:T(8,128)(2,1)S(1)}, u32[]{:S(2)}, u32[]{:S(2)}) collective-permute-start(bf16[4,64,1024]{2,1,0:T(8,128)(2,1)S(1)} %bitcast.11), channel_id=1, source_target_pairs={{0,1},{1,0},{2,3},{3,2},{4,5},{5,4},{6,7},{7,6},{8,9},{9,8},{10,11... | collective-permute-start | bytes 1572872 | tf_op jit(solution)/shard_map/ppermute | solution.py:211
  21.4 11.7 %collective-permute-done.other_ref = bf16[4,64,1024]{2,1,0:T(8,128)(2,1)S(1)} collective-permute-done((bf16[4,64,1024]{2,1,0:T(8,128)(2,1)S(1)}, bf16[4,64,1024]{2,1,0:T(8,128)(2,1)S(1)}, u32[]{:S(2)}, u32[]{:S(2)}) %collective-permute-start) | collective-permute-done | bytes 524320 | tf_op jit(solution)/shard_map/ppermute | solution.py:211
  33.1 5.2 %all-to-all-done = bf16[64,8,640]{2,1,0:T(8,128)(2,1)S(1)} async-done(((bf16[64,8,640]{2,1,0:T(8,128)(2,1)}), bf16[64,8,640]{2,1,0:T(8,128)(2,1)S(1)}, u32[]{:S(2)}, u32[]{:S(2)}) %all-to-all-start) | async-done | bytes 655392 | tf_op jit(solution)/shard_map/all_to_all | solution.py:205
  38.3 1.5 %shard_map.57 = (bf16[8,64,128]{2,1,0:T(8,128)(2,1)}, bf16[2,128,128]{2,1,0:T(8,128)(2,1)S(1)}) custom-call(bf16[512,640]{1,0:T(8,128)(2,1)S(1)} %bitcast.10, bf16[4,64,1024]{2,1,0:T(8,128)(2,1)S(1)} %bitcast.12, bf16[4,64,1024]{2,1,0:T(8,128)(2,1)S(1)} %collective-permute-done.other_ref), custom_call_target="tpu_custom_call" | custom-call | bytes 1703936 | tf_op jit(solution)/shard_map/pallas_call | solution.py:172
  39.8 6.8 %all-to-all-start.1 = ((bf16[8,64,128]{2,1,0:T(8,128)(2,1)}), bf16[8,64,128]{2,1,0:T(8,128)(2,1)S(1)}, u32[]{:S(2)}, u32[]{:S(2)}) async-start(bf16[8,64,128]{2,1,0:T(8,128)(2,1)} %get-tuple-element.9), calls=%async_computation.1 | async-start | bytes 262144 | tf_op jit(solution)/shard_map/all_to_all | solution.py:222
  46.6 0.0 copy-done.2
  46.6 0.3 shard_map.55.place_ref
  46.9 7.7 %all-to-all-done.1.partial_ref = bf16[8,64,128]{2,1,0:T(8,128)(2,1)S(1)} async-done(((bf16[8,64,128]{2,1,0:T(8,128)(2,1)}), bf16[8,64,128]{2,1,0:T(8,128)(2,1)S(1)}, u32[]{:S(2)}, u32[]{:S(2)}) %all-to-all-start.1) | async-done | bytes 131104 | tf_op jit(solution)/shard_map/all_to_all | solution.py:222
  54.6 0.0 copy-done.1
  54.6 0.9 %shard_map.58 = f32[256,128]{1,0:T(8,128)} custom-call(bf16[8,64,128]{2,1,0:T(8,128)(2,1)S(1)} %all-to-all-done.1.partial_ref, bf16[2,128,128]{2,1,0:T(8,128)(2,1)S(1)} %get-tuple-element.10.label_ref, bf16[256,128]{1,0:T(8,128)(2,1)S(1)} %bitcast.14), custom_call_target="tpu_custom_call" | custom-call | bytes 262144 | tf_op jit(solution)/shard_map/pallas_call | solution.py:172
  55.5 7.6 %all-to-all-start.2 = ((f32[64,4,128]{2,1,0:T(4,128)}), f32[64,4,128]{2,1,0:T(4,128)S(1)}, u32[]{:S(2)}, u32[]{:S(2)}) async-start(f32[64,4,128]{2,1,0:T(4,128)} %bitcast.4), calls=%async_computation.2 | async-start | bytes 262144 | tf_op jit(solution)/shard_map/all_to_all | solution.py:228
  63.2 2.9 %fusion.base_ref = f32[128,128]{1,0:T(8,128)S(1)} fusion(bf16[128,8192]{1,0:T(8,128)(2,1)} %bitcast.15, bf16[8192,128]{1,0:T(8,128)(2,1)} %param.6), kind=kOutput, calls=%fused_computation | convolution fusion | flops 268435456 | bytes 4259840 | tf_op jit(solution)/shard_map/dot_general | solution.py:212
  66.1 7.4 %all-to-all-done.2 = f32[64,4,128]{2,1,0:T(4,128)S(1)} async-done(((f32[64,4,128]{2,1,0:T(4,128)}), f32[64,4,128]{2,1,0:T(4,128)S(1)}, u32[]{:S(2)}, u32[]{:S(2)}) %all-to-all-start.2) | async-done | bytes 131104 | tf_op jit(solution)/shard_map/all_to_all | solution.py:228
  73.5 0.8 %shard_map.59 = bf16[128,128]{1,0:T(8,128)(2,1)} custom-call(bf16[128,256]{1,0:T(8,128)(2,1)S(1)} %shard_map.55.place_ref, f32[256,128]{1,0:T(8,128)S(1)} %bitcast.13, f32[128,128]{1,0:T(8,128)S(1)} %fusion.base_ref), custom_call_target="tpu_custom_call" | custom-call | bytes 262144 | tf_op jit(solution)/shard_map/pallas_call | solution.py:172
Async XLA Ops:
  0.0 18.2 %copy-start = (bf16[4,1024,64]{1,2,0:T(8,128)(2,1)S(1)}, bf16[4,1024,64]{1,2,0:T(8,128)(2,1)}, u32[]{:S(2)}) copy-start(bf16[4,1024,64]{1,2,0:T(8,128)(2,1)} %param.7) | copy-start | bytes 1572868
  3.2 43.5 %copy-start.2 = (s32[2,64]{1,0:T(2,128)S(1)}, s32[2,64]{1,0:T(2,128)}, u32[]{:S(2)}) copy-start(s32[2,64]{1,0:T(2,128)} %index_ref.3) | copy-start | bytes 1540
  3.2 51.5 %copy-start.1 = (bf16[4,64,128]{2,1,0:T(8,128)(2,1)S(1)}, bf16[4,64,128]{2,1,0:T(8,128)(2,1)}, u32[]{:S(2)}) copy-start(bf16[4,64,128]{2,1,0:T(8,128)(2,1)} %param.8) | copy-start | bytes 196612
  3.2 35.1 %all-to-all-start = ((bf16[64,8,640]{2,1,0:T(8,128)(2,1)}), bf16[64,8,640]{2,1,0:T(8,128)(2,1)S(1)}, u32[]{:S(2)}, u32[]{:S(2)}) async-start(bf16[64,8,640]{2,1,0:T(8,128)(2,1)} %bitcast.16), calls=%async_computation | async-start | bytes 1310720 | tf_op jit(solution)/shard_map/all_to_all | solution.py:205
  18.2 14.9 %collective-permute-start = (bf16[4,64,1024]{2,1,0:T(8,128)(2,1)S(1)}, bf16[4,64,1024]{2,1,0:T(8,128)(2,1)S(1)}, u32[]{:S(2)}, u32[]{:S(2)}) collective-permute-start(bf16[4,64,1024]{2,1,0:T(8,128)(2,1)S(1)} %bitcast.11), channel_id=1, source_target_pairs={{0,1},{1,0},{2,3},{3,2},{4,5},{5,4},{6,7},{7,6},{8,9},{9,8},{10,11... | collective-permute-start | bytes 1572872 | tf_op jit(solution)/shard_map/ppermute | solution.py:211
  39.8 14.8 %all-to-all-start.1 = ((bf16[8,64,128]{2,1,0:T(8,128)(2,1)}), bf16[8,64,128]{2,1,0:T(8,128)(2,1)S(1)}, u32[]{:S(2)}, u32[]{:S(2)}) async-start(bf16[8,64,128]{2,1,0:T(8,128)(2,1)} %get-tuple-element.9), calls=%async_computation.1 | async-start | bytes 262144 | tf_op jit(solution)/shard_map/all_to_all | solution.py:222
  55.5 18.0 %all-to-all-start.2 = ((f32[64,4,128]{2,1,0:T(4,128)}), f32[64,4,128]{2,1,0:T(4,128)S(1)}, u32[]{:S(2)}, u32[]{:S(2)}) async-start(f32[64,4,128]{2,1,0:T(4,128)} %bitcast.4), calls=%async_computation.2 | async-start | bytes 262144 | tf_op jit(solution)/shard_map/all_to_all | solution.py:228

commit v3 on v2

v3 whole, which is shorter than its diff:
```python
import functools

import jax
import jax.numpy as jnp
from jax import lax
from jax.experimental import pallas as pl
from jax.experimental.pallas import tpu as pltpu
from jax.sharding import PartitionSpec as P

BF16, F32, I32 = jnp.bfloat16, jnp.float32, jnp.int32
MIB = 1024 * 1024


def iota(shape, dim):
    return lax.broadcasted_iota(I32, shape, dim)


def read_index(index_ref, owned):
    along = jnp.concatenate([index_ref[0:1, :], index_ref[1:2, :]], axis=1)
    rows = along.shape[1]
    wide = jnp.broadcast_to(along, (rows, rows))
    line, column = iota((rows, rows), 0), iota((rows, rows), 1)
    down = jnp.sum(jnp.where(line == column, wide, 0), axis=1, keepdims=True)
    half = rows // 2
    same = (wide // owned == down // owned) & ((line >= half) == (column >= half))
    place = jnp.sum(jnp.where(same & (line < column), 1, 0), axis=0, keepdims=True)
    place_down = jnp.sum(jnp.where(same & (column < line), 1, 0), axis=1, keepdims=True)
    group = jnp.where(iota((1, rows), 1) >= half, 1, 0)
    group_down = jnp.where(iota((rows, 1), 0) >= half, 1, 0)
    return (along, place, group), (down, place_down, group_down)


def spread(first, second):
    first, second = (v.reshape(v.shape[0] // 8, 8, 128) for v in (first, second))
    pair = iota(first.shape, 1) // 2

    def turn(total, by):
        return pltpu.roll(total, by, 1)

    def pick(*pieces):
        out = pieces[0]
        for d in range(1, 4):
            out = jnp.where(pair == d, pieces[d], out)
        return out

    even = pick(first, turn(second, 2), turn(first, 2), turn(second, 4))
    odd = pick(turn(first, 4), turn(second, 6), turn(first, 6), second)
    return jnp.stack([even, odd], axis=1).reshape(first.shape[0] * 16, 128)


def pack_kernel(owned, owners, index_ref, tokens_ref, out_ref, held, sems):
    width = held.shape[2] // 2
    plane = lax.axis_index("tensor")
    parity = plane % 2
    copies = []
    for e in range(2):
        from_plane = plane if e == 0 else plane + 1 - 2 * parity
        start = pl.multiple_of(from_plane * width, width)
        copies.append(
            pltpu.make_async_copy(
                tokens_ref.at[:, :, pl.ds(start, width)],
                held.at[:, :, e * width : (e + 1) * width],
                sems.at[e],
            )
        )
        copies[-1].start()
    (along, place, group), (down, _, _) = read_index(index_ref, owned)
    rows = along.shape[1]
    lines = owners * 2
    wanted = along // owned * 2 + group
    select = jnp.where(
        (iota((lines, rows), 0) == wanted) & (place == parity), 1.0, 0.0
    ).astype(BF16)
    both = jnp.concatenate([jnp.where(place == p, wanted, -1) for p in range(2)], axis=1)
    choose = jnp.where(iota((lines, 2 * rows), 0) == both, 1.0, 0.0).astype(BF16)
    label = jnp.broadcast_to((down % owned + 1).astype(F32), (rows, 128))
    upper = iota((rows, 128), 1) >= 64
    labels = jnp.concatenate(
        [jnp.where(upper, 0.0, label), jnp.where(upper, label, 0.0)], axis=0
    ).astype(BF16)
    labels = jnp.dot(choose, labels, preferred_element_type=F32).astype(BF16)
    out_ref[:, :, 2 * width :] = labels.reshape(owners, 2, 128)
    for copy in copies:
        copy.wait()
    tokens = held[...].reshape(rows, 2 * width)
    packed = jnp.dot(select, tokens, preferred_element_type=F32).astype(BF16)
    out_ref[:, :, : 2 * width] = packed.reshape(owners, 2, 2 * width)


def shrink_kernel(received_ref, own_ref, other_ref, partial_ref, label_ref):
    shards, groups, width = received_ref.shape
    width = (width - 128) // 2
    lines = shards * groups
    parity = lax.axis_index("tensor") % 2
    product = None
    for e in range(2):
        rows = received_ref[:, :, e * width : (e + 1) * width].reshape(lines, width)
        weight = (own_ref if e == 0 else other_ref)[...].reshape(256, width)
        mine = lax.dot_general(
            rows, weight, (((1,), (1,)), ((), ())), preferred_element_type=F32
        )
        product = mine if e == 0 else product + mine
    label = received_ref[:, :, 2 * width :].reshape(lines, 128).astype(F32)
    turned = pltpu.roll(label, 64, 1)
    upper = iota((lines, 128), 1) // 64
    here = jnp.where(upper == parity, label, turned)
    total = jnp.where(here == upper.astype(F32) + 1.0, product[:, :128], 0.0)
    total = total + jnp.where(here == upper.astype(F32) + 3.0, product[:, 128:], 0.0)
    total = total + pltpu.roll(total, 64, 1)
    half = lines // 2
    packed = jnp.where(upper[:half] == 0, total[:half], total[half:]).astype(BF16)
    for peer in range(partial_ref.shape[0]):
        partial_ref[peer] = packed
    low = jnp.where(upper == 0, label, turned)
    high = jnp.where(upper == 0, turned, label)
    label_ref[...] = spread(low, high).astype(BF16)


def expand_kernel(partial_ref, label_ref, up_ref, out_ref):
    sums = []
    for p in range(2):
        total = partial_ref[p].astype(F32)
        for peer in range(p + 2, partial_ref.shape[0], 2):
            total = total + partial_ref[peer].astype(F32)
        sums.append(total)
    total = spread(*sums)
    turned = pltpu.roll(total, 64, 1)
    upper = iota(total.shape, 1) // 64
    lines = total.shape[0]
    for e in range(2):
        row = jnp.where(upper == e, total, turned)
        label = label_ref[e * lines : (e + 1) * lines].astype(F32)
        left = jnp.where(label == upper.astype(F32) + 1.0, row, 0.0)
        right = jnp.where(label == upper.astype(F32) + 3.0, row, 0.0)
        wide = jnp.concatenate([left, right], axis=1).astype(BF16)
        out_ref[e * lines : (e + 1) * lines] = jnp.dot(
            wide, up_ref[...], preferred_element_type=F32
        )


def place_kernel(owned, owners, index_ref, out_ref):
    _, (down, place, group) = read_index(index_ref, owned)
    target = down // owned * 4 + place * 2 + group
    out_ref[...] = jnp.where(iota(out_ref.shape, 1) == target, 1.0, 0.0).astype(BF16)


def add_kernel(place_ref, arrived_ref, base_ref, out_ref):
    arrived = arrived_ref[...]
    high = arrived.astype(BF16)
    low = (arrived - high.astype(F32)).astype(BF16)
    place = place_ref[...]
    terms = jnp.dot(place, high, preferred_element_type=F32) + jnp.dot(
        place, low, preferred_element_type=F32
    )
    out_ref[...] = (base_ref[...] + terms).astype(BF16)


def call(kernel, shapes, ins, scratch=(), flops=0, in_hbm=(), vmem=40):
    nbytes = sum(v.size * v.dtype.itemsize for v in ins)
    return pl.pallas_call(
        kernel,
        out_shape=shapes,
        in_specs=[
            pl.BlockSpec(memory_space=pltpu.HBM if i in in_hbm else pltpu.VMEM)
            for i in range(len(ins))
        ],
        out_specs=jax.tree.map(lambda _: pl.BlockSpec(memory_space=pltpu.VMEM), shapes),
        scratch_shapes=scratch,
        compiler_params=pltpu.CompilerParams(vmem_limit_bytes=vmem * MIB),
        cost_estimate=pl.CostEstimate(flops=flops, bytes_accessed=nbytes, transcendentals=0),
    )(*ins)


def on_device(tokens, value_matrix, down, up, index):
    groups, rows_local, features = tokens.shape
    owners = lax.axis_size("dp")
    planes = lax.axis_size("tensor")
    owned, width, rank = down.shape
    columns = up.shape[2]
    rows = groups * rows_local
    shape = jax.ShapeDtypeStruct

    packed = call(
        functools.partial(pack_kernel, owned, owners),
        shape((owners, groups, 2 * width + 128), BF16),
        (index, tokens),
        [pltpu.VMEM((groups, rows_local, 2 * width), BF16), pltpu.SemaphoreType.DMA((2,))],
        in_hbm=(1,),
        vmem=62,
    )
    received = lax.all_to_all(packed, "dp", split_axis=0, concat_axis=0, tiled=True)

    down_own = down.transpose(0, 2, 1)
    sent_first, _ = lax.optimization_barrier((down_own, packed))
    down_other = lax.ppermute(sent_first, "tensor", [(i, i ^ 1) for i in range(planes)])
    base = jnp.dot(tokens.reshape(rows, features), value_matrix, preferred_element_type=F32)
    place = call(
        functools.partial(place_kernel, owned, owners), shape((rows, owners * 4), BF16), (index,)
    )

    partial, label = call(
        shrink_kernel,
        (shape((planes, owners, 128), BF16), shape((owners * 4, 128), BF16)),
        (received, down_own, down_other),
    )
    partials = lax.all_to_all(partial, "tensor", split_axis=0, concat_axis=0, tiled=True)
    terms = call(
        expand_kernel,
        shape((owners * 4, columns), F32),
        (partials, label, up.reshape(owned * rank, columns)),
    )
    arrived = lax.all_to_all(
        terms.reshape(owners, 4, columns), "dp", split_axis=0, concat_axis=0, tiled=True
    ).reshape(owners * 4, columns)
    out = call(add_kernel, shape((rows, columns), BF16), (place, arrived, base))
    return out.reshape(groups, rows_local, columns)


def solution(mesh):
    in_specs = (
        P(None, "dp", None),
        P(None, "tensor"),
        P("dp", "tensor", None),
        P("dp", None, "tensor"),
        P(None, "dp"),
    )
    out_specs = P(None, "dp", "tensor")
    return jax.shard_map(
        on_device, mesh=mesh, in_specs=in_specs, out_specs=out_specs, check_vma=False
    )
```

time: 74.7 us -> 74 us (level)
  waiting for transfers between devices: 32 us -> 29.8 us
  starting transfers between devices: 32.6 us -> 34.7 us
    all_to_all x1, waiting for transfers between devices: 5.18 us -> 3.1 us  [on_device(): lax.all_to_all(packed, 'dp', split_axis=0, concat_axis=0, tiled=True)]
    all_to_all x1, starting transfers between devices: 7.63 us -> 9.67 us  [on_device(): lax.all_to_all(terms.reshape(owners, 4, columns), 'dp', split_axis=0, con...]
where the time goes in v3:
time: 74 us; the launch traced here: 73.6 us
  starting transfers between devices  34.7 us (47%)
  waiting for transfers between devices  29.8 us (40%)
  Pallas kernels  6.1 us (8%)
  matrix products  2.92 us (4%)
    all_to_all x1, starting transfers between devices, on_device(): lax.all_to_all(packed, 'dp', split_axis=0, concat_axis=0, tiled=True)  15 us
    ppermute x1, waiting for transfers between devices, on_device(): lax.ppermute(sent_first, 'tensor', [(i, i ^ 1) for i in range(planes)])  11.7 us
    all_to_all x1, starting transfers between devices, on_device(): lax.all_to_all(terms.reshape(owners, 4, columns), 'dp', split_axis=0, con...  9.67 us
    all_to_all x1, waiting for transfers between devices, on_device(): lax.all_to_all(partial, 'tensor', split_axis=0, concat_axis=0, tiled=True)  7.52 us
    all_to_all x1, waiting for transfers between devices, on_device(): lax.all_to_all(terms.reshape(owners, 4, columns), 'dp', split_axis=0, con...  7.44 us
    all_to_all x1, starting transfers between devices, on_device(): lax.all_to_all(partial, 'tensor', split_axis=0, concat_axis=0, tiled=True)  6.82 us
    pallas_call x5, Pallas kernels, call(): pl.pallas_call(kernel, out_shape=shapes, in_specs=[pl.BlockSpec(memory_sp...  6.1 us
    ppermute x1, starting transfers between devices, on_device(): lax.ppermute(sent_first, 'tensor', [(i, i ^ 1) for i in range(planes)])  3.2 us
  transfers between devices with their start and end apart: 4, of which 4 were waited for; matrix products, arithmetic and copies ran while one was open for 4% of the time, Pallas kernels for 0%

profile of v3, /device:TPU:1, one launch (start us, length us, event | category | flops | bytes accessed | tf_op | source)
XLA Modules:
  0.0 73.6 jit_solution(17902886224355459152)
XLA Ops:
  0.0 0.0 copy-start
  0.0 2.9 %shard_map.56 = bf16[64,2,2176]{2,1,0:T(2,128)(2,1)} custom-call(s32[2,64]{1,0:T(2,128)} %index_ref.3, bf16[2,64,8192]{2,1,0:T(8,128)(2,1)} %tokens_ref.1), custom_call_target="tpu_custom_call" | custom-call | bytes 2097664 | tf_op jit(solution)/shard_map/pallas_call | solution.py:160
  2.9 0.0 copy-start.2
  2.9 0.0 copy-start.1
  2.9 15.0 %all-to-all-start = ((bf16[64,2,2176]{2,1,0:T(2,128)(2,1)}), bf16[64,2,2176]{2,1,0:T(2,128)(2,1)S(1)}, u32[]{:S(2)}, u32[]{:S(2)}) async-start(bf16[64,2,2176]{2,1,0:T(2,128)(2,1)} %shard_map.56), calls=%async_computation | async-start | bytes 1114112 | tf_op jit(solution)/shard_map/all_to_all | solution.py:191
  17.9 0.0 copy-done
  17.9 3.2 %collective-permute-start = (bf16[4,64,1024]{2,1,0:T(8,128)(2,1)S(1)}, bf16[4,64,1024]{2,1,0:T(8,128)(2,1)S(1)}, u32[]{:S(2)}, u32[]{:S(2)}) collective-permute-start(bf16[4,64,1024]{2,1,0:T(8,128)(2,1)S(1)} %bitcast.8), channel_id=1, source_target_pairs={{0,1},{1,0},{2,3},{3,2},{4,5},{5,4},{6,7},{7,6},{8,9},{9,8},{10,11... | collective-permute-start | bytes 1572872 | tf_op jit(solution)/shard_map/ppermute | solution.py:195
  21.1 11.7 %collective-permute-done.other_ref = bf16[4,64,1024]{2,1,0:T(8,128)(2,1)S(1)} collective-permute-done((bf16[4,64,1024]{2,1,0:T(8,128)(2,1)S(1)}, bf16[4,64,1024]{2,1,0:T(8,128)(2,1)S(1)}, u32[]{:S(2)}, u32[]{:S(2)}) %collective-permute-start) | collective-permute-done | bytes 524320 | tf_op jit(solution)/shard_map/ppermute | solution.py:195
  32.9 3.1 %all-to-all-done.received_ref = bf16[64,2,2176]{2,1,0:T(2,128)(2,1)S(1)} async-done(((bf16[64,2,2176]{2,1,0:T(2,128)(2,1)}), bf16[64,2,2176]{2,1,0:T(2,128)(2,1)S(1)}, u32[]{:S(2)}, u32[]{:S(2)}) %all-to-all-start) | async-done | bytes 557088 | tf_op jit(solution)/shard_map/all_to_all | solution.py:191
  36.0 1.2 %shard_map.57 = (bf16[8,64,128]{2,1,0:T(8,128)(2,1)}, bf16[256,128]{1,0:T(8,128)(2,1)S(1)}) custom-call(bf16[64,2,2176]{2,1,0:T(2,128)(2,1)S(1)} %all-to-all-done.received_ref, bf16[4,64,1024]{2,1,0:T(8,128)(2,1)S(1)} %bitcast.9, bf16[4,64,1024]{2,1,0:T(8,128)(2,1)S(1)} %collective-permute-done.other_ref), custom_call_target="tpu_custom_call" | custom-call | bytes 1605632 | tf_op jit(solution)/shard_map/pallas_call | solution.py:160
  37.2 6.8 %all-to-all-start.1 = ((bf16[8,64,128]{2,1,0:T(8,128)(2,1)}), bf16[8,64,128]{2,1,0:T(8,128)(2,1)S(1)}, u32[]{:S(2)}, u32[]{:S(2)}) async-start(bf16[8,64,128]{2,1,0:T(8,128)(2,1)} %get-tuple-element.9), calls=%async_computation.1 | async-start | bytes 262144 | tf_op jit(solution)/shard_map/all_to_all | solution.py:206
  44.0 0.0 copy-done.2
  44.0 0.3 shard_map.55.place_ref
  44.3 7.5 %all-to-all-done.1.partial_ref = bf16[8,64,128]{2,1,0:T(8,128)(2,1)S(1)} async-done(((bf16[8,64,128]{2,1,0:T(8,128)(2,1)}), bf16[8,64,128]{2,1,0:T(8,128)(2,1)S(1)}, u32[]{:S(2)}, u32[]{:S(2)}) %all-to-all-start.1) | async-done | bytes 131104 | tf_op jit(solution)/shard_map/all_to_all | solution.py:206
  51.8 0.0 copy-done.1
  51.8 0.9 %shard_map.58 = f32[256,128]{1,0:T(8,128)} custom-call(bf16[8,64,128]{2,1,0:T(8,128)(2,1)S(1)} %all-to-all-done.1.partial_ref, bf16[256,128]{1,0:T(8,128)(2,1)S(1)} %get-tuple-element.10.label_ref, bf16[256,128]{1,0:T(8,128)(2,1)S(1)} %bitcast.11), custom_call_target="tpu_custom_call" | custom-call | bytes 262144 | tf_op jit(solution)/shard_map/pallas_call | solution.py:160
  52.7 9.7 %all-to-all-start.2 = ((f32[64,4,128]{2,1,0:T(4,128)}), f32[64,4,128]{2,1,0:T(4,128)S(1)}, u32[]{:S(2)}, u32[]{:S(2)}) async-start(f32[64,4,128]{2,1,0:T(4,128)} %bitcast.2), calls=%async_computation.2 | async-start | bytes 262144 | tf_op jit(solution)/shard_map/all_to_all | solution.py:212
  62.4 2.9 %fusion.base_ref = f32[128,128]{1,0:T(8,128)S(1)} fusion(bf16[128,8192]{1,0:T(8,128)(2,1)} %bitcast.12, bf16[8192,128]{1,0:T(8,128)(2,1)} %param.6), kind=kOutput, calls=%fused_computation | convolution fusion | flops 268435456 | bytes 4259840 | tf_op jit(solution)/shard_map/dot_general | solution.py:196
  65.3 7.4 %all-to-all-done.2 = f32[64,4,128]{2,1,0:T(4,128)S(1)} async-done(((f32[64,4,128]{2,1,0:T(4,128)}), f32[64,4,128]{2,1,0:T(4,128)S(1)}, u32[]{:S(2)}, u32[]{:S(2)}) %all-to-all-start.2) | async-done | bytes 131104 | tf_op jit(solution)/shard_map/all_to_all | solution.py:212
  72.8 0.8 %shard_map.59 = bf16[128,128]{1,0:T(8,128)(2,1)} custom-call(bf16[128,256]{1,0:T(8,128)(2,1)S(1)} %shard_map.55.place_ref, f32[256,128]{1,0:T(8,128)S(1)} %bitcast.10, f32[128,128]{1,0:T(8,128)S(1)} %fusion.base_ref), custom_call_target="tpu_custom_call" | custom-call | bytes 262144 | tf_op jit(solution)/shard_map/pallas_call | solution.py:160
Async XLA Ops:
  0.0 17.9 %copy-start = (bf16[4,1024,64]{1,2,0:T(8,128)(2,1)S(1)}, bf16[4,1024,64]{1,2,0:T(8,128)(2,1)}, u32[]{:S(2)}) copy-start(bf16[4,1024,64]{1,2,0:T(8,128)(2,1)} %param.7) | copy-start | bytes 1572868
  2.9 41.1 %copy-start.2 = (s32[2,64]{1,0:T(2,128)S(1)}, s32[2,64]{1,0:T(2,128)}, u32[]{:S(2)}) copy-start(s32[2,64]{1,0:T(2,128)} %index_ref.3) | copy-start | bytes 1540
  2.9 48.9 %copy-start.1 = (bf16[4,64,128]{2,1,0:T(8,128)(2,1)S(1)}, bf16[4,64,128]{2,1,0:T(8,128)(2,1)}, u32[]{:S(2)}) copy-start(bf16[4,64,128]{2,1,0:T(8,128)(2,1)} %param.8) | copy-start | bytes 196612
  2.9 33.0 %all-to-all-start = ((bf16[64,2,2176]{2,1,0:T(2,128)(2,1)}), bf16[64,2,2176]{2,1,0:T(2,128)(2,1)S(1)}, u32[]{:S(2)}, u32[]{:S(2)}) async-start(bf16[64,2,2176]{2,1,0:T(2,128)(2,1)} %shard_map.56), calls=%async_computation | async-start | bytes 1114112 | tf_op jit(solution)/shard_map/all_to_all | solution.py:191
  17.9 14.9 %collective-permute-start = (bf16[4,64,1024]{2,1,0:T(8,128)(2,1)S(1)}, bf16[4,64,1024]{2,1,0:T(8,128)(2,1)S(1)}, u32[]{:S(2)}, u32[]{:S(2)}) collective-permute-start(bf16[4,64,1024]{2,1,0:T(8,128)(2,1)S(1)} %bitcast.8), channel_id=1, source_target_pairs={{0,1},{1,0},{2,3},{3,2},{4,5},{5,4},{6,7},{7,6},{8,9},{9,8},{10,11... | collective-permute-start | bytes 1572872 | tf_op jit(solution)/shard_map/ppermute | solution.py:195
  37.2 14.7 %all-to-all-start.1 = ((bf16[8,64,128]{2,1,0:T(8,128)(2,1)}), bf16[8,64,128]{2,1,0:T(8,128)(2,1)S(1)}, u32[]{:S(2)}, u32[]{:S(2)}) async-start(bf16[8,64,128]{2,1,0:T(8,128)(2,1)} %get-tuple-element.9), calls=%async_computation.1 | async-start | bytes 262144 | tf_op jit(solution)/shard_map/all_to_all | solution.py:206
  52.7 20.0 %all-to-all-start.2 = ((f32[64,4,128]{2,1,0:T(4,128)}), f32[64,4,128]{2,1,0:T(4,128)S(1)}, u32[]{:S(2)}, u32[]{:S(2)}) async-start(f32[64,4,128]{2,1,0:T(4,128)} %bitcast.2), calls=%async_computation.2 | async-start | bytes 262144 | tf_op jit(solution)/shard_map/all_to_all | solution.py:212

commit v4 on v3

v4 whole, which is shorter than its diff:
```python
import functools

import jax
import jax.numpy as jnp
from jax import lax
from jax.experimental import pallas as pl
from jax.experimental.pallas import tpu as pltpu
from jax.sharding import PartitionSpec as P

BF16, F32, I32 = jnp.bfloat16, jnp.float32, jnp.int32
MIB = 1024 * 1024


def iota(shape, dim):
    return lax.broadcasted_iota(I32, shape, dim)


def read_index(index_ref, owned):
    along = jnp.concatenate([index_ref[0:1, :], index_ref[1:2, :]], axis=1)
    rows = along.shape[1]
    shift = owned.bit_length() - 1
    assert owned == 1 << shift
    key = (along >> shift) * 2 + jnp.where(iota((1, rows), 1) >= rows // 2, 1, 0)
    wide = jnp.broadcast_to(key, (rows, rows))
    line, column = iota((rows, rows), 0), iota((rows, rows), 1)
    same = jnp.sum(jnp.where(line == column, wide, 0).astype(F32), axis=1, keepdims=True)
    earlier = (wide.astype(F32) == same) & (line < column)
    place = jnp.sum(jnp.where(earlier, 1.0, 0.0), axis=0, keepdims=True)
    return wide, place, ((along & (owned - 1)) + 1).astype(F32)


def spread(first, second):
    first, second = (v.reshape(v.shape[0] // 8, 8, 128) for v in (first, second))
    pair = iota(first.shape, 1) // 2

    def turn(total, by):
        return pltpu.roll(total, by, 1)

    def pick(*pieces):
        out = pieces[0]
        for d in range(1, 4):
            out = jnp.where(pair == d, pieces[d], out)
        return out

    even = pick(first, turn(second, 2), turn(first, 2), turn(second, 4))
    odd = pick(turn(first, 4), turn(second, 6), turn(first, 6), second)
    return jnp.stack([even, odd], axis=1).reshape(first.shape[0] * 16, 128)


def pack_kernel(
    owned, planes, index_ref, tokens_ref, down_ref, out_ref, lower_ref, upper_ref, held, indices, sems
):
    width = down_ref.shape[2]
    half = width // 2
    features = planes * width
    plane = lax.axis_index("tensor")
    parity = plane % 2
    starts = [(plane * width + features - half) % features, plane * width]
    starts.append((plane * width + width) % features)
    spans = [(0, half), (half, width), (half + width, half)]
    copies = [pltpu.make_async_copy(index_ref, indices, sems.at[0])]
    for e in range(3):
        start, (to, size) = pl.multiple_of(starts[e], half), spans[e]
        copies.append(
            pltpu.make_async_copy(
                tokens_ref.at[:, :, pl.ds(start, size)],
                held.at[:, :, to : to + size],
                sems.at[1 + e],
            )
        )
    copies.append(pltpu.make_async_copy(down_ref.at[:, :, :half], lower_ref, sems.at[4]))
    copies.append(pltpu.make_async_copy(down_ref.at[:, :, half:], upper_ref, sems.at[5]))
    for copy in copies:
        copy.start()
    copies[0].wait()
    wide, place, label = read_index(indices, owned)
    rows = wide.shape[0]
    line, column = iota((rows, rows), 0), iota((rows, rows), 1)
    hit = line == wide
    label = jnp.broadcast_to(label, (rows, rows))
    labels = [
        jnp.sum(jnp.where(hit & (place == p), label, 0.0), axis=1, keepdims=True)
        for p in (0.0, 1.0)
    ]
    labels = jnp.where(column < 64, labels[0], labels[1]).astype(BF16)
    out_ref[:, :, 2 * width :] = labels.reshape(rows // 2, 2, 128)
    select = jnp.where(hit & (place == parity.astype(F32)), 1.0, 0.0).astype(BF16)
    for copy in copies[1:4]:
        copy.wait()
    tokens = held[...].reshape(rows, 2 * width)
    packed = jnp.dot(select, tokens, preferred_element_type=F32).astype(BF16)
    out_ref[:, :, : 2 * width] = packed.reshape(rows // 2, 2, 2 * width)
    for copy in copies[4:]:
        copy.wait()


def shrink_kernel(received_ref, before_ref, own_ref, after_ref, partial_ref, label_ref):
    shards, groups, width = received_ref.shape
    width = (width - 128) // 2
    lines = shards * groups
    parity = lax.axis_index("tensor") % 2
    product, at = None, 0
    for weight_ref in (before_ref, own_ref, after_ref):
        size = weight_ref.shape[2]
        rows = received_ref[:, :, at : at + size].reshape(lines, size)
        mine = lax.dot_general(
            rows,
            weight_ref[...].reshape(256, size),
            (((1,), (1,)), ((), ())),
            preferred_element_type=F32,
        )
        product = mine if at == 0 else product + mine
        at += size
    label = received_ref[:, :, 2 * width :].reshape(lines, 128).astype(F32)
    turned = pltpu.roll(label, 64, 1)
    upper = iota((lines, 128), 1) // 64
    here = jnp.where(upper == parity, label, turned)
    total = jnp.where(here == upper.astype(F32) + 1.0, product[:, :128], 0.0)
    total = total + jnp.where(here == upper.astype(F32) + 3.0, product[:, 128:], 0.0)
    total = total + pltpu.roll(total, 64, 1)
    half = lines // 2
    packed = jnp.where(upper[:half] == 0, total[:half], total[half:]).astype(BF16)
    for peer in range(partial_ref.shape[0]):
        partial_ref[peer] = packed
    low = jnp.where(upper == 0, label, turned)
    high = jnp.where(upper == 0, turned, label)
    label_ref[...] = spread(low, high).astype(BF16)


def expand_kernel(partial_ref, label_ref, up_ref, out_ref):
    sums = []
    for p in range(2):
        total = partial_ref[p].astype(F32)
        for peer in range(p + 2, partial_ref.shape[0], 2):
            total = total + partial_ref[peer].astype(F32)
        sums.append(total)
    total = spread(*sums)
    turned = pltpu.roll(total, 64, 1)
    upper = iota(total.shape, 1) // 64
    lines = total.shape[0]
    for e in range(2):
        row = jnp.where(upper == e, total, turned)
        label = label_ref[e * lines : (e + 1) * lines].astype(F32)
        left = jnp.where(label == upper.astype(F32) + 1.0, row, 0.0)
        right = jnp.where(label == upper.astype(F32) + 3.0, row, 0.0)
        wide = jnp.concatenate([left, right], axis=1).astype(BF16)
        out_ref[e * lines : (e + 1) * lines] = jnp.dot(
            wide, up_ref[...], preferred_element_type=F32
        )


def place_kernel(owned, index_ref, out_ref):
    wide, place, _ = read_index(index_ref, owned)
    rows = wide.shape[0]
    key = wide[:1]
    target = (key >> 1) * 4 + place.astype(I32) * 2 + (key & 1)
    line, column = iota((rows, rows), 0), iota((rows, rows), 1)
    target = jnp.broadcast_to(target, (rows, rows))
    target = jnp.sum(jnp.where(line == column, target, 0).astype(F32), axis=1, keepdims=True)
    out_ref[...] = jnp.where(iota(out_ref.shape, 1).astype(F32) == target, 1.0, 0.0).astype(BF16)


def add_kernel(place_ref, arrived_ref, base_ref, out_ref):
    arrived = arrived_ref[...]
    high = arrived.astype(BF16)
    low = (arrived - high.astype(F32)).astype(BF16)
    place = place_ref[...]
    terms = jnp.dot(place, high, preferred_element_type=F32) + jnp.dot(
        place, low, preferred_element_type=F32
    )
    out_ref[...] = (base_ref[...] + terms).astype(BF16)


def call(kernel, shapes, ins, scratch=(), in_hbm=(), out_hbm=(), vmem=40):
    nbytes = sum(v.size * v.dtype.itemsize for v in ins)

    def spec(hbm):
        return pl.BlockSpec(memory_space=pltpu.HBM if hbm else pltpu.VMEM)

    return pl.pallas_call(
        kernel,
        out_shape=shapes,
        in_specs=[spec(i in in_hbm) for i in range(len(ins))],
        out_specs=[spec(i in out_hbm) for i in range(len(shapes))],
        scratch_shapes=scratch,
        compiler_params=pltpu.CompilerParams(vmem_limit_bytes=vmem * MIB),
        cost_estimate=pl.CostEstimate(flops=0, bytes_accessed=nbytes, transcendentals=0),
    )(*ins)


def on_device(tokens, value_matrix, down, up, index):
    groups, rows_local, features = tokens.shape
    owners = lax.axis_size("dp")
    planes = lax.axis_size("tensor")
    owned, width, rank = down.shape
    columns = up.shape[2]
    rows = groups * rows_local
    shape = jax.ShapeDtypeStruct

    down_own = down.transpose(0, 2, 1)
    piece = shape((owned, rank, width // 2), BF16)
    packed, lower, upper = call(
        functools.partial(pack_kernel, owned, planes),
        [shape((owners, groups, 2 * width + 128), BF16), piece, piece],
        (index, tokens, down_own),
        [
            pltpu.VMEM((groups, rows_local, 2 * width), BF16),
            pltpu.VMEM(index.shape, I32),
            pltpu.SemaphoreType.DMA((6,)),
        ],
        in_hbm=(0, 1, 2),
        out_hbm=(1, 2),
        vmem=62,
    )
    received = lax.all_to_all(packed, "dp", split_axis=0, concat_axis=0, tiled=True)
    before = lax.ppermute(upper, "tensor", [(i, (i + 1) % planes) for i in range(planes)])
    after = lax.ppermute(lower, "tensor", [(i, (i - 1) % planes) for i in range(planes)])

    base = jnp.dot(tokens.reshape(rows, features), value_matrix, preferred_element_type=F32)
    (place,) = call(
        functools.partial(place_kernel, owned), [shape((rows, owners * 4), BF16)], (index,)
    )
    partial, label = call(
        shrink_kernel,
        [shape((planes, owners, 128), BF16), shape((owners * 4, 128), BF16)],
        (received, before, down_own, after),
    )
    partials = lax.all_to_all(partial, "tensor", split_axis=0, concat_axis=0, tiled=True)
    (terms,) = call(
        expand_kernel,
        [shape((owners * 4, columns), F32)],
        (partials, label, up.reshape(owned * rank, columns)),
    )
    arrived = lax.all_to_all(
        terms.reshape(owners, 4, columns), "dp", split_axis=0, concat_axis=0, tiled=True
    ).reshape(owners * 4, columns)
    (out,) = call(add_kernel, [shape((rows, columns), BF16)], (place, arrived, base))
    return out.reshape(groups, rows_local, columns)


def solution(mesh):
    in_specs = (
        P(None, "dp", None),
        P(None, "tensor"),
        P("dp", "tensor", None),
        P("dp", None, "tensor"),
        P(None, "dp"),
    )
    out_specs = P(None, "dp", "tensor")
    return jax.shard_map(
        on_device, mesh=mesh, in_specs=in_specs, out_specs=out_specs, check_vma=False
    )
```

time: 74 us -> 87.1 us (1.18)
  Pallas kernels: 6.1 us -> 21 us
  waiting for transfers between devices: 29.8 us -> 26 us
  starting transfers between devices: 34.7 us -> 36.6 us
    pallas_call x5, Pallas kernels: 6.1 us -> 21 us  [call(): pl.pallas_call(kernel, out_shape=shapes, in_specs=[spec(i in in_hbm) for...]
    ppermute x1 -> x2, waiting for transfers between devices: 11.7 us -> 5.52 us  [the longest x1 4.55 us: on_device(): lax.ppermute(upper, 'tensor', [(i, (i + 1) % planes) for i in range(plane...]
    ppermute x1 -> x2, starting transfers between devices: 3.2 us -> 7.02 us  [the longest x1 3.81 us: on_device(): lax.ppermute(lower, 'tensor', [(i, (i - 1) % planes) for i in range(plane...]
    all_to_all x1, waiting for transfers between devices: 3.1 us -> 5.5 us  [on_device(): lax.all_to_all(packed, 'dp', split_axis=0, concat_axis=0, tiled=True)]
    all_to_all x1, starting transfers between devices: 9.67 us -> 7.77 us  [on_device(): lax.all_to_all(terms.reshape(owners, 4, columns), 'dp', split_axis=0, con...]
  transfers between devices with their start and end apart: 4 -> 5, of which waited for: 4 -> 5; matrix products, arithmetic and copies ran while one was open for 4% -> 3% of each run, Pallas kernels for 0% -> 0%
where the time goes in v4:
time: 87.1 us; the launch traced here: 86.6 us
  starting transfers between devices  36.6 us (42%)
  waiting for transfers between devices  26 us (30%)
  Pallas kernels  21 us (24%)
  matrix products  2.92 us (3%)
    pallas_call x5, Pallas kernels, call(): pl.pallas_call(kernel, out_shape=shapes, in_specs=[spec(i in in_hbm) for...  21 us
    all_to_all x1, starting transfers between devices, on_device(): lax.all_to_all(packed, 'dp', split_axis=0, concat_axis=0, tiled=True)  15 us
    all_to_all x1, starting transfers between devices, on_device(): lax.all_to_all(terms.reshape(owners, 4, columns), 'dp', split_axis=0, con...  7.77 us
    all_to_all x1, waiting for transfers between devices, on_device(): lax.all_to_all(partial, 'tensor', split_axis=0, concat_axis=0, tiled=True)  7.56 us
    all_to_all x1, waiting for transfers between devices, on_device(): lax.all_to_all(terms.reshape(owners, 4, columns), 'dp', split_axis=0, con...  7.44 us
    all_to_all x1, starting transfers between devices, on_device(): lax.all_to_all(partial, 'tensor', split_axis=0, concat_axis=0, tiled=True)  6.82 us
    all_to_all x1, waiting for transfers between devices, on_device(): lax.all_to_all(packed, 'dp', split_axis=0, concat_axis=0, tiled=True)  5.5 us
    ppermute x1, waiting for transfers between devices, on_device(): lax.ppermute(upper, 'tensor', [(i, (i + 1) % planes) for i in range(plane...  4.55 us
  transfers between devices with their start and end apart: 5, of which 5 were waited for; matrix products, arithmetic and copies ran while one was open for 3% of the time, Pallas kernels for 0%

profile of v4, /device:TPU:1, one launch (start us, length us, event | category | flops | bytes accessed | tf_op | source)
XLA Modules:
  0.0 86.6 jit_solution(12406616286422838787)
XLA Ops:
  0.0 0.0 copy-start
  0.0 17.8 %shard_map.56 = (bf16[64,2,2176]{2,1,0:T(2,128)(2,1)}, bf16[4,64,512]{2,1,0:T(8,128)(2,1)}, bf16[4,64,512]{2,1,0:T(8,128)(2,1)}) custom-call(s32[2,64]{1,0:T(2,128)} %index_ref.3, bf16[2,64,8192]{2,1,0:T(8,128)(2,1)} %tokens_ref.1, bf16[4,64,1024]{2,1,0:T(8,128)(2,1)} %bitcast.8), custom_call_target="tpu_custom_call" | custom-call | bytes 2621952 | tf_op jit(solution)/shard_map/pallas_call | solution.py:180
  17.9 0.0 copy-start.2
  17.9 0.0 copy-start.1
  17.9 15.0 %all-to-all-start = ((bf16[64,2,2176]{2,1,0:T(2,128)(2,1)}), bf16[64,2,2176]{2,1,0:T(2,128)(2,1)S(1)}, u32[]{:S(2)}, u32[]{:S(2)}) async-start(bf16[64,2,2176]{2,1,0:T(2,128)(2,1)} %get-tuple-element.10), calls=%async_computation | async-start | bytes 1114112 | tf_op jit(solution)/shard_map/all_to_all | solution.py:215
  32.9 3.2 %collective-permute-start = (bf16[4,64,512]{2,1,0:T(8,128)(2,1)}, bf16[4,64,512]{2,1,0:T(8,128)(2,1)S(1)}, u32[]{:S(2)}, u32[]{:S(2)}) collective-permute-start(bf16[4,64,512]{2,1,0:T(8,128)(2,1)} %get-tuple-element.11), channel_id=1, source_target_pairs={{0,1},{1,2},{2,3},{3,4},{4,5},{5,6},{6,7},{7,0},{8,9},{9,10},{10,1... | collective-permute-start | bytes 786440 | tf_op jit(solution)/shard_map/ppermute | solution.py:216
  36.1 3.8 %collective-permute-start.1 = (bf16[4,64,512]{2,1,0:T(8,128)(2,1)}, bf16[4,64,512]{2,1,0:T(8,128)(2,1)S(1)}, u32[]{:S(2)}, u32[]{:S(2)}) collective-permute-start(bf16[4,64,512]{2,1,0:T(8,128)(2,1)} %get-tuple-element.12), channel_id=1, source_target_pairs={{0,7},{1,0},{2,1},{3,2},{4,3},{5,4},{6,5},{7,6},{8,15},{9,8},{10,9... | collective-permute-start | bytes 786440 | tf_op jit(solution)/shard_map/ppermute | solution.py:217
  39.9 4.6 %collective-permute-done.before_ref = bf16[4,64,512]{2,1,0:T(8,128)(2,1)S(1)} collective-permute-done((bf16[4,64,512]{2,1,0:T(8,128)(2,1)}, bf16[4,64,512]{2,1,0:T(8,128)(2,1)S(1)}, u32[]{:S(2)}, u32[]{:S(2)}) %collective-permute-start) | collective-permute-done | bytes 262176 | tf_op jit(solution)/shard_map/ppermute | solution.py:216
  44.4 1.0 %collective-permute-done.1.after_ref = bf16[4,64,512]{2,1,0:T(8,128)(2,1)S(1)} collective-permute-done((bf16[4,64,512]{2,1,0:T(8,128)(2,1)}, bf16[4,64,512]{2,1,0:T(8,128)(2,1)S(1)}, u32[]{:S(2)}, u32[]{:S(2)}) %collective-permute-start.1) | collective-permute-done | bytes 262176 | tf_op jit(solution)/shard_map/ppermute | solution.py:217
  45.4 5.5 %all-to-all-done.received_ref = bf16[64,2,2176]{2,1,0:T(2,128)(2,1)S(1)} async-done(((bf16[64,2,2176]{2,1,0:T(2,128)(2,1)}), bf16[64,2,2176]{2,1,0:T(2,128)(2,1)S(1)}, u32[]{:S(2)}, u32[]{:S(2)}) %all-to-all-start) | async-done | bytes 557088 | tf_op jit(solution)/shard_map/all_to_all | solution.py:215
  50.9 0.0 copy-done
  50.9 1.2 %shard_map.57 = (bf16[8,64,128]{2,1,0:T(8,128)(2,1)}, bf16[256,128]{1,0:T(8,128)(2,1)S(1)}) custom-call(bf16[64,2,2176]{2,1,0:T(2,128)(2,1)S(1)} %all-to-all-done.received_ref, bf16[4,64,512]{2,1,0:T(8,128)(2,1)S(1)} %collective-permute-done.before_ref, bf16[4,64,1024]{2,1,0:T(8,128)(2,1)S(1)} %bitcast.9, ...), custom_call_target="tpu_custom_call" | custom-call | bytes 1605632 | tf_op jit(solution)/shard_map/pallas_call | solution.py:180
  52.1 6.8 %all-to-all-start.1 = ((bf16[8,64,128]{2,1,0:T(8,128)(2,1)}), bf16[8,64,128]{2,1,0:T(8,128)(2,1)S(1)}, u32[]{:S(2)}, u32[]{:S(2)}) async-start(bf16[8,64,128]{2,1,0:T(8,128)(2,1)} %get-tuple-element.13), calls=%async_computation.1 | async-start | bytes 262144 | tf_op jit(solution)/shard_map/all_to_all | solution.py:228
  59.0 0.0 copy-done.2
  59.0 0.3 shard_map.55.place_ref
  59.2 7.6 %all-to-all-done.1.partial_ref = bf16[8,64,128]{2,1,0:T(8,128)(2,1)S(1)} async-done(((bf16[8,64,128]{2,1,0:T(8,128)(2,1)}), bf16[8,64,128]{2,1,0:T(8,128)(2,1)S(1)}, u32[]{:S(2)}, u32[]{:S(2)}) %all-to-all-start.1) | async-done | bytes 131104 | tf_op jit(solution)/shard_map/all_to_all | solution.py:228
  66.8 0.0 copy-done.1
  66.8 0.9 %shard_map.58 = f32[256,128]{1,0:T(8,128)} custom-call(bf16[8,64,128]{2,1,0:T(8,128)(2,1)S(1)} %all-to-all-done.1.partial_ref, bf16[256,128]{1,0:T(8,128)(2,1)S(1)} %get-tuple-element.14.label_ref, bf16[256,128]{1,0:T(8,128)(2,1)S(1)} %bitcast.11), custom_call_target="tpu_custom_call" | custom-call | bytes 262144 | tf_op jit(solution)/shard_map/pallas_call | solution.py:180
  67.7 7.8 %all-to-all-start.2 = ((f32[64,4,128]{2,1,0:T(4,128)}), f32[64,4,128]{2,1,0:T(4,128)S(1)}, u32[]{:S(2)}, u32[]{:S(2)}) async-start(f32[64,4,128]{2,1,0:T(4,128)} %bitcast.2), calls=%async_computation.2 | async-start | bytes 262144 | tf_op jit(solution)/shard_map/all_to_all | solution.py:234
  75.5 2.9 %fusion.base_ref = f32[128,128]{1,0:T(8,128)S(1)} fusion(bf16[128,8192]{1,0:T(8,128)(2,1)} %bitcast.12, bf16[8192,128]{1,0:T(8,128)(2,1)} %param.6), kind=kOutput, calls=%fused_computation | convolution fusion | flops 268435456 | bytes 4259840 | tf_op jit(solution)/shard_map/dot_general | solution.py:219
  78.4 7.4 %all-to-all-done.2 = f32[64,4,128]{2,1,0:T(4,128)S(1)} async-done(((f32[64,4,128]{2,1,0:T(4,128)}), f32[64,4,128]{2,1,0:T(4,128)S(1)}, u32[]{:S(2)}, u32[]{:S(2)}) %all-to-all-start.2) | async-done | bytes 131104 | tf_op jit(solution)/shard_map/all_to_all | solution.py:234
  85.8 0.8 shard_map.59
Async XLA Ops:
  0.0 50.9 %copy-start = (bf16[4,1024,64]{1,2,0:T(8,128)(2,1)S(1)}, bf16[4,1024,64]{1,2,0:T(8,128)(2,1)}, u32[]{:S(2)}) copy-start(bf16[4,1024,64]{1,2,0:T(8,128)(2,1)} %param.7) | copy-start | bytes 1572868
  17.9 41.1 %copy-start.2 = (s32[2,64]{1,0:T(2,128)S(1)}, s32[2,64]{1,0:T(2,128)}, u32[]{:S(2)}) copy-start(s32[2,64]{1,0:T(2,128)} %index_ref.3) | copy-start | bytes 1540
  17.9 48.9 %copy-start.1 = (bf16[4,64,128]{2,1,0:T(8,128)(2,1)S(1)}, bf16[4,64,128]{2,1,0:T(8,128)(2,1)}, u32[]{:S(2)}) copy-start(bf16[4,64,128]{2,1,0:T(8,128)(2,1)} %param.8) | copy-start | bytes 196612
  17.9 33.0 %all-to-all-start = ((bf16[64,2,2176]{2,1,0:T(2,128)(2,1)}), bf16[64,2,2176]{2,1,0:T(2,128)(2,1)S(1)}, u32[]{:S(2)}, u32[]{:S(2)}) async-start(bf16[64,2,2176]{2,1,0:T(2,128)(2,1)} %get-tuple-element.10), calls=%async_computation | async-start | bytes 1114112 | tf_op jit(solution)/shard_map/all_to_all | solution.py:215
  32.9 11.6 %collective-permute-start = (bf16[4,64,512]{2,1,0:T(8,128)(2,1)}, bf16[4,64,512]{2,1,0:T(8,128)(2,1)S(1)}, u32[]{:S(2)}, u32[]{:S(2)}) collective-permute-start(bf16[4,64,512]{2,1,0:T(8,128)(2,1)} %get-tuple-element.11), channel_id=1, source_target_pairs={{0,1},{1,2},{2,3},{3,4},{4,5},{5,6},{6,7},{7,0},{8,9},{9,10},{10,1... | collective-permute-start | bytes 786440 | tf_op jit(solution)/shard_map/ppermute | solution.py:216
  36.1 9.3 %collective-permute-start.1 = (bf16[4,64,512]{2,1,0:T(8,128)(2,1)}, bf16[4,64,512]{2,1,0:T(8,128)(2,1)S(1)}, u32[]{:S(2)}, u32[]{:S(2)}) collective-permute-start(bf16[4,64,512]{2,1,0:T(8,128)(2,1)} %get-tuple-element.12), channel_id=1, source_target_pairs={{0,7},{1,0},{2,1},{3,2},{4,3},{5,4},{6,5},{7,6},{8,15},{9,8},{10,9... | collective-permute-start | bytes 786440 | tf_op jit(solution)/shard_map/ppermute | solution.py:217
  52.1 14.7 %all-to-all-start.1 = ((bf16[8,64,128]{2,1,0:T(8,128)(2,1)}), bf16[8,64,128]{2,1,0:T(8,128)(2,1)S(1)}, u32[]{:S(2)}, u32[]{:S(2)}) async-start(bf16[8,64,128]{2,1,0:T(8,128)(2,1)} %get-tuple-element.13), calls=%async_computation.1 | async-start | bytes 262144 | tf_op jit(solution)/shard_map/all_to_all | solution.py:228
  67.7 18.1 %all-to-all-start.2 = ((f32[64,4,128]{2,1,0:T(4,128)}), f32[64,4,128]{2,1,0:T(4,128)S(1)}, u32[]{:S(2)}, u32[]{:S(2)}) async-start(f32[64,4,128]{2,1,0:T(4,128)} %bitcast.2), calls=%async_computation.2 | async-start | bytes 262144 | tf_op jit(solution)/shard_map/all_to_all | solution.py:234

commit v5 on v4

--- a/solution.py
+++ b/solution.py
@@ -47,12 +47,10 @@
     return jnp.stack([even, odd], axis=1).reshape(first.shape[0] * 16, 128)
 
 
-def pack_kernel(
-    owned, planes, index_ref, tokens_ref, down_ref, out_ref, lower_ref, upper_ref, held, indices, sems
-):
-    width = down_ref.shape[2]
+def pack_kernel(owned, planes, index_ref, tokens_ref, out_ref, held, indices, sems):
+    features = tokens_ref.shape[2]
+    width = features // planes
     half = width // 2
-    features = planes * width
     plane = lax.axis_index("tensor")
     parity = plane % 2
     starts = [(plane * width + features - half) % features, plane * width]
@@ -68,8 +66,6 @@
                 sems.at[1 + e],
             )
         )
-    copies.append(pltpu.make_async_copy(down_ref.at[:, :, :half], lower_ref, sems.at[4]))
-    copies.append(pltpu.make_async_copy(down_ref.at[:, :, half:], upper_ref, sems.at[5]))
     for copy in copies:
         copy.start()
     copies[0].wait()
@@ -85,13 +81,11 @@
     labels = jnp.where(column < 64, labels[0], labels[1]).astype(BF16)
     out_ref[:, :, 2 * width :] = labels.reshape(rows // 2, 2, 128)
     select = jnp.where(hit & (place == parity.astype(F32)), 1.0, 0.0).astype(BF16)
-    for copy in copies[1:4]:
+    for copy in copies[1:]:
         copy.wait()
     tokens = held[...].reshape(rows, 2 * width)
     packed = jnp.dot(select, tokens, preferred_element_type=F32).astype(BF16)
     out_ref[:, :, : 2 * width] = packed.reshape(rows // 2, 2, 2 * width)
-    for copy in copies[4:]:
-        copy.wait()
 
 
 def shrink_kernel(received_ref, before_ref, own_ref, after_ref, partial_ref, label_ref):
@@ -171,7 +165,7 @@
     out_ref[...] = (base_ref[...] + terms).astype(BF16)
 
 
-def call(kernel, shapes, ins, scratch=(), in_hbm=(), out_hbm=(), vmem=40):
+def call(kernel, shapes, ins, scratch=(), in_hbm=(), vmem=40):
     nbytes = sum(v.size * v.dtype.itemsize for v in ins)
 
     def spec(hbm):
@@ -181,7 +175,7 @@
         kernel,
         out_shape=shapes,
         in_specs=[spec(i in in_hbm) for i in range(len(ins))],
-        out_specs=[spec(i in out_hbm) for i in range(len(shapes))],
+        out_specs=[spec(False) for _ in shapes],
         scratch_shapes=scratch,
         compiler_params=pltpu.CompilerParams(vmem_limit_bytes=vmem * MIB),
         cost_estimate=pl.CostEstimate(flops=0, bytes_accessed=nbytes, transcendentals=0),
@@ -197,22 +191,23 @@
     rows = groups * rows_local
     shape = jax.ShapeDtypeStruct
 
-    down_own = down.transpose(0, 2, 1)
-    piece = shape((owned, rank, width // 2), BF16)
-    packed, lower, upper = call(
+    (packed,) = call(
         functools.partial(pack_kernel, owned, planes),
-        [shape((owners, groups, 2 * width + 128), BF16), piece, piece],
-        (index, tokens, down_own),
+        [shape((owners, groups, 2 * width + 128), BF16)],
+        (index, tokens),
         [
             pltpu.VMEM((groups, rows_local, 2 * width), BF16),
             pltpu.VMEM(index.shape, I32),
-            pltpu.SemaphoreType.DMA((6,)),
+            pltpu.SemaphoreType.DMA((4,)),
         ],
-        in_hbm=(0, 1, 2),
-        out_hbm=(1, 2),
+        in_hbm=(0, 1),
         vmem=62,
     )
     received = lax.all_to_all(packed, "dp", split_axis=0, concat_axis=0, tiled=True)
+
+    down_own = down.transpose(0, 2, 1)
+    later, _ = lax.optimization_barrier((down_own, packed))
+    upper, lower = later[:, :, width // 2 :], later[:, :, : width // 2]
     before = lax.ppermute(upper, "tensor", [(i, (i + 1) % planes) for i in range(planes)])
     after = lax.ppermute(lower, "tensor", [(i, (i - 1) % planes) for i in range(planes)])
 

time: 87.1 us -> 71.5 us (0.82)
  Pallas kernels: 21 us -> 5.43 us
    pallas_call x5, Pallas kernels: 21 us -> 5.43 us  [call(): pl.pallas_call(kernel, out_shape=shapes, in_specs=[spec(i in in_hbm) for...]
  transfers between devices with their start and end apart: 5 -> 5, of which waited for: 5 -> 5; matrix products, arithmetic and copies ran while one was open for 3% -> 4% of each run, Pallas kernels for 0% -> 0%
where the time goes in v5:
time: 71.5 us; the launch traced here: 71 us
  starting transfers between devices  36.6 us (51%)
  waiting for transfers between devices  26 us (36%)
  Pallas kernels  5.43 us (8%)
  matrix products  2.92 us (4%)
    all_to_all x1, starting transfers between devices, on_device(): lax.all_to_all(packed, 'dp', split_axis=0, concat_axis=0, tiled=True)  15 us
    all_to_all x1, starting transfers between devices, on_device(): lax.all_to_all(terms.reshape(owners, 4, columns), 'dp', split_axis=0, con...  7.77 us
    all_to_all x1, waiting for transfers between devices, on_device(): lax.all_to_all(partial, 'tensor', split_axis=0, concat_axis=0, tiled=True)  7.56 us
    all_to_all x1, waiting for transfers between devices, on_device(): lax.all_to_all(terms.reshape(owners, 4, columns), 'dp', split_axis=0, con...  7.44 us
    all_to_all x1, starting transfers between devices, on_device(): lax.all_to_all(partial, 'tensor', split_axis=0, concat_axis=0, tiled=True)  6.82 us
    all_to_all x1, waiting for transfers between devices, on_device(): lax.all_to_all(packed, 'dp', split_axis=0, concat_axis=0, tiled=True)  5.76 us
    pallas_call x5, Pallas kernels, call(): pl.pallas_call(kernel, out_shape=shapes, in_specs=[spec(i in in_hbm) for...  5.43 us
    ppermute x1, waiting for transfers between devices, on_device(): lax.ppermute(upper, 'tensor', [(i, (i + 1) % planes) for i in range(plane...  4.34 us
  transfers between devices with their start and end apart: 5, of which 5 were waited for; matrix products, arithmetic and copies ran while one was open for 4% of the time, Pallas kernels for 0%

profile of v5, /device:TPU:1, one launch (start us, length us, event | category | flops | bytes accessed | tf_op | source)
XLA Modules:
  0.0 71.0 jit_solution(12963693581563429847)
XLA Ops:
  0.0 0.0 copy-start
  0.0 2.3 %shard_map.56 = bf16[64,2,2176]{2,1,0:T(2,128)(2,1)} custom-call(s32[2,64]{1,0:T(2,128)} %index_ref.3, bf16[2,64,8192]{2,1,0:T(8,128)(2,1)} %tokens_ref.1), custom_call_target="tpu_custom_call" | custom-call | bytes 2097664 | tf_op jit(solution)/shard_map/pallas_call | solution.py:174
  2.3 0.0 copy-start.2
  2.3 0.0 copy-start.1
  2.3 15.0 %all-to-all-start = ((bf16[64,2,2176]{2,1,0:T(2,128)(2,1)}), bf16[64,2,2176]{2,1,0:T(2,128)(2,1)S(1)}, u32[]{:S(2)}, u32[]{:S(2)}) async-start(bf16[64,2,2176]{2,1,0:T(2,128)(2,1)} %shard_map.56), calls=%async_computation | async-start | bytes 1114112 | tf_op jit(solution)/shard_map/all_to_all | solution.py:206
  17.3 0.0 copy-done
  17.3 3.2 %collective-permute-start = (bf16[4,64,512]{2,1,0:T(8,128)(2,1)S(1)}, bf16[4,64,512]{2,1,0:T(8,128)(2,1)S(1)}, u32[]{:S(2)}, u32[]{:S(2)}) collective-permute-start(bf16[4,64,512]{2,1,0:T(8,128)(2,1)S(1)} %get-tuple-element.12), channel_id=1, source_target_pairs={{0,1},{1,2},{2,3},{3,4},{4,5},{5,6},{6,7},{7,0},{8,9},{9,10},{10,1... | collective-permute-start | bytes 786440 | tf_op jit(solution)/shard_map/ppermute | solution.py:211
  20.5 3.8 %collective-permute-start.1 = (bf16[4,64,512]{2,1,0:T(8,128)(2,1)S(1)}, bf16[4,64,512]{2,1,0:T(8,128)(2,1)S(1)}, u32[]{:S(2)}, u32[]{:S(2)}) collective-permute-start(bf16[4,64,512]{2,1,0:T(8,128)(2,1)S(1)} %get-tuple-element.11), channel_id=1, source_target_pairs={{0,7},{1,0},{2,1},{3,2},{4,3},{5,4},{6,5},{7,6},{8,15},{9,8},{10,9... | collective-permute-start | bytes 786440 | tf_op jit(solution)/shard_map/ppermute | solution.py:212
  24.4 4.3 %collective-permute-done.before_ref = bf16[4,64,512]{2,1,0:T(8,128)(2,1)S(1)} collective-permute-done((bf16[4,64,512]{2,1,0:T(8,128)(2,1)S(1)}, bf16[4,64,512]{2,1,0:T(8,128)(2,1)S(1)}, u32[]{:S(2)}, u32[]{:S(2)}) %collective-permute-start) | collective-permute-done | bytes 262176 | tf_op jit(solution)/shard_map/ppermute | solution.py:211
  28.7 0.9 %collective-permute-done.1.after_ref = bf16[4,64,512]{2,1,0:T(8,128)(2,1)S(1)} collective-permute-done((bf16[4,64,512]{2,1,0:T(8,128)(2,1)S(1)}, bf16[4,64,512]{2,1,0:T(8,128)(2,1)S(1)}, u32[]{:S(2)}, u32[]{:S(2)}) %collective-permute-start.1) | collective-permute-done | bytes 262176 | tf_op jit(solution)/shard_map/ppermute | solution.py:212
  29.6 5.8 %all-to-all-done.received_ref = bf16[64,2,2176]{2,1,0:T(2,128)(2,1)S(1)} async-done(((bf16[64,2,2176]{2,1,0:T(2,128)(2,1)}), bf16[64,2,2176]{2,1,0:T(2,128)(2,1)S(1)}, u32[]{:S(2)}, u32[]{:S(2)}) %all-to-all-start) | async-done | bytes 557088 | tf_op jit(solution)/shard_map/all_to_all | solution.py:206
  35.3 1.2 %shard_map.57 = (bf16[8,64,128]{2,1,0:T(8,128)(2,1)}, bf16[256,128]{1,0:T(8,128)(2,1)S(1)}) custom-call(bf16[64,2,2176]{2,1,0:T(2,128)(2,1)S(1)} %all-to-all-done.received_ref, bf16[4,64,512]{2,1,0:T(8,128)(2,1)S(1)} %collective-permute-done.before_ref, bf16[4,64,1024]{2,1,0:T(8,128)(2,1)S(1)} %bitcast.9, ...), custom_call_target="tpu_custom_call" | custom-call | bytes 1605632 | tf_op jit(solution)/shard_map/pallas_call | solution.py:174
  36.5 6.8 %all-to-all-start.1 = ((bf16[8,64,128]{2,1,0:T(8,128)(2,1)}), bf16[8,64,128]{2,1,0:T(8,128)(2,1)S(1)}, u32[]{:S(2)}, u32[]{:S(2)}) async-start(bf16[8,64,128]{2,1,0:T(8,128)(2,1)} %get-tuple-element.9), calls=%async_computation.1 | async-start | bytes 262144 | tf_op jit(solution)/shard_map/all_to_all | solution.py:223
  43.4 0.0 copy-done.2
  43.4 0.3 shard_map.55.place_ref
  43.7 7.6 %all-to-all-done.1.partial_ref = bf16[8,64,128]{2,1,0:T(8,128)(2,1)S(1)} async-done(((bf16[8,64,128]{2,1,0:T(8,128)(2,1)}), bf16[8,64,128]{2,1,0:T(8,128)(2,1)S(1)}, u32[]{:S(2)}, u32[]{:S(2)}) %all-to-all-start.1) | async-done | bytes 131104 | tf_op jit(solution)/shard_map/all_to_all | solution.py:223
  51.2 0.0 copy-done.1
  51.2 0.9 %shard_map.58 = f32[256,128]{1,0:T(8,128)} custom-call(bf16[8,64,128]{2,1,0:T(8,128)(2,1)S(1)} %all-to-all-done.1.partial_ref, bf16[256,128]{1,0:T(8,128)(2,1)S(1)} %get-tuple-element.10.label_ref, bf16[256,128]{1,0:T(8,128)(2,1)S(1)} %bitcast.11), custom_call_target="tpu_custom_call" | custom-call | bytes 262144 | tf_op jit(solution)/shard_map/pallas_call | solution.py:174
  52.1 7.8 %all-to-all-start.2 = ((f32[64,4,128]{2,1,0:T(4,128)}), f32[64,4,128]{2,1,0:T(4,128)S(1)}, u32[]{:S(2)}, u32[]{:S(2)}) async-start(f32[64,4,128]{2,1,0:T(4,128)} %bitcast.2), calls=%async_computation.2 | async-start | bytes 262144 | tf_op jit(solution)/shard_map/all_to_all | solution.py:229
  59.9 2.9 %fusion.1.base_ref = f32[128,128]{1,0:T(8,128)S(1)} fusion(bf16[128,8192]{1,0:T(8,128)(2,1)} %bitcast.12, bf16[8192,128]{1,0:T(8,128)(2,1)} %param.6), kind=kOutput, calls=%fused_computation.1 | convolution fusion | flops 268435456 | bytes 4259840 | tf_op jit(solution)/shard_map/dot_general | solution.py:214
  62.8 7.4 %all-to-all-done.2 = f32[64,4,128]{2,1,0:T(4,128)S(1)} async-done(((f32[64,4,128]{2,1,0:T(4,128)}), f32[64,4,128]{2,1,0:T(4,128)S(1)}, u32[]{:S(2)}, u32[]{:S(2)}) %all-to-all-start.2) | async-done | bytes 131104 | tf_op jit(solution)/shard_map/all_to_all | solution.py:229
  70.2 0.8 %shard_map.59 = bf16[128,128]{1,0:T(8,128)(2,1)} custom-call(bf16[128,256]{1,0:T(8,128)(2,1)S(1)} %shard_map.55.place_ref, f32[256,128]{1,0:T(8,128)S(1)} %bitcast.10, f32[128,128]{1,0:T(8,128)S(1)} %fusion.1.base_ref), custom_call_target="tpu_custom_call" | custom-call | bytes 262144 | tf_op jit(solution)/shard_map/pallas_call | solution.py:174
  (1 shorter events, 0.0 us)
Async XLA Ops:
  0.0 17.3 %copy-start = (bf16[4,1024,64]{1,2,0:T(8,128)(2,1)S(1)}, bf16[4,1024,64]{1,2,0:T(8,128)(2,1)}, u32[]{:S(2)}) copy-start(bf16[4,1024,64]{1,2,0:T(8,128)(2,1)} %param.7) | copy-start | bytes 1572868
  2.3 41.1 %copy-start.2 = (s32[2,64]{1,0:T(2,128)S(1)}, s32[2,64]{1,0:T(2,128)}, u32[]{:S(2)}) copy-start(s32[2,64]{1,0:T(2,128)} %index_ref.3) | copy-start | bytes 1540
  2.3 48.9 %copy-start.1 = (bf16[4,64,128]{2,1,0:T(8,128)(2,1)S(1)}, bf16[4,64,128]{2,1,0:T(8,128)(2,1)}, u32[]{:S(2)}) copy-start(bf16[4,64,128]{2,1,0:T(8,128)(2,1)} %param.8) | copy-start | bytes 196612
  2.3 33.0 %all-to-all-start = ((bf16[64,2,2176]{2,1,0:T(2,128)(2,1)}), bf16[64,2,2176]{2,1,0:T(2,128)(2,1)S(1)}, u32[]{:S(2)}, u32[]{:S(2)}) async-start(bf16[64,2,2176]{2,1,0:T(2,128)(2,1)} %shard_map.56), calls=%async_computation | async-start | bytes 1114112 | tf_op jit(solution)/shard_map/all_to_all | solution.py:206
  17.3 11.4 %collective-permute-start = (bf16[4,64,512]{2,1,0:T(8,128)(2,1)S(1)}, bf16[4,64,512]{2,1,0:T(8,128)(2,1)S(1)}, u32[]{:S(2)}, u32[]{:S(2)}) collective-permute-start(bf16[4,64,512]{2,1,0:T(8,128)(2,1)S(1)} %get-tuple-element.12), channel_id=1, source_target_pairs={{0,1},{1,2},{2,3},{3,4},{4,5},{5,6},{6,7},{7,0},{8,9},{9,10},{10,1... | collective-permute-start | bytes 786440 | tf_op jit(solution)/shard_map/ppermute | solution.py:211
  20.5 9.0 %collective-permute-start.1 = (bf16[4,64,512]{2,1,0:T(8,128)(2,1)S(1)}, bf16[4,64,512]{2,1,0:T(8,128)(2,1)S(1)}, u32[]{:S(2)}, u32[]{:S(2)}) collective-permute-start(bf16[4,64,512]{2,1,0:T(8,128)(2,1)S(1)} %get-tuple-element.11), channel_id=1, source_target_pairs={{0,7},{1,0},{2,1},{3,2},{4,3},{5,4},{6,5},{7,6},{8,15},{9,8},{10,9... | collective-permute-start | bytes 786440 | tf_op jit(solution)/shard_map/ppermute | solution.py:212
  36.5 14.7 %all-to-all-start.1 = ((bf16[8,64,128]{2,1,0:T(8,128)(2,1)}), bf16[8,64,128]{2,1,0:T(8,128)(2,1)S(1)}, u32[]{:S(2)}, u32[]{:S(2)}) async-start(bf16[8,64,128]{2,1,0:T(8,128)(2,1)} %get-tuple-element.9), calls=%async_computation.1 | async-start | bytes 262144 | tf_op jit(solution)/shard_map/all_to_all | solution.py:223
  52.1 18.1 %all-to-all-start.2 = ((f32[64,4,128]{2,1,0:T(4,128)}), f32[64,4,128]{2,1,0:T(4,128)S(1)}, u32[]{:S(2)}, u32[]{:S(2)}) async-start(f32[64,4,128]{2,1,0:T(4,128)} %bitcast.2), calls=%async_computation.2 | async-start | bytes 262144 | tf_op jit(solution)/shard_map/all_to_all | solution.py:229

commit v6 on v5

--- a/solution.py
+++ b/solution.py
@@ -29,22 +29,9 @@
     return wide, place, ((along & (owned - 1)) + 1).astype(F32)
 
 
-def spread(first, second):
-    first, second = (v.reshape(v.shape[0] // 8, 8, 128) for v in (first, second))
-    pair = iota(first.shape, 1) // 2
-
-    def turn(total, by):
-        return pltpu.roll(total, by, 1)
-
-    def pick(*pieces):
-        out = pieces[0]
-        for d in range(1, 4):
-            out = jnp.where(pair == d, pieces[d], out)
-        return out
-
-    even = pick(first, turn(second, 2), turn(first, 2), turn(second, 4))
-    odd = pick(turn(first, 4), turn(second, 6), turn(first, 6), second)
-    return jnp.stack([even, odd], axis=1).reshape(first.shape[0] * 16, 128)
+def over_lanes(values):
+    share = jnp.full((128, 128), 1.0 / 32.0, BF16)
+    return jnp.dot(values.astype(BF16), share, preferred_element_type=F32)
 
 
 def pack_kernel(owned, planes, index_ref, tokens_ref, out_ref, held, indices, sems):
@@ -74,11 +61,14 @@
     line, column = iota((rows, rows), 0), iota((rows, rows), 1)
     hit = line == wide
     label = jnp.broadcast_to(label, (rows, rows))
-    labels = [
-        jnp.sum(jnp.where(hit & (place == p), label, 0.0), axis=1, keepdims=True)
-        for p in (0.0, 1.0)
-    ]
-    labels = jnp.where(column < 64, labels[0], labels[1]).astype(BF16)
+    labels = None
+    for field in range(4):
+        core, p = field // 2, float(field % 2)
+        chip_hit = wide == (line & -4) + 2 * core + (line & 1)
+        found = jnp.where(chip_hit & (place == p), label, 0.0)
+        found = jnp.sum(found, axis=1, keepdims=True)
+        labels = found if field == 0 else jnp.where(column // 32 == field, found, labels)
+    labels = jnp.broadcast_to(labels, (rows, 128)).astype(BF16)
     out_ref[:, :, 2 * width :] = labels.reshape(rows // 2, 2, 128)
     select = jnp.where(hit & (place == parity.astype(F32)), 1.0, 0.0).astype(BF16)
     for copy in copies[1:]:
@@ -88,11 +78,12 @@
     out_ref[:, :, : 2 * width] = packed.reshape(rows // 2, 2, 2 * width)
 
 
-def shrink_kernel(received_ref, before_ref, own_ref, after_ref, partial_ref, label_ref):
+def shrink_kernel(received_ref, before_ref, own_ref, after_ref, partial_ref):
     shards, groups, width = received_ref.shape
     width = (width - 128) // 2
     lines = shards * groups
     parity = lax.axis_index("tensor") % 2
+    core = lax.axis_index("dp") % 2
     product, at = None, 0
     for weight_ref in (before_ref, own_ref, after_ref):
         size = weight_ref.shape[2]
@@ -105,42 +96,84 @@
         )
         product = mine if at == 0 else product + mine
         at += size
-    label = received_ref[:, :, 2 * width :].reshape(lines, 128).astype(F32)
-    turned = pltpu.roll(label, 64, 1)
-    upper = iota((lines, 128), 1) // 64
-    here = jnp.where(upper == parity, label, turned)
-    total = jnp.where(here == upper.astype(F32) + 1.0, product[:, :128], 0.0)
-    total = total + jnp.where(here == upper.astype(F32) + 3.0, product[:, 128:], 0.0)
+    label = received_ref[:, :, 2 * width :].reshape(lines, 128)
+    field = iota((lines, 128), 1) // 32
+    here = over_lanes(jnp.where(field == core * 2 + parity, label.astype(F32), 0.0))
+    upper = (iota((lines, 128), 1) // 64).astype(F32)
+    total = jnp.where(here == upper + 1.0, product[:, :128], 0.0)
+    total = total + jnp.where(here == upper + 3.0, product[:, 128:], 0.0)
     total = total + pltpu.roll(total, 64, 1)
     half = lines // 2
-    packed = jnp.where(upper[:half] == 0, total[:half], total[half:]).astype(BF16)
-    for peer in range(partial_ref.shape[0]):
-        partial_ref[peer] = packed
-    low = jnp.where(upper == 0, label, turned)
-    high = jnp.where(upper == 0, turned, label)
-    label_ref[...] = spread(low, high).astype(BF16)
-
-
-def expand_kernel(partial_ref, label_ref, up_ref, out_ref):
+    packed = jnp.where(upper[:half] == 0.0, total[:half], total[half:])
+    chips = packed.reshape(half // 8, 8, 128)
+    for c in range(2):
+        by_pair = chips.reshape(half // 16, 2, 8, 128)
+        left, right = by_pair[:, 0], by_pair[:, 1]
+        place = iota(left.shape, 1) // 2
+        turn = pltpu.roll
+        if c == 0:
+            pieces = [left, turn(left, 6, 1), turn(right, 4, 1), turn(right, 2, 1)]
+        else:
+            pieces = [turn(left, 6, 1), turn(left, 4, 1), turn(right, 2, 1), right]
+        out = pieces[0]
+        for d in range(1, 4):
+            out = jnp.where(place == d, pieces[d], out)
+        out = out.reshape(half // 2, 128).astype(BF16)
+        planes = partial_ref.shape[0] // 2
+        for peer in range(planes):
+            partial_ref[c * planes + peer] = out
+
+
+def label_kernel(received_ref, out_ref):
+    shards, groups, width = received_ref.shape
+    label = received_ref[:, :, width - 128 :].reshape(shards * groups, 128)
+    core = lax.axis_index("dp") % 2
+    lines = out_ref.shape[0]
+    line = iota((lines, shards * groups), 0)
+    source = (line // 8 * 2 + core) * 2 + line % 2
+    take = jnp.where(iota((lines, shards * groups), 1) == source, 1.0, 0.0).astype(BF16)
+    label = jnp.dot(take, label, preferred_element_type=F32)
+    line = iota((lines, 128), 0)
+    label = over_lanes(jnp.where(iota((lines, 128), 1) // 32 == line // 2 % 4, label, 0.0))
+    other = (label > 0.0) & (line // 4 % 2 != core)
+    out_ref[...] = jnp.where(other, label + 4.0, label).astype(BF16)
+
+
+def expand_kernel(partial_ref, label_ref, up_own_ref, up_other_ref, out_ref):
+    planes, half, _ = partial_ref.shape
+    planes //= 2
     sums = []
-    for p in range(2):
-        total = partial_ref[p].astype(F32)
-        for peer in range(p + 2, partial_ref.shape[0], 2):
-            total = total + partial_ref[peer].astype(F32)
-        sums.append(total)
-    total = spread(*sums)
+    for core in range(2):
+        for p in range(2):
+            total = partial_ref[core * planes + p].astype(F32)
+            for peer in range(p + 2, planes, 2):
+                total = total + partial_ref[core * planes + peer].astype(F32)
+            sums.append(total.reshape(half // 8, 8, 128))
+    place = iota(sums[0].shape, 1) // 2
+    by_chip = []
+    for chip in range(4):
+        out = None
+        for field in range(4):
+            by = 2 * (field - chip) % 8
+            piece = pltpu.roll(sums[field], by, 1) if by else sums[field]
+            out = piece if field == 0 else jnp.where(place == field, piece, out)
+        by_chip.append(out)
+    total = jnp.stack(by_chip, axis=1).reshape(half * 4, 128)
     turned = pltpu.roll(total, 64, 1)
     upper = iota(total.shape, 1) // 64
     lines = total.shape[0]
     for e in range(2):
         row = jnp.where(upper == e, total, turned)
         label = label_ref[e * lines : (e + 1) * lines].astype(F32)
-        left = jnp.where(label == upper.astype(F32) + 1.0, row, 0.0)
-        right = jnp.where(label == upper.astype(F32) + 3.0, row, 0.0)
-        wide = jnp.concatenate([left, right], axis=1).astype(BF16)
-        out_ref[e * lines : (e + 1) * lines] = jnp.dot(
-            wide, up_ref[...], preferred_element_type=F32
-        )
+        terms = None
+        for up_ref, add in ((up_own_ref, 1.0), (up_other_ref, 5.0)):
+            first = upper.astype(F32) + add
+            left = jnp.where(label == first, row, 0.0)
+            right = jnp.where(label == first + 2.0, row, 0.0)
+            wide = jnp.concatenate([left, right], axis=1).astype(BF16)
+            mine = jnp.dot(wide, up_ref[...], preferred_element_type=F32)
+            terms = mine if terms is None else terms + mine
+        out_ref[e * lines : (e + 1) * lines] = terms
 
 
 def place_kernel(owned, index_ref, out_ref):
@@ -205,29 +238,39 @@
     )
     received = lax.all_to_all(packed, "dp", split_axis=0, concat_axis=0, tiled=True)
 
-    down_own = down.transpose(0, 2, 1)
-    later, _ = lax.optimization_barrier((down_own, packed))
+    down_own, up_own = down.transpose(0, 2, 1), up.reshape(owned * rank, columns)
+    later, up_later, _ = lax.optimization_barrier((down_own, up_own, packed))
     upper, lower = later[:, :, width // 2 :], later[:, :, : width // 2]
     before = lax.ppermute(upper, "tensor", [(i, (i + 1) % planes) for i in range(planes)])
     after = lax.ppermute(lower, "tensor", [(i, (i - 1) % planes) for i in range(planes)])
+    up_other = lax.ppermute(up_later, "dp", [(i, i ^ 1) for i in range(owners)])
 
     base = jnp.dot(tokens.reshape(rows, features), value_matrix, preferred_element_type=F32)
     (place,) = call(
         functools.partial(place_kernel, owned), [shape((rows, owners * 4), BF16)], (index,)
     )
-    partial, label = call(
+    (partial,) = call(
         shrink_kernel,
-        [shape((planes, owners, 128), BF16), shape((owners * 4, 128), BF16)],
+        [shape((2 * planes, owners // 2, 128), BF16)],
         (received, before, down_own, after),
     )
-    partials = lax.all_to_all(partial, "tensor", split_axis=0, concat_axis=0, tiled=True)
+    chips = [list(range(i, i + 2 * planes)) for i in range(0, owners * planes, 2 * planes)]
+    partials = lax.all_to_all(
+        partial, ("dp", "tensor"), split_axis=0, concat_axis=0, tiled=True, axis_index_groups=chips
+    )
+    (label,) = call(label_kernel, [shape((owners * 4, 128), BF16)], (received,))
     (terms,) = call(
         expand_kernel,
         [shape((owners * 4, columns), F32)],
-        (partials, label, up.reshape(owned * rank, columns)),
+        (partials, label, up_own, up_other),
     )
     arrived = lax.all_to_all(
-        terms.reshape(owners, 4, columns), "dp", split_axis=0, concat_axis=0, tiled=True
+        terms.reshape(owners // 2, 8, columns),
+        "dp",
+        split_axis=0,
+        concat_axis=0,
+        tiled=True,
+        axis_index_groups=[list(range(core, owners, 2)) for core in range(2)],
     ).reshape(owners * 4, columns)
     (out,) = call(add_kernel, [shape((rows, columns), BF16)], (place, arrived, base))
     return out.reshape(groups, rows_local, columns)

time: 71.5 us -> 69.5 us (0.972)
  the two profiles are of different devices: /device:TPU:1 before, /device:TPU:8 now
where the time goes in v6:
time: 69.5 us; the launch traced here: 69.1 us
  starting transfers between devices  35.1 us (51%)
  waiting for transfers between devices  25.1 us (36%)
  Pallas kernels  5.8 us (8%)
  matrix products  2.92 us (4%)
    all_to_all x1, starting transfers between devices, on_device(): lax.all_to_all(packed, 'dp', split_axis=0, concat_axis=0, tiled=True)  13.9 us
    all_to_all x1, starting transfers between devices, on_device(): lax.all_to_all(partial, ('dp', 'tensor'), split_axis=0, concat_axis=0, ti...  7.56 us
    all_to_all x1, waiting for transfers between devices, on_device(): lax.all_to_all(terms.reshape(owners // 2, 8, columns), 'dp', split_axis=0...  7.48 us
    pallas_call x6, Pallas kernels, call(): pl.pallas_call(kernel, out_shape=shapes, in_specs=[spec(i in in_hbm) for...  5.8 us
    all_to_all x1, starting transfers between devices, on_device(): lax.all_to_all(terms.reshape(owners // 2, 8, columns), 'dp', split_axis=0...  5.69 us
    all_to_all x1, waiting for transfers between devices, on_device(): lax.all_to_all(partial, ('dp', 'tensor'), split_axis=0, concat_axis=0, ti...  5.06 us
    all_to_all x1, waiting for transfers between devices, on_device(): lax.all_to_all(packed, 'dp', split_axis=0, concat_axis=0, tiled=True)  4.57 us
    ppermute x1, waiting for transfers between devices, on_device(): lax.ppermute(upper, 'tensor', [(i, (i + 1) % planes) for i in range(plane...  4.3 us
  transfers between devices with their start and end apart: 6, of which 6 were waited for; matrix products, arithmetic and copies ran while one was open for 4% of the time, Pallas kernels for 1%

profile of v6, /device:TPU:8, one launch (start us, length us, event | category | flops | bytes accessed | tf_op | source)
XLA Modules:
  0.0 69.1 jit_solution(3838924374754541627)
XLA Ops:
  0.0 0.0 copy-start
  0.0 2.3 %shard_map.56 = bf16[64,2,2176]{2,1,0:T(2,128)(2,1)} custom-call(s32[2,64]{1,0:T(2,128)} %index_ref.3, bf16[2,64,8192]{2,1,0:T(8,128)(2,1)} %tokens_ref.1), custom_call_target="tpu_custom_call" | custom-call | bytes 2097664 | tf_op jit(solution)/shard_map/pallas_call | solution.py:207
  2.3 0.0 copy-start.1
  2.3 0.0 copy-start.2
  2.3 13.9 %all-to-all-start = ((bf16[64,2,2176]{2,1,0:T(2,128)(2,1)}), bf16[64,2,2176]{2,1,0:T(2,128)(2,1)S(1)}, u32[]{:S(2)}, u32[]{:S(2)}) async-start(bf16[64,2,2176]{2,1,0:T(2,128)(2,1)} %shard_map.56), calls=%async_computation | async-start | bytes 1114112 | tf_op jit(solution)/shard_map/all_to_all | solution.py:239
  16.2 0.0 copy-done
  16.3 3.5 %collective-permute-start = (bf16[4,64,512]{2,1,0:T(8,128)(2,1)S(1)}, bf16[4,64,512]{2,1,0:T(8,128)(2,1)S(1)}, u32[]{:S(2)}, u32[]{:S(2)}) collective-permute-start(bf16[4,64,512]{2,1,0:T(8,128)(2,1)S(1)} %get-tuple-element.10), channel_id=1, source_target_pairs={{0,1},{1,2},{2,3},{3,4},{4,5},{5,6},{6,7},{7,0},{8,9},{9,10},{10,1... | collective-permute-start | bytes 786440 | tf_op jit(solution)/shard_map/ppermute | solution.py:244
  19.8 2.4 %collective-permute-start.1 = (bf16[4,64,512]{2,1,0:T(8,128)(2,1)S(1)}, bf16[4,64,512]{2,1,0:T(8,128)(2,1)S(1)}, u32[]{:S(2)}, u32[]{:S(2)}) collective-permute-start(bf16[4,64,512]{2,1,0:T(8,128)(2,1)S(1)} %get-tuple-element.9), channel_id=1, source_target_pairs={{0,7},{1,0},{2,1},{3,2},{4,3},{5,4},{6,5},{7,6},{8,15},{9,8},{10,9... | collective-permute-start | bytes 786440 | tf_op jit(solution)/shard_map/ppermute | solution.py:245
  22.1 4.3 %collective-permute-done.before_ref = bf16[4,64,512]{2,1,0:T(8,128)(2,1)S(1)} collective-permute-done((bf16[4,64,512]{2,1,0:T(8,128)(2,1)S(1)}, bf16[4,64,512]{2,1,0:T(8,128)(2,1)S(1)}, u32[]{:S(2)}, u32[]{:S(2)}) %collective-permute-start) | collective-permute-done | bytes 262176 | tf_op jit(solution)/shard_map/ppermute | solution.py:244
  26.4 3.2 %collective-permute-done.1.after_ref = bf16[4,64,512]{2,1,0:T(8,128)(2,1)S(1)} collective-permute-done((bf16[4,64,512]{2,1,0:T(8,128)(2,1)S(1)}, bf16[4,64,512]{2,1,0:T(8,128)(2,1)S(1)}, u32[]{:S(2)}, u32[]{:S(2)}) %collective-permute-start.1) | collective-permute-done | bytes 262176 | tf_op jit(solution)/shard_map/ppermute | solution.py:245
  29.7 4.6 %all-to-all-done.received_ref = bf16[64,2,2176]{2,1,0:T(2,128)(2,1)S(1)} async-done(((bf16[64,2,2176]{2,1,0:T(2,128)(2,1)}), bf16[64,2,2176]{2,1,0:T(2,128)(2,1)S(1)}, u32[]{:S(2)}, u32[]{:S(2)}) %all-to-all-start) | async-done | bytes 557088 | tf_op jit(solution)/shard_map/all_to_all | solution.py:239
  34.2 1.2 %shard_map.57 = bf16[16,32,128]{2,1,0:T(8,128)(2,1)} custom-call(bf16[64,2,2176]{2,1,0:T(2,128)(2,1)S(1)} %all-to-all-done.received_ref, bf16[4,64,512]{2,1,0:T(8,128)(2,1)S(1)} %collective-permute-done.before_ref, bf16[4,64,1024]{2,1,0:T(8,128)(2,1)S(1)} %bitcast.9, bf16[4,64,512]{2,1,0:T(8,128)(2,1)S(1)} %collective-permute-done.1.after_ref), custom_call_target="tpu_custom_call" | custom-call | bytes 1605632 | tf_op jit(solution)/shard_map/pallas_call | solution.py:207
  35.5 7.6 %all-to-all-start.1 = ((bf16[16,32,128]{2,1,0:T(8,128)(2,1)}), bf16[16,32,128]{2,1,0:T(8,128)(2,1)S(1)}, u32[]{:S(2)}, u32[]{:S(2)}) async-start(bf16[16,32,128]{2,1,0:T(8,128)(2,1)} %shard_map.57), calls=%async_computation.1 | async-start | bytes 262144 | tf_op jit(solution)/shard_map/all_to_all | solution.py:258
  43.0 0.0 copy-done.1
  43.0 2.1 %collective-permute-start.2 = (bf16[256,128]{1,0:T(8,128)(2,1)S(1)}, bf16[256,128]{1,0:T(8,128)(2,1)S(1)}, u32[]{:S(2)}, u32[]{:S(2)}) collective-permute-start(bf16[256,128]{1,0:T(8,128)(2,1)S(1)} %bitcast.11), channel_id=1, source_target_pairs={{0,8},{8,0},{16,24},{24,16},{32,40},{40,32},{48,56},{56,48},{64,72... | collective-permute-start | bytes 196616 | tf_op jit(solution)/shard_map/ppermute | solution.py:246
  45.1 0.0 copy-done.2
  45.1 0.3 shard_map.55.place_ref
  45.4 0.3 shard_map.58.label_ref
  45.7 0.5 collective-permute-done.2.up_other_ref
  46.2 5.1 %all-to-all-done.1.partial_ref = bf16[16,32,128]{2,1,0:T(8,128)(2,1)S(1)} async-done(((bf16[16,32,128]{2,1,0:T(8,128)(2,1)}), bf16[16,32,128]{2,1,0:T(8,128)(2,1)S(1)}, u32[]{:S(2)}, u32[]{:S(2)}) %all-to-all-start.1) | async-done | bytes 131104 | tf_op jit(solution)/shard_map/all_to_all | solution.py:258
  51.2 0.9 %shard_map.59 = f32[256,128]{1,0:T(8,128)} custom-call(bf16[16,32,128]{2,1,0:T(8,128)(2,1)S(1)} %all-to-all-done.1.partial_ref, bf16[256,128]{1,0:T(8,128)(2,1)S(1)} %shard_map.58.label_ref, bf16[256,128]{1,0:T(8,128)(2,1)S(1)} %bitcast.12, bf16[256,128]{1,0:T(8,128)(2,1)S(1)} %collective-permute-done.2.up_other_ref), custom_call_target="tpu_custom_call" | custom-call | bytes 327680 | tf_op jit(solution)/shard_map/pallas_call | solution.py:207
  52.2 5.7 %all-to-all-start.2 = ((f32[32,8,128]{2,1,0:T(8,128)}), f32[32,8,128]{2,1,0:T(8,128)S(1)}, u32[]{:S(2)}, u32[]{:S(2)}) async-start(f32[32,8,128]{2,1,0:T(8,128)} %bitcast.2), calls=%async_computation.2 | async-start | bytes 262144 | tf_op jit(solution)/shard_map/all_to_all | solution.py:267
  57.9 2.9 %fusion.1.base_ref = f32[128,128]{1,0:T(8,128)S(1)} fusion(bf16[128,8192]{1,0:T(8,128)(2,1)} %bitcast.13, bf16[8192,128]{1,0:T(8,128)(2,1)} %param.6), kind=kOutput, calls=%fused_computation.1 | convolution fusion | flops 268435456 | bytes 4259840 | tf_op jit(solution)/shard_map/dot_general | solution.py:248
  60.8 7.5 %all-to-all-done.2 = f32[32,8,128]{2,1,0:T(8,128)S(1)} async-done(((f32[32,8,128]{2,1,0:T(8,128)}), f32[32,8,128]{2,1,0:T(8,128)S(1)}, u32[]{:S(2)}, u32[]{:S(2)}) %all-to-all-start.2) | async-done | bytes 131104 | tf_op jit(solution)/shard_map/all_to_all | solution.py:267
  68.3 0.8 %shard_map.60 = bf16[128,128]{1,0:T(8,128)(2,1)} custom-call(bf16[128,256]{1,0:T(8,128)(2,1)S(1)} %shard_map.55.place_ref, f32[256,128]{1,0:T(8,128)S(1)} %bitcast.10, f32[128,128]{1,0:T(8,128)S(1)} %fusion.1.base_ref), custom_call_target="tpu_custom_call" | custom-call | bytes 262144 | tf_op jit(solution)/shard_map/pallas_call | solution.py:207
  (1 shorter events, 0.0 us)
Async XLA Ops:
  0.0 16.2 %copy-start = (bf16[4,1024,64]{1,2,0:T(8,128)(2,1)S(1)}, bf16[4,1024,64]{1,2,0:T(8,128)(2,1)}, u32[]{:S(2)}) copy-start(bf16[4,1024,64]{1,2,0:T(8,128)(2,1)} %param.7) | copy-start | bytes 1572868
  2.3 40.8 %copy-start.1 = (bf16[4,64,128]{2,1,0:T(8,128)(2,1)S(1)}, bf16[4,64,128]{2,1,0:T(8,128)(2,1)}, u32[]{:S(2)}) copy-start(bf16[4,64,128]{2,1,0:T(8,128)(2,1)} %param.8) | copy-start | bytes 196612
  2.3 42.8 %copy-start.2 = (s32[2,64]{1,0:T(2,128)S(1)}, s32[2,64]{1,0:T(2,128)}, u32[]{:S(2)}) copy-start(s32[2,64]{1,0:T(2,128)} %index_ref.3) | copy-start | bytes 1540
  2.3 31.9 %all-to-all-start = ((bf16[64,2,2176]{2,1,0:T(2,128)(2,1)}), bf16[64,2,2176]{2,1,0:T(2,128)(2,1)S(1)}, u32[]{:S(2)}, u32[]{:S(2)}) async-start(bf16[64,2,2176]{2,1,0:T(2,128)(2,1)} %shard_map.56), calls=%async_computation | async-start | bytes 1114112 | tf_op jit(solution)/shard_map/all_to_all | solution.py:239
  16.3 10.2 %collective-permute-start = (bf16[4,64,512]{2,1,0:T(8,128)(2,1)S(1)}, bf16[4,64,512]{2,1,0:T(8,128)(2,1)S(1)}, u32[]{:S(2)}, u32[]{:S(2)}) collective-permute-start(bf16[4,64,512]{2,1,0:T(8,128)(2,1)S(1)} %get-tuple-element.10), channel_id=1, source_target_pairs={{0,1},{1,2},{2,3},{3,4},{4,5},{5,6},{6,7},{7,0},{8,9},{9,10},{10,1... | collective-permute-start | bytes 786440 | tf_op jit(solution)/shard_map/ppermute | solution.py:244
  19.8 9.9 %collective-permute-start.1 = (bf16[4,64,512]{2,1,0:T(8,128)(2,1)S(1)}, bf16[4,64,512]{2,1,0:T(8,128)(2,1)S(1)}, u32[]{:S(2)}, u32[]{:S(2)}) collective-permute-start(bf16[4,64,512]{2,1,0:T(8,128)(2,1)S(1)} %get-tuple-element.9), channel_id=1, source_target_pairs={{0,7},{1,0},{2,1},{3,2},{4,3},{5,4},{6,5},{7,6},{8,15},{9,8},{10,9... | collective-permute-start | bytes 786440 | tf_op jit(solution)/shard_map/ppermute | solution.py:245
  35.5 15.8 %all-to-all-start.1 = ((bf16[16,32,128]{2,1,0:T(8,128)(2,1)}), bf16[16,32,128]{2,1,0:T(8,128)(2,1)S(1)}, u32[]{:S(2)}, u32[]{:S(2)}) async-start(bf16[16,32,128]{2,1,0:T(8,128)(2,1)} %shard_map.57), calls=%async_computation.1 | async-start | bytes 262144 | tf_op jit(solution)/shard_map/all_to_all | solution.py:258
  43.0 3.1 %collective-permute-start.2 = (bf16[256,128]{1,0:T(8,128)(2,1)S(1)}, bf16[256,128]{1,0:T(8,128)(2,1)S(1)}, u32[]{:S(2)}, u32[]{:S(2)}) collective-permute-start(bf16[256,128]{1,0:T(8,128)(2,1)S(1)} %bitcast.11), channel_id=1, source_target_pairs={{0,8},{8,0},{16,24},{24,16},{32,40},{40,32},{48,56},{56,48},{64,72... | collective-permute-start | bytes 196616 | tf_op jit(solution)/shard_map/ppermute | solution.py:246
  52.2 16.1 %all-to-all-start.2 = ((f32[32,8,128]{2,1,0:T(8,128)}), f32[32,8,128]{2,1,0:T(8,128)S(1)}, u32[]{:S(2)}, u32[]{:S(2)}) async-start(f32[32,8,128]{2,1,0:T(8,128)} %bitcast.2), calls=%async_computation.2 | async-start | bytes 262144 | tf_op jit(solution)/shard_map/all_to_all | solution.py:267

commit v7 on v6

--- a/solution.py
+++ b/solution.py
@@ -170,10 +170,12 @@
             first = upper.astype(F32) + add
             left = jnp.where(label == first, row, 0.0)
             right = jnp.where(label == first + 2.0, row, 0.0)
-            wide = jnp.concatenate([left, right], axis=1).astype(BF16)
-            mine = jnp.dot(wide, up_ref[...], preferred_element_type=F32)
-            terms = mine if terms is None else terms + mine
-        out_ref[e * lines : (e + 1) * lines] = terms
+            wide = jnp.concatenate([left, right], axis=1)
+            high = wide.astype(BF16)
+            for part in (high, (wide - high.astype(F32)).astype(BF16)):
+                mine = jnp.dot(part, up_ref[...], preferred_element_type=F32)
+                terms = mine if terms is None else terms + mine
+        out_ref[e * lines : (e + 1) * lines] = terms.astype(BF16)
 
 
 def place_kernel(owned, index_ref, out_ref):
@@ -188,13 +190,7 @@
 
 
 def add_kernel(place_ref, arrived_ref, base_ref, out_ref):
-    arrived = arrived_ref[...]
-    high = arrived.astype(BF16)
-    low = (arrived - high.astype(F32)).astype(BF16)
-    place = place_ref[...]
-    terms = jnp.dot(place, high, preferred_element_type=F32) + jnp.dot(
-        place, low, preferred_element_type=F32
-    )
+    terms = jnp.dot(place_ref[...], arrived_ref[...], preferred_element_type=F32)
     out_ref[...] = (base_ref[...] + terms).astype(BF16)
 
 
@@ -261,7 +257,7 @@
     (label,) = call(label_kernel, [shape((owners * 4, 128), BF16)], (received,))
     (terms,) = call(
         expand_kernel,
-        [shape((owners * 4, columns), F32)],
+        [shape((owners * 4, columns), BF16)],
         (partials, label, up_own, up_other),
     )
     arrived = lax.all_to_all(

time: 69.5 us -> 69.2 us (level)
    all_to_all x1, waiting for transfers between devices: 7.48 us -> 6.77 us  [on_device(): lax.all_to_all(terms.reshape(owners // 2, 8, columns), 'dp', split_axis=0...]
where the time goes in v7:
time: 69.2 us; the launch traced here: 68.7 us
  starting transfers between devices  35.1 us (51%)
  waiting for transfers between devices  24.7 us (36%)
  Pallas kernels  5.86 us (8%)
  matrix products  2.92 us (4%)
    all_to_all x1, starting transfers between devices, on_device(): lax.all_to_all(packed, 'dp', split_axis=0, concat_axis=0, tiled=True)  13.9 us
    all_to_all x1, starting transfers between devices, on_device(): lax.all_to_all(partial, ('dp', 'tensor'), split_axis=0, concat_axis=0, ti...  7.56 us
    all_to_all x1, waiting for transfers between devices, on_device(): lax.all_to_all(terms.reshape(owners // 2, 8, columns), 'dp', split_axis=0...  6.77 us
    pallas_call x6, Pallas kernels, call(): pl.pallas_call(kernel, out_shape=shapes, in_specs=[spec(i in in_hbm) for...  5.86 us
    all_to_all x1, starting transfers between devices, on_device(): lax.all_to_all(terms.reshape(owners // 2, 8, columns), 'dp', split_axis=0...  5.69 us
    all_to_all x1, waiting for transfers between devices, on_device(): lax.all_to_all(partial, ('dp', 'tensor'), split_axis=0, concat_axis=0, ti...  5.06 us
    all_to_all x1, waiting for transfers between devices, on_device(): lax.all_to_all(packed, 'dp', split_axis=0, concat_axis=0, tiled=True)  4.57 us
    ppermute x1, waiting for transfers between devices, on_device(): lax.ppermute(upper, 'tensor', [(i, (i + 1) % planes) for i in range(plane...  4.3 us
  transfers between devices with their start and end apart: 6, of which 6 were waited for; matrix products, arithmetic and copies ran while one was open for 4% of the time, Pallas kernels for 1%

profile of v7, /device:TPU:8, one launch (start us, length us, event | category | flops | bytes accessed | tf_op | source)
XLA Modules:
  0.0 68.7 jit_solution(333287280879003044)
XLA Ops:
  0.0 0.0 copy-start
  0.0 2.3 %shard_map.56 = bf16[64,2,2176]{2,1,0:T(2,128)(2,1)} custom-call(s32[2,64]{1,0:T(2,128)} %index_ref.3, bf16[2,64,8192]{2,1,0:T(8,128)(2,1)} %tokens_ref.1), custom_call_target="tpu_custom_call" | custom-call | bytes 2097664 | tf_op jit(solution)/shard_map/pallas_call | solution.py:203
  2.3 0.0 copy-start.1
  2.3 13.9 %all-to-all-start = ((bf16[64,2,2176]{2,1,0:T(2,128)(2,1)}), bf16[64,2,2176]{2,1,0:T(2,128)(2,1)S(1)}, u32[]{:S(2)}, u32[]{:S(2)}) async-start(bf16[64,2,2176]{2,1,0:T(2,128)(2,1)} %shard_map.56), calls=%async_computation | async-start | bytes 1114112 | tf_op jit(solution)/shard_map/all_to_all | solution.py:235
  16.2 0.0 copy-done
  16.3 3.5 %collective-permute-start = (bf16[4,64,512]{2,1,0:T(8,128)(2,1)S(1)}, bf16[4,64,512]{2,1,0:T(8,128)(2,1)S(1)}, u32[]{:S(2)}, u32[]{:S(2)}) collective-permute-start(bf16[4,64,512]{2,1,0:T(8,128)(2,1)S(1)} %get-tuple-element.10), channel_id=1, source_target_pairs={{0,1},{1,2},{2,3},{3,4},{4,5},{5,6},{6,7},{7,0},{8,9},{9,10},{10,1... | collective-permute-start | bytes 786440 | tf_op jit(solution)/shard_map/ppermute | solution.py:240
  19.8 2.4 %collective-permute-start.1 = (bf16[4,64,512]{2,1,0:T(8,128)(2,1)S(1)}, bf16[4,64,512]{2,1,0:T(8,128)(2,1)S(1)}, u32[]{:S(2)}, u32[]{:S(2)}) collective-permute-start(bf16[4,64,512]{2,1,0:T(8,128)(2,1)S(1)} %get-tuple-element.9), channel_id=1, source_target_pairs={{0,7},{1,0},{2,1},{3,2},{4,3},{5,4},{6,5},{7,6},{8,15},{9,8},{10,9... | collective-permute-start | bytes 786440 | tf_op jit(solution)/shard_map/ppermute | solution.py:241
  22.1 4.3 %collective-permute-done.before_ref = bf16[4,64,512]{2,1,0:T(8,128)(2,1)S(1)} collective-permute-done((bf16[4,64,512]{2,1,0:T(8,128)(2,1)S(1)}, bf16[4,64,512]{2,1,0:T(8,128)(2,1)S(1)}, u32[]{:S(2)}, u32[]{:S(2)}) %collective-permute-start) | collective-permute-done | bytes 262176 | tf_op jit(solution)/shard_map/ppermute | solution.py:240
  26.4 3.2 %collective-permute-done.1.after_ref = bf16[4,64,512]{2,1,0:T(8,128)(2,1)S(1)} collective-permute-done((bf16[4,64,512]{2,1,0:T(8,128)(2,1)S(1)}, bf16[4,64,512]{2,1,0:T(8,128)(2,1)S(1)}, u32[]{:S(2)}, u32[]{:S(2)}) %collective-permute-start.1) | collective-permute-done | bytes 262176 | tf_op jit(solution)/shard_map/ppermute | solution.py:241
  29.6 4.6 %all-to-all-done.received_ref = bf16[64,2,2176]{2,1,0:T(2,128)(2,1)S(1)} async-done(((bf16[64,2,2176]{2,1,0:T(2,128)(2,1)}), bf16[64,2,2176]{2,1,0:T(2,128)(2,1)S(1)}, u32[]{:S(2)}, u32[]{:S(2)}) %all-to-all-start) | async-done | bytes 557088 | tf_op jit(solution)/shard_map/all_to_all | solution.py:235
  34.2 1.2 %shard_map.57 = bf16[16,32,128]{2,1,0:T(8,128)(2,1)} custom-call(bf16[64,2,2176]{2,1,0:T(2,128)(2,1)S(1)} %all-to-all-done.received_ref, bf16[4,64,512]{2,1,0:T(8,128)(2,1)S(1)} %collective-permute-done.before_ref, bf16[4,64,1024]{2,1,0:T(8,128)(2,1)S(1)} %bitcast.9, bf16[4,64,512]{2,1,0:T(8,128)(2,1)S(1)} %collective-permute-done.1.after_ref), custom_call_target="tpu_custom_call" | custom-call | bytes 1605632 | tf_op jit(solution)/shard_map/pallas_call | solution.py:203
  35.4 7.6 %all-to-all-start.1 = ((bf16[16,32,128]{2,1,0:T(8,128)(2,1)}), bf16[16,32,128]{2,1,0:T(8,128)(2,1)S(1)}, u32[]{:S(2)}, u32[]{:S(2)}) async-start(bf16[16,32,128]{2,1,0:T(8,128)(2,1)} %shard_map.57), calls=%async_computation.1 | async-start | bytes 262144 | tf_op jit(solution)/shard_map/all_to_all | solution.py:254
  43.0 0.0 copy-done.1
  43.0 2.1 %collective-permute-start.2 = (bf16[256,128]{1,0:T(8,128)(2,1)S(1)}, bf16[256,128]{1,0:T(8,128)(2,1)S(1)}, u32[]{:S(2)}, u32[]{:S(2)}) collective-permute-start(bf16[256,128]{1,0:T(8,128)(2,1)S(1)} %bitcast.11), channel_id=1, source_target_pairs={{0,8},{8,0},{16,24},{24,16},{32,40},{40,32},{48,56},{56,48},{64,72... | collective-permute-start | bytes 196616 | tf_op jit(solution)/shard_map/ppermute | solution.py:242
  45.1 0.3 shard_map.58.label_ref
  45.4 0.8 %collective-permute-done.2.up_other_ref = bf16[256,128]{1,0:T(8,128)(2,1)S(1)} collective-permute-done((bf16[256,128]{1,0:T(8,128)(2,1)S(1)}, bf16[256,128]{1,0:T(8,128)(2,1)S(1)}, u32[]{:S(2)}, u32[]{:S(2)}) %collective-permute-start.2) | collective-permute-done | bytes 65568 | tf_op jit(solution)/shard_map/ppermute | solution.py:242
  46.2 5.1 %all-to-all-done.1.partial_ref = bf16[16,32,128]{2,1,0:T(8,128)(2,1)S(1)} async-done(((bf16[16,32,128]{2,1,0:T(8,128)(2,1)}), bf16[16,32,128]{2,1,0:T(8,128)(2,1)S(1)}, u32[]{:S(2)}, u32[]{:S(2)}) %all-to-all-start.1) | async-done | bytes 131104 | tf_op jit(solution)/shard_map/all_to_all | solution.py:254
  51.2 1.0 %shard_map.59 = bf16[256,128]{1,0:T(8,128)(2,1)} custom-call(bf16[16,32,128]{2,1,0:T(8,128)(2,1)S(1)} %all-to-all-done.1.partial_ref, bf16[256,128]{1,0:T(8,128)(2,1)S(1)} %shard_map.58.label_ref, bf16[256,128]{1,0:T(8,128)(2,1)S(1)} %bitcast.12, bf16[256,128]{1,0:T(8,128)(2,1)S(1)} %collective-permute-done.2.up_other_ref), custom_call_target="tpu_custom_call" | custom-call | bytes 327680 | tf_op jit(solution)/shard_map/pallas_call | solution.py:203
  52.3 5.7 %all-to-all-start.2 = ((bf16[32,8,128]{2,1,0:T(8,128)(2,1)}), bf16[32,8,128]{2,1,0:T(8,128)(2,1)S(1)}, u32[]{:S(2)}, u32[]{:S(2)}) async-start(bf16[32,8,128]{2,1,0:T(8,128)(2,1)} %bitcast.2), calls=%async_computation.2 | async-start | bytes 131072 | tf_op jit(solution)/shard_map/all_to_all | solution.py:263
  58.0 0.0 copy-start.2
  58.0 2.9 %fusion.1.base_ref = f32[128,128]{1,0:T(8,128)S(1)} fusion(bf16[128,8192]{1,0:T(8,128)(2,1)} %bitcast.13, bf16[8192,128]{1,0:T(8,128)(2,1)} %param.6), kind=kOutput, calls=%fused_computation.1 | convolution fusion | flops 268435456 | bytes 4259840 | tf_op jit(solution)/shard_map/dot_general | solution.py:244
  60.9 0.0 copy-done.2
  60.9 0.3 shard_map.55.place_ref
  61.2 6.8 %all-to-all-done.2 = bf16[32,8,128]{2,1,0:T(8,128)(2,1)S(1)} async-done(((bf16[32,8,128]{2,1,0:T(8,128)(2,1)}), bf16[32,8,128]{2,1,0:T(8,128)(2,1)S(1)}, u32[]{:S(2)}, u32[]{:S(2)}) %all-to-all-start.2) | async-done | bytes 65568 | tf_op jit(solution)/shard_map/all_to_all | solution.py:263
  68.0 0.8 %shard_map.60 = bf16[128,128]{1,0:T(8,128)(2,1)} custom-call(bf16[128,256]{1,0:T(8,128)(2,1)S(1)} %shard_map.55.place_ref, bf16[256,128]{1,0:T(8,128)(2,1)S(1)} %bitcast.10, f32[128,128]{1,0:T(8,128)S(1)} %fusion.1.base_ref), custom_call_target="tpu_custom_call" | custom-call | bytes 196608 | tf_op jit(solution)/shard_map/pallas_call | solution.py:203
  (1 shorter events, 0.0 us)
Async XLA Ops:
  0.0 16.2 %copy-start = (bf16[4,1024,64]{1,2,0:T(8,128)(2,1)S(1)}, bf16[4,1024,64]{1,2,0:T(8,128)(2,1)}, u32[]{:S(2)}) copy-start(bf16[4,1024,64]{1,2,0:T(8,128)(2,1)} %param.7) | copy-start | bytes 1572868
  2.3 40.7 %copy-start.1 = (bf16[4,64,128]{2,1,0:T(8,128)(2,1)S(1)}, bf16[4,64,128]{2,1,0:T(8,128)(2,1)}, u32[]{:S(2)}) copy-start(bf16[4,64,128]{2,1,0:T(8,128)(2,1)} %param.8) | copy-start | bytes 196612
  2.3 31.9 %all-to-all-start = ((bf16[64,2,2176]{2,1,0:T(2,128)(2,1)}), bf16[64,2,2176]{2,1,0:T(2,128)(2,1)S(1)}, u32[]{:S(2)}, u32[]{:S(2)}) async-start(bf16[64,2,2176]{2,1,0:T(2,128)(2,1)} %shard_map.56), calls=%async_computation | async-start | bytes 1114112 | tf_op jit(solution)/shard_map/all_to_all | solution.py:235
  16.3 10.2 %collective-permute-start = (bf16[4,64,512]{2,1,0:T(8,128)(2,1)S(1)}, bf16[4,64,512]{2,1,0:T(8,128)(2,1)S(1)}, u32[]{:S(2)}, u32[]{:S(2)}) collective-permute-start(bf16[4,64,512]{2,1,0:T(8,128)(2,1)S(1)} %get-tuple-element.10), channel_id=1, source_target_pairs={{0,1},{1,2},{2,3},{3,4},{4,5},{5,6},{6,7},{7,0},{8,9},{9,10},{10,1... | collective-permute-start | bytes 786440 | tf_op jit(solution)/shard_map/ppermute | solution.py:240
  19.8 9.9 %collective-permute-start.1 = (bf16[4,64,512]{2,1,0:T(8,128)(2,1)S(1)}, bf16[4,64,512]{2,1,0:T(8,128)(2,1)S(1)}, u32[]{:S(2)}, u32[]{:S(2)}) collective-permute-start(bf16[4,64,512]{2,1,0:T(8,128)(2,1)S(1)} %get-tuple-element.9), channel_id=1, source_target_pairs={{0,7},{1,0},{2,1},{3,2},{4,3},{5,4},{6,5},{7,6},{8,15},{9,8},{10,9... | collective-permute-start | bytes 786440 | tf_op jit(solution)/shard_map/ppermute | solution.py:241
  35.4 15.8 %all-to-all-start.1 = ((bf16[16,32,128]{2,1,0:T(8,128)(2,1)}), bf16[16,32,128]{2,1,0:T(8,128)(2,1)S(1)}, u32[]{:S(2)}, u32[]{:S(2)}) async-start(bf16[16,32,128]{2,1,0:T(8,128)(2,1)} %shard_map.57), calls=%async_computation.1 | async-start | bytes 262144 | tf_op jit(solution)/shard_map/all_to_all | solution.py:254
  43.0 3.1 %collective-permute-start.2 = (bf16[256,128]{1,0:T(8,128)(2,1)S(1)}, bf16[256,128]{1,0:T(8,128)(2,1)S(1)}, u32[]{:S(2)}, u32[]{:S(2)}) collective-permute-start(bf16[256,128]{1,0:T(8,128)(2,1)S(1)} %bitcast.11), channel_id=1, source_target_pairs={{0,8},{8,0},{16,24},{24,16},{32,40},{40,32},{48,56},{56,48},{64,72... | collective-permute-start | bytes 196616 | tf_op jit(solution)/shard_map/ppermute | solution.py:242
  52.3 15.7 %all-to-all-start.2 = ((bf16[32,8,128]{2,1,0:T(8,128)(2,1)}), bf16[32,8,128]{2,1,0:T(8,128)(2,1)S(1)}, u32[]{:S(2)}, u32[]{:S(2)}) async-start(bf16[32,8,128]{2,1,0:T(8,128)(2,1)} %bitcast.2), calls=%async_computation.2 | async-start | bytes 131072 | tf_op jit(solution)/shard_map/all_to_all | solution.py:263
  58.0 2.9 %copy-start.2 = (s32[2,64]{1,0:T(2,128)S(1)}, s32[2,64]{1,0:T(2,128)}, u32[]{:S(2)}) copy-start(s32[2,64]{1,0:T(2,128)} %index_ref.3) | copy-start | bytes 1540

commit v8 on v7

--- a/solution.py
+++ b/solution.py
@@ -67,7 +67,7 @@
         chip_hit = wide == (line & -4) + 2 * core + (line & 1)
         found = jnp.where(chip_hit & (place == p), label, 0.0)
         found = jnp.sum(found, axis=1, keepdims=True)
-        labels = found if field == 0 else jnp.where(column // 32 == field, found, labels)
+        labels = found if field == 0 else jnp.where(column >> 5 == field, found, labels)
     labels = jnp.broadcast_to(labels, (rows, 128)).astype(BF16)
     out_ref[:, :, 2 * width :] = labels.reshape(rows // 2, 2, 128)
     select = jnp.where(hit & (place == parity.astype(F32)), 1.0, 0.0).astype(BF16)
@@ -78,7 +78,7 @@
     out_ref[:, :, : 2 * width] = packed.reshape(rows // 2, 2, 2 * width)
 
 
-def shrink_kernel(received_ref, before_ref, own_ref, after_ref, partial_ref):
+def shrink_kernel(received_ref, before_ref, own_ref, after_ref, partial_ref, label_ref):
     shards, groups, width = received_ref.shape
     width = (width - 128) // 2
     lines = shards * groups
@@ -97,7 +97,7 @@
         product = mine if at == 0 else product + mine
         at += size
     label = received_ref[:, :, 2 * width :].reshape(lines, 128)
-    field = iota((lines, 128), 1) // 32
+    field = iota((lines, 128), 1) >> 5
     here = over_lanes(jnp.where(field == core * 2 + parity, label.astype(F32), 0.0))
     upper = (iota((lines, 128), 1) // 64).astype(F32)
     total = jnp.where(here == upper + 1.0, product[:, :128], 0.0)
@@ -122,21 +122,15 @@
         planes = partial_ref.shape[0] // 2
         for peer in range(planes):
             partial_ref[c * planes + peer] = out
-
-
-def label_kernel(received_ref, out_ref):
-    shards, groups, width = received_ref.shape
-    label = received_ref[:, :, width - 128 :].reshape(shards * groups, 128)
-    core = lax.axis_index("dp") % 2
-    lines = out_ref.shape[0]
-    line = iota((lines, shards * groups), 0)
-    source = (line // 8 * 2 + core) * 2 + line % 2
-    take = jnp.where(iota((lines, shards * groups), 1) == source, 1.0, 0.0).astype(BF16)
+    out_lines = label_ref.shape[0]
+    line = iota((out_lines, lines), 0)
+    source = ((line >> 3) * 2 + core) * 2 + (line & 1)
+    take = jnp.where(iota((out_lines, lines), 1) == source, 1.0, 0.0).astype(BF16)
     label = jnp.dot(take, label, preferred_element_type=F32)
-    line = iota((lines, 128), 0)
-    label = over_lanes(jnp.where(iota((lines, 128), 1) // 32 == line // 2 % 4, label, 0.0))
-    other = (label > 0.0) & (line // 4 % 2 != core)
-    out_ref[...] = jnp.where(other, label + 4.0, label).astype(BF16)
+    line = iota((out_lines, 128), 0)
+    label = over_lanes(jnp.where(iota((out_lines, 128), 1) >> 5 == (line >> 1) & 3, label, 0.0))
+    other = (label > 0.0) & ((line >> 2) & 1 != core)
+    label_ref[...] = jnp.where(other, label + 4.0, label).astype(BF16)
 
 
 def expand_kernel(partial_ref, label_ref, up_own_ref, up_other_ref, out_ref):
@@ -245,16 +239,18 @@
     (place,) = call(
         functools.partial(place_kernel, owned), [shape((rows, owners * 4), BF16)], (index,)
     )
-    (partial,) = call(
+    received, before, after, up_other, base, place = lax.optimization_barrier(
+        (received, before, after, up_other, base, place)
+    )
+    partial, label = call(
         shrink_kernel,
-        [shape((2 * planes, owners // 2, 128), BF16)],
+        [shape((2 * planes, owners // 2, 128), BF16), shape((owners * 4, 128), BF16)],
         (received, before, down_own, after),
     )
     chips = [list(range(i, i + 2 * planes)) for i in range(0, owners * planes, 2 * planes)]
     partials = lax.all_to_all(
         partial, ("dp", "tensor"), split_axis=0, concat_axis=0, tiled=True, axis_index_groups=chips
     )
-    (label,) = call(label_kernel, [shape((owners * 4, 128), BF16)], (received,))
     (terms,) = call(
         expand_kernel,
         [shape((owners * 4, columns), BF16)],

time: 69.2 us -> 67.3 us (0.973)
  blocking collectives: 0 us -> 31.1 us
  waiting for transfers between devices: 24.7 us -> 6.88 us
  starting transfers between devices: 35.1 us -> 21.6 us
  Pallas kernels: 5.86 us -> 4.31 us
    all_to_all x0 -> x2, blocking collectives: none -> 31.1 us  [the longest x1 15.6 us: on_device(): lax.all_to_all(partial, ('dp', 'tensor'), split_axis=0, concat_axis=0, ti...]
    all_to_all x2 -> x0, starting transfers between devices: 13.2 us -> none  [the longest x1 7.56 us: on_device(): lax.all_to_all(partial, ('dp', 'tensor'), split_axis=0, concat_axis=0, ti...]
    all_to_all x2 -> x0, waiting for transfers between devices: 11.8 us -> none  [the longest x1 6.77 us: on_device(): lax.all_to_all(terms.reshape(owners // 2, 8, columns), 'dp', split_axis=0...]
    ppermute x1, waiting for transfers between devices: 4.3 us -> 0.01 us  [on_device(): lax.ppermute(upper, 'tensor', [(i, (i + 1) % planes) for i in range(plane...]
    pallas_call x6 -> x5, Pallas kernels: 5.86 us -> 4.31 us  [call(): pl.pallas_call(kernel, out_shape=shapes, in_specs=[spec(i in in_hbm) for...]
    ppermute x1, waiting for transfers between devices: 3.21 us -> 2.32 us  [on_device(): lax.ppermute(lower, 'tensor', [(i, (i - 1) % planes) for i in range(plane...]
    ppermute x1, waiting for transfers between devices: 0.78 us -> 0.01 us  [on_device(): up_other = lax.ppermute(up_later, 'dp', [(i, i ^ 1) for i in range(owners)])]
  transfers between devices with their start and end apart: 6 -> 4, of which waited for: 6 -> 2; matrix products, arithmetic and copies ran while one was open for 4% -> 4% of each run, Pallas kernels for 1% -> 0%
where the time goes in v8:
time: 67.3 us; the launch traced here: 66.9 us
  blocking collectives  31.1 us (46%)
  starting transfers between devices  21.6 us (32%)
  waiting for transfers between devices  6.88 us (10%)
  Pallas kernels  4.31 us (6%)
  matrix products  2.92 us (4%)
    all_to_all x1, blocking collectives, on_device(): lax.all_to_all(partial, ('dp', 'tensor'), split_axis=0, concat_axis=0, ti...  15.6 us
    all_to_all x1, blocking collectives, on_device(): lax.all_to_all(terms.reshape(owners // 2, 8, columns), 'dp', split_axis=0...  15.5 us
    all_to_all x1, starting transfers between devices, on_device(): lax.all_to_all(packed, 'dp', split_axis=0, concat_axis=0, tiled=True)  13.8 us
    all_to_all x1, waiting for transfers between devices, on_device(): lax.all_to_all(packed, 'dp', split_axis=0, concat_axis=0, tiled=True)  4.56 us
    pallas_call x5, Pallas kernels, call(): pl.pallas_call(kernel, out_shape=shapes, in_specs=[spec(i in in_hbm) for...  4.31 us
    ppermute x1, starting transfers between devices, on_device(): lax.ppermute(upper, 'tensor', [(i, (i + 1) % planes) for i in range(plane...  3.49 us
    dot_general x1, matrix products, on_device(): jnp.dot(tokens.reshape(rows, features), value_matrix, preferred_element_t...  2.92 us
    ppermute x1, starting transfers between devices, on_device(): lax.ppermute(lower, 'tensor', [(i, (i - 1) % planes) for i in range(plane...  2.35 us
  transfers between devices with their start and end apart: 4, of which 2 were waited for; matrix products, arithmetic and copies ran while one was open for 4% of the time, Pallas kernels for 0%

profile of v8, /device:TPU:8, one launch (start us, length us, event | category | flops | bytes accessed | tf_op | source)
XLA Modules:
  0.0 66.9 jit_solution(9185618508302455846)
XLA Ops:
  0.0 0.0 copy-start
  0.0 0.0 copy-start.1
  0.0 2.2 %shard_map.55 = bf16[64,2,2176]{2,1,0:T(2,128)(2,1)} custom-call(s32[2,64]{1,0:T(2,128)} %index_ref.3, bf16[2,64,8192]{2,1,0:T(8,128)(2,1)} %tokens_ref.1), custom_call_target="tpu_custom_call" | custom-call | bytes 2097664 | tf_op jit(solution)/shard_map/pallas_call | solution.py:197
  2.3 13.8 %all-to-all-start = ((bf16[64,2,2176]{2,1,0:T(2,128)(2,1)}), bf16[64,2,2176]{2,1,0:T(2,128)(2,1)S(1)}, u32[]{:S(2)}, u32[]{:S(2)}) async-start(bf16[64,2,2176]{2,1,0:T(2,128)(2,1)} %shard_map.55), calls=%async_computation | async-start | bytes 1114112 | tf_op jit(solution)/shard_map/all_to_all | solution.py:229
  16.1 0.0 copy-done
  16.1 3.5 %collective-permute-start = (bf16[4,64,512]{2,1,0:T(8,128)(2,1)S(1)}, bf16[4,64,512]{2,1,0:T(8,128)(2,1)S(1)}, u32[]{:S(2)}, u32[]{:S(2)}) collective-permute-start(bf16[4,64,512]{2,1,0:T(8,128)(2,1)S(1)} %get-tuple-element.26), channel_id=1, source_target_pairs={{0,1},{1,2},{2,3},{3,4},{4,5},{5,6},{6,7},{7,0},{8,9},{9,10},{10,1... | collective-permute-start | bytes 786440 | tf_op jit(solution)/shard_map/ppermute | solution.py:234
  19.6 2.4 %collective-permute-start.1 = (bf16[4,64,512]{2,1,0:T(8,128)(2,1)S(1)}, bf16[4,64,512]{2,1,0:T(8,128)(2,1)S(1)}, u32[]{:S(2)}, u32[]{:S(2)}) collective-permute-start(bf16[4,64,512]{2,1,0:T(8,128)(2,1)S(1)} %get-tuple-element.25), channel_id=1, source_target_pairs={{0,7},{1,0},{2,1},{3,2},{4,3},{5,4},{6,5},{7,6},{8,15},{9,8},{10,9... | collective-permute-start | bytes 786440 | tf_op jit(solution)/shard_map/ppermute | solution.py:235
  22.0 0.0 copy-done.1
  22.0 1.9 %collective-permute-start.2 = (bf16[256,128]{1,0:T(8,128)(2,1)S(1)}, bf16[256,128]{1,0:T(8,128)(2,1)S(1)}, u32[]{:S(2)}, u32[]{:S(2)}) collective-permute-start(bf16[256,128]{1,0:T(8,128)(2,1)S(1)} %bitcast.12), channel_id=1, source_target_pairs={{0,8},{8,0},{16,24},{24,16},{32,40},{40,32},{48,56},{56,48},{64,72... | collective-permute-start | bytes 196616 | tf_op jit(solution)/shard_map/ppermute | solution.py:236
  23.9 0.0 copy-start.2
  23.9 2.9 %fusion.1.base_ref = f32[128,128]{1,0:T(8,128)S(1)} fusion(bf16[128,8192]{1,0:T(8,128)(2,1)} %bitcast.14, bf16[8192,128]{1,0:T(8,128)(2,1)} %param.6), kind=kOutput, calls=%fused_computation.1 | convolution fusion | flops 268435456 | bytes 4259840 | tf_op jit(solution)/shard_map/dot_general | solution.py:238
  26.9 0.0 copy-done.2
  26.9 0.3 shard_map.56.place_ref
  27.2 0.0 collective-permute-done.2.up_other_ref
  27.2 0.0 collective-permute-done.before_ref
  27.2 2.3 %collective-permute-done.1.after_ref = bf16[4,64,512]{2,1,0:T(8,128)(2,1)S(1)} collective-permute-done((bf16[4,64,512]{2,1,0:T(8,128)(2,1)S(1)}, bf16[4,64,512]{2,1,0:T(8,128)(2,1)S(1)}, u32[]{:S(2)}, u32[]{:S(2)}) %collective-permute-start.1) | collective-permute-done | bytes 262176 | tf_op jit(solution)/shard_map/ppermute | solution.py:235
  29.5 4.6 %all-to-all-done.received_ref = bf16[64,2,2176]{2,1,0:T(2,128)(2,1)S(1)} async-done(((bf16[64,2,2176]{2,1,0:T(2,128)(2,1)}), bf16[64,2,2176]{2,1,0:T(2,128)(2,1)S(1)}, u32[]{:S(2)}, u32[]{:S(2)}) %all-to-all-start) | async-done | bytes 557088 | tf_op jit(solution)/shard_map/all_to_all | solution.py:229
  34.1 0.6 shard_map.57
  34.7 15.6 %all_to_all.15.partial_ref = bf16[16,32,128]{2,1,0:T(8,128)(2,1)S(1)} all-to-all(bf16[16,32,128]{2,1,0:T(8,128)(2,1)S(1)} %get-tuple-element.21), channel_id=1, replica_groups={{0,1,2,3,4,5,6,7,8,9,10,11,12,13,14,15},{16,17,18,19,20,21,22,23,24,25,..., dimensions={0} | all-to-all | bytes 262144 | tf_op jit(solution)/shard_map/all_to_all | solution.py:251
  50.3 0.4 shard_map.58
  50.7 15.5 %all_to_all.16 = bf16[32,8,128]{2,1,0:T(8,128)(2,1)S(1)} all-to-all(bf16[32,8,128]{2,1,0:T(8,128)(2,1)S(1)} %bitcast.11), channel_id=1, replica_groups={{0,16,32,48,64,80,96,112,128,144,160,176,192,208,224,240,256,272,288,30..., dimensions={0} | all-to-all | bytes 131072 | tf_op jit(solution)/shard_map/all_to_all | solution.py:259
  66.2 0.8 %shard_map.59 = bf16[128,128]{1,0:T(8,128)(2,1)} custom-call(bf16[128,256]{1,0:T(8,128)(2,1)S(1)} %shard_map.56.place_ref, bf16[256,128]{1,0:T(8,128)(2,1)S(1)} %bitcast.10, f32[128,128]{1,0:T(8,128)S(1)} %fusion.1.base_ref), custom_call_target="tpu_custom_call" | custom-call | bytes 196608 | tf_op jit(solution)/shard_map/pallas_call | solution.py:197
  (1 shorter events, 0.0 us)
Async XLA Ops:
  0.0 16.1 %copy-start = (bf16[4,1024,64]{1,2,0:T(8,128)(2,1)S(1)}, bf16[4,1024,64]{1,2,0:T(8,128)(2,1)}, u32[]{:S(2)}) copy-start(bf16[4,1024,64]{1,2,0:T(8,128)(2,1)} %param.7) | copy-start | bytes 1572868
  0.0 22.0 %copy-start.1 = (bf16[4,64,128]{2,1,0:T(8,128)(2,1)S(1)}, bf16[4,64,128]{2,1,0:T(8,128)(2,1)}, u32[]{:S(2)}) copy-start(bf16[4,64,128]{2,1,0:T(8,128)(2,1)} %param.8) | copy-start | bytes 196612
  2.3 31.8 %all-to-all-start = ((bf16[64,2,2176]{2,1,0:T(2,128)(2,1)}), bf16[64,2,2176]{2,1,0:T(2,128)(2,1)S(1)}, u32[]{:S(2)}, u32[]{:S(2)}) async-start(bf16[64,2,2176]{2,1,0:T(2,128)(2,1)} %shard_map.55), calls=%async_computation | async-start | bytes 1114112 | tf_op jit(solution)/shard_map/all_to_all | solution.py:229
  16.1 11.0 %collective-permute-start = (bf16[4,64,512]{2,1,0:T(8,128)(2,1)S(1)}, bf16[4,64,512]{2,1,0:T(8,128)(2,1)S(1)}, u32[]{:S(2)}, u32[]{:S(2)}) collective-permute-start(bf16[4,64,512]{2,1,0:T(8,128)(2,1)S(1)} %get-tuple-element.26), channel_id=1, source_target_pairs={{0,1},{1,2},{2,3},{3,4},{4,5},{5,6},{6,7},{7,0},{8,9},{9,10},{10,1... | collective-permute-start | bytes 786440 | tf_op jit(solution)/shard_map/ppermute | solution.py:234
  19.6 9.9 %collective-permute-start.1 = (bf16[4,64,512]{2,1,0:T(8,128)(2,1)S(1)}, bf16[4,64,512]{2,1,0:T(8,128)(2,1)S(1)}, u32[]{:S(2)}, u32[]{:S(2)}) collective-permute-start(bf16[4,64,512]{2,1,0:T(8,128)(2,1)S(1)} %get-tuple-element.25), channel_id=1, source_target_pairs={{0,7},{1,0},{2,1},{3,2},{4,3},{5,4},{6,5},{7,6},{8,15},{9,8},{10,9... | collective-permute-start | bytes 786440 | tf_op jit(solution)/shard_map/ppermute | solution.py:235
  22.0 5.2 %collective-permute-start.2 = (bf16[256,128]{1,0:T(8,128)(2,1)S(1)}, bf16[256,128]{1,0:T(8,128)(2,1)S(1)}, u32[]{:S(2)}, u32[]{:S(2)}) collective-permute-start(bf16[256,128]{1,0:T(8,128)(2,1)S(1)} %bitcast.12), channel_id=1, source_target_pairs={{0,8},{8,0},{16,24},{24,16},{32,40},{40,32},{48,56},{56,48},{64,72... | collective-permute-start | bytes 196616 | tf_op jit(solution)/shard_map/ppermute | solution.py:236
  23.9 2.9 %copy-start.2 = (s32[2,64]{1,0:T(2,128)S(1)}, s32[2,64]{1,0:T(2,128)}, u32[]{:S(2)}) copy-start(s32[2,64]{1,0:T(2,128)} %index_ref.3) | copy-start | bytes 1540

commit v9 on v8

v9 whole, which is shorter than its diff:
```python
import functools

import jax
import jax.numpy as jnp
from jax import lax
from jax.experimental import pallas as pl
from jax.experimental.pallas import tpu as pltpu
from jax.sharding import PartitionSpec as P

BF16, F32, I32 = jnp.bfloat16, jnp.float32, jnp.int32
MIB = 1024 * 1024


def iota(shape, dim):
    return lax.broadcasted_iota(I32, shape, dim)


def read_index(index_ref, owned):
    along = jnp.concatenate([index_ref[0:1, :], index_ref[1:2, :]], axis=1)
    rows = along.shape[1]
    shift = owned.bit_length() - 1
    assert owned == 1 << shift
    key = (along >> shift) * 2 + jnp.where(iota((1, rows), 1) >= rows // 2, 1, 0)
    wide = jnp.broadcast_to(key, (rows, rows))
    line, column = iota((rows, rows), 0), iota((rows, rows), 1)
    same = jnp.sum(jnp.where(line == column, wide, 0).astype(F32), axis=1, keepdims=True)
    earlier = (wide.astype(F32) == same) & (line < column)
    place = jnp.sum(jnp.where(earlier, 1.0, 0.0), axis=0, keepdims=True)
    return wide, place, ((along & (owned - 1)) + 1).astype(F32)


def over_lanes(values):
    share = jnp.full((128, 128), 1.0 / 64.0, BF16)
    return jnp.dot(values.astype(BF16), share, preferred_element_type=F32)


def partner(plane, core, planes):
    step = (1 - 2 * (plane % 2)) * (1 - 2 * core)
    return (plane + step + planes) % planes


def pack_kernel(owned, planes, index_ref, tokens_ref, out_ref, held, pairs, indices, sems):
    width = held.shape[2]
    plane = lax.axis_index("tensor")
    parity = plane % 2

    def slice_of(plane):
        return tokens_ref.at[:, :, pl.ds(pl.multiple_of(plane * width, width), width)]

    copies = [
        pltpu.make_async_copy(index_ref, indices, sems.at[0]),
        pltpu.make_async_copy(slice_of(plane), held, sems.at[1]),
    ]
    for core in range(2):
        copies.append(
            pltpu.make_async_copy(
                slice_of(partner(plane, core, planes)), pairs.at[core], sems.at[2 + core]
            )
        )
    for copy in copies:
        copy.start()
    copies[0].wait()
    wide, place, label = read_index(indices, owned)
    rows = wide.shape[0]
    line, column = iota((rows, rows), 0), iota((rows, rows), 1)
    hit = line == wide
    label = jnp.broadcast_to(label, (rows, rows))
    labels = [
        jnp.sum(jnp.where(hit & (place == p), label, 0.0), axis=1, keepdims=True)
        for p in (0.0, 1.0)
    ]
    labels = jnp.where(column < 64, labels[0], labels[1]).astype(BF16)
    out_ref[:, :, 2 * width :] = labels.reshape(rows // 4, 4, 128)
    select = jnp.where(hit & (place == parity.astype(F32)), 1.0, 0.0)
    core = (line >> 1) & 1
    by_core = jnp.concatenate([jnp.where(core == c, select, 0.0) for c in range(2)], axis=1)
    copies[1].wait()
    packed = jnp.dot(
        select.astype(BF16), held[...].reshape(rows, width), preferred_element_type=F32
    )
    out_ref[:, :, :width] = packed.astype(BF16).reshape(rows // 4, 4, width)
    copies[2].wait()
    copies[3].wait()
    packed = jnp.dot(
        by_core.astype(BF16), pairs[...].reshape(2 * rows, width), preferred_element_type=F32
    )
    out_ref[:, :, width : 2 * width] = packed.astype(BF16).reshape(rows // 4, 4, width)


def shrink_kernel(
    received_ref, own_ref, own_pair_ref, other_ref, other_pair_ref, partial_ref, label_ref
):
    chips, per_chip, width = received_ref.shape
    width = (width - 128) // 2
    lines = chips * per_chip
    parity = lax.axis_index("tensor") % 2
    core = lax.axis_index("dp") % 2
    products = []
    for weights in ((own_ref, own_pair_ref), (other_ref, other_pair_ref)):
        product = None
        for e in range(2):
            mine = lax.dot_general(
                received_ref[:, :, e * width : (e + 1) * width].reshape(lines, width),
                weights[e][...].reshape(256, width),
                (((1,), (1,)), ((), ())),
                preferred_element_type=F32,
            )
            product = mine if e == 0 else product + mine
        products.append(product)
    own = (iota((lines, 256), 0) >> 1) & 1 == core
    product = jnp.where(own, products[0], products[1])
    label = received_ref[:, :, 2 * width :].reshape(lines, 128)
    upper = iota((lines, 128), 1) >> 6
    here = over_lanes(jnp.where(upper == parity, label.astype(F32), 0.0))
    upper = upper.astype(F32)
    total = jnp.where(here == upper + 1.0, product[:, :128], 0.0)
    total = total + jnp.where(here == upper + 3.0, product[:, 128:], 0.0)
    total = total + pltpu.roll(total, 64, 1)
    half = lines // 2
    packed = jnp.where(upper[:half] == 0.0, total[:half], total[half:]).astype(BF16)
    for peer in range(partial_ref.shape[0]):
        partial_ref[peer] = packed
    out_lines = label_ref.shape[0]
    line = iota((out_lines, lines), 0)
    source = (line >> 2) * 2 + (line & 1)
    take = jnp.where(iota((out_lines, lines), 1) == source, 1.0, 0.0).astype(BF16)
    label = jnp.dot(take, label, preferred_element_type=F32)
    line = iota((out_lines, 128), 0)
    label = over_lanes(jnp.where(iota((out_lines, 128), 1) >> 6 == (line >> 1) & 1, label, 0.0))
    other = (label > 0.0) & ((line >> 2) & 1 != core)
    label_ref[...] = jnp.where(other, label + 4.0, label).astype(BF16)


def expand_kernel(partial_ref, label_ref, up_own_ref, up_other_ref, out_ref):
    planes, half, _ = partial_ref.shape
    sums = []
    for p in range(2):
        total = partial_ref[p].astype(F32)
        for peer in range(p + 2, planes, 2):
            total = total + partial_ref[peer].astype(F32)
        sums.append(total.reshape(half // 8, 8, 128))
    spot = iota(sums[0].shape, 1) >> 1
    by_chip = []
    for chip in range(2):
        out = None
        for core in range(2):
            for p in range(2):
                by = (2 * core + 2 * p - 4 * chip) % 8
                piece = pltpu.roll(sums[p], by, 1) if by else sums[p]
                out = piece if out is None else jnp.where(spot == 2 * core + p, piece, out)
        by_chip.append(out)
    total = jnp.stack(by_chip, axis=1).reshape(half * 2, 128)
    turned = pltpu.roll(total, 64, 1)
    upper = iota(total.shape, 1) // 64
    lines = total.shape[0]
    for e in range(2):
        row = jnp.where(upper == e, total, turned)
        label = label_ref[e * lines : (e + 1) * lines].astype(F32)
        terms = None
        for up_ref, add in ((up_own_ref, 1.0), (up_other_ref, 5.0)):
            first = upper.astype(F32) + add
            left = jnp.where(label == first, row, 0.0)
            right = jnp.where(label == first + 2.0, row, 0.0)
            wide = jnp.concatenate([left, right], axis=1)
            high = wide.astype(BF16)
            for part in (high, (wide - high.astype(F32)).astype(BF16)):
                mine = jnp.dot(part, up_ref[...], preferred_element_type=F32)
                terms = mine if terms is None else terms + mine
        out_ref[e * lines : (e + 1) * lines] = terms.astype(BF16)


def place_kernel(owned, index_ref, out_ref):
    wide, place, _ = read_index(index_ref, owned)
    rows = wide.shape[0]
    key = wide[:1]
    target = (key >> 1) * 4 + place.astype(I32) * 2 + (key & 1)
    line, column = iota((rows, rows), 0), iota((rows, rows), 1)
    target = jnp.broadcast_to(target, (rows, rows))
    target = jnp.sum(jnp.where(line == column, target, 0).astype(F32), axis=1, keepdims=True)
    out_ref[...] = jnp.where(iota(out_ref.shape, 1).astype(F32) == target, 1.0, 0.0).astype(BF16)


def call(kernel, shapes, ins, scratch=(), in_hbm=(), vmem=40):
    nbytes = sum(v.size * v.dtype.itemsize for v in ins)

    def spec(hbm):
        return pl.BlockSpec(memory_space=pltpu.HBM if hbm else pltpu.VMEM)

    return pl.pallas_call(
        kernel,
        out_shape=shapes,
        in_specs=[spec(i in in_hbm) for i in range(len(ins))],
        out_specs=[spec(False) for _ in shapes],
        scratch_shapes=scratch,
        compiler_params=pltpu.CompilerParams(vmem_limit_bytes=vmem * MIB),
        cost_estimate=pl.CostEstimate(flops=0, bytes_accessed=nbytes, transcendentals=0),
    )(*ins)


def on_device(tokens, value_matrix, down, up, index):
    groups, rows_local, features = tokens.shape
    owners = lax.axis_size("dp")
    planes = lax.axis_size("tensor")
    owned, width, rank = down.shape
    columns = up.shape[2]
    rows = groups * rows_local
    shape = jax.ShapeDtypeStruct

    cores = 2
    same_core = [list(range(core, owners, cores)) for core in range(cores)]

    (packed,) = call(
        functools.partial(pack_kernel, owned, planes),
        [shape((owners // cores, cores * groups, 2 * width + 128), BF16)],
        (index, tokens),
        [
            pltpu.VMEM((groups, rows_local, width), BF16),
            pltpu.VMEM((cores, groups, rows_local, width), BF16),
            pltpu.VMEM(index.shape, I32),
            pltpu.SemaphoreType.DMA((4,)),
        ],
        in_hbm=(0, 1),
        vmem=62,
    )
    received = lax.all_to_all(
        packed, "dp", split_axis=0, concat_axis=0, tiled=True, axis_index_groups=same_core
    )

    def from_other_core(x):
        return lax.ppermute(x, "dp", [(i, i ^ 1) for i in range(owners)])

    down_own, up_own = down.transpose(0, 2, 1), up.reshape(owned * rank, columns)
    down_later, up_later, _ = lax.optimization_barrier((down_own, up_own, packed))
    pair_own = lax.ppermute(
        down_later,
        ("dp", "tensor"),
        [
            (i * planes + t, i * planes + partner(t, i % cores, planes))
            for i in range(owners)
            for t in range(planes)
        ],
    )
    down_other, up_other = from_other_core(down_later), from_other_core(up_later)
    pair_other = from_other_core(pair_own)

    base = jnp.dot(tokens.reshape(rows, features), value_matrix, preferred_element_type=F32)
    (place,) = call(
        functools.partial(place_kernel, owned), [shape((rows, owners * 4), BF16)], (index,)
    )
    received, pair_own, down_other, pair_other, up_other, base, place = lax.optimization_barrier(
        (received, pair_own, down_other, pair_other, up_other, base, place)
    )
    partial, label = call(
        shrink_kernel,
        [shape((planes, owners, 128), BF16), shape((owners * 4, 128), BF16)],
        (received, down_own, pair_own, down_other, pair_other),
    )
    partials = lax.all_to_all(partial, "tensor", split_axis=0, concat_axis=0, tiled=True)
    (terms,) = call(
        expand_kernel,
        [shape((owners * 4, columns), BF16)],
        (partials, label, up_own, up_other),
    )
    arrived = lax.all_to_all(
        terms.reshape(owners // cores, 4 * cores, columns),
        "dp",
        split_axis=0,
        concat_axis=0,
        tiled=True,
        axis_index_groups=same_core,
    ).reshape(owners * 4, columns)
    out = (base + jnp.dot(place, arrived, preferred_element_type=F32)).astype(BF16)
    return out.reshape(groups, rows_local, columns)


def solution(mesh):
    in_specs = (
        P(None, "dp", None),
        P(None, "tensor"),
        P("dp", "tensor", None),
        P("dp", None, "tensor"),
        P(None, "dp"),
    )
    out_specs = P(None, "dp", "tensor")
    return jax.shard_map(
        on_device, mesh=mesh, in_specs=in_specs, out_specs=out_specs, check_vma=False
    )
```

time: 67.3 us -> 71.7 us (1.065)
  the two profiles are of different devices: /device:TPU:8 before, /device:TPU:2 now
where the time goes in v9:
time: 71.7 us; the launch traced here: 71.4 us
  blocking collectives  34.7 us (48%)
  starting transfers between devices  24.1 us (34%)
  waiting for transfers between devices  4.78 us (7%)
  Pallas kernels  3.98 us (6%)
  matrix products  3.06 us (4%)
    all_to_all x1, blocking collectives, on_device(): lax.all_to_all(terms.reshape(owners // cores, 4 * cores, columns), 'dp',...  18.5 us
    all_to_all x1, blocking collectives, on_device(): lax.all_to_all(partial, 'tensor', split_axis=0, concat_axis=0, tiled=True)  16.2 us
    all_to_all x1, starting transfers between devices, on_device(): lax.all_to_all(packed, 'dp', split_axis=0, concat_axis=0, tiled=True, axi...  13.5 us
    ppermute x3, starting transfers between devices, from_other_core(): return lax.ppermute(x, 'dp', [(i, i ^ 1) for i in range(owners)])  7.12 us
    ppermute x1, waiting for transfers between devices, on_device(): lax.ppermute(down_later, ('dp', 'tensor'), [(i * planes + t, i * planes +...  4.77 us
    pallas_call x4, Pallas kernels, call(): pl.pallas_call(kernel, out_shape=shapes, in_specs=[spec(i in in_hbm) for...  3.98 us
    ppermute x1, starting transfers between devices, on_device(): lax.ppermute(down_later, ('dp', 'tensor'), [(i * planes + t, i * planes +...  3.49 us
    dot_general x1, matrix products, on_device(): jnp.dot(tokens.reshape(rows, features), value_matrix, preferred_element_t...  2.92 us
  transfers between devices with their start and end apart: 5, of which 1 were waited for; matrix products, arithmetic and copies ran while one was open for 4% of the time, Pallas kernels for 0%

profile of v9, /device:TPU:2, one launch (start us, length us, event | category | flops | bytes accessed | tf_op | source)
XLA Modules:
  0.0 71.4 jit_solution(2825235131790427108)
XLA Ops:
  0.0 0.0 copy-start.1
  0.0 0.0 copy-start
  0.0 2.3 %shard_map.55 = bf16[32,4,2176]{2,1,0:T(4,128)(2,1)} custom-call(s32[2,64]{1,0:T(2,128)} %index_ref.3, bf16[2,64,8192]{2,1,0:T(8,128)(2,1)} %tokens_ref.1), custom_call_target="tpu_custom_call" | custom-call | bytes 2097664 | tf_op jit(solution)/shard_map/pallas_call | solution.py:189
  2.3 13.5 %all-to-all-start = ((bf16[32,4,2176]{2,1,0:T(4,128)(2,1)}), bf16[32,4,2176]{2,1,0:T(4,128)(2,1)S(1)}, u32[]{:S(2)}, u32[]{:S(2)}) async-start(bf16[32,4,2176]{2,1,0:T(4,128)(2,1)} %shard_map.55), calls=%async_computation | async-start | bytes 1114112 | tf_op jit(solution)/shard_map/all_to_all | solution.py:225
  15.8 0.0 copy-done
  15.8 3.5 %collective-permute-start = (bf16[4,64,1024]{2,1,0:T(8,128)(2,1)S(1)}, bf16[4,64,1024]{2,1,0:T(8,128)(2,1)S(1)}, u32[]{:S(2)}, u32[]{:S(2)}) collective-permute-start(bf16[4,64,1024]{2,1,0:T(8,128)(2,1)S(1)} %bitcast.11), channel_id=1, source_target_pairs={{0,1},{1,0},{2,3},{3,2},{4,5},{5,4},{6,7},{7,6},{8,15},{9,10},{10,... | collective-permute-start | bytes 1572872 | tf_op jit(solution)/shard_map/ppermute | solution.py:234
  19.3 2.8 %collective-permute-start.1 = (bf16[4,64,1024]{2,1,0:T(8,128)(2,1)S(1)}, bf16[4,64,1024]{2,1,0:T(8,128)(2,1)S(1)}, u32[]{:S(2)}, u32[]{:S(2)}) collective-permute-start(bf16[4,64,1024]{2,1,0:T(8,128)(2,1)S(1)} %bitcast.12), channel_id=1, source_target_pairs={{0,8},{8,0},{16,24},{24,16},{32,40},{40,32},{48,56},{56,48},{64,72... | collective-permute-start | bytes 1572872 | tf_op jit(solution)/shard_map/ppermute | solution.py:230
  22.1 4.8 %collective-permute-done.own_pair_ref = bf16[4,64,1024]{2,1,0:T(8,128)(2,1)S(1)} collective-permute-done((bf16[4,64,1024]{2,1,0:T(8,128)(2,1)S(1)}, bf16[4,64,1024]{2,1,0:T(8,128)(2,1)S(1)}, u32[]{:S(2)}, u32[]{:S(2)}) %collective-permute-start) | collective-permute-done | bytes 524320 | tf_op jit(solution)/shard_map/ppermute | solution.py:234
  26.9 2.1 %collective-permute-start.2 = (bf16[4,64,1024]{2,1,0:T(8,128)(2,1)S(1)}, bf16[4,64,1024]{2,1,0:T(8,128)(2,1)S(1)}, u32[]{:S(2)}, u32[]{:S(2)}) collective-permute-start(bf16[4,64,1024]{2,1,0:T(8,128)(2,1)S(1)} %collective-permute-done.own_pair_ref), channel_id=1, source_target_pairs={{0,8},{8,0},{16,24},{24,16},{32,40},{40,32},{48,56},{56,48},{64,72... | collective-permute-start | bytes 1572872 | tf_op jit(solution)/shard_map/ppermute | solution.py:230
  29.0 0.0 copy-done.1
  29.0 2.3 %collective-permute-start.3 = (bf16[256,128]{1,0:T(8,128)(2,1)S(1)}, bf16[256,128]{1,0:T(8,128)(2,1)S(1)}, u32[]{:S(2)}, u32[]{:S(2)}) collective-permute-start(bf16[256,128]{1,0:T(8,128)(2,1)S(1)} %bitcast.15), channel_id=1, source_target_pairs={{0,8},{8,0},{16,24},{24,16},{32,40},{40,32},{48,56},{56,48},{64,72... | collective-permute-start | bytes 196616 | tf_op jit(solution)/shard_map/ppermute | solution.py:230
  31.3 0.0 copy-start.2
  31.3 2.9 %fusion.2 = f32[128,128]{1,0:T(8,128)S(1)} fusion(bf16[128,8192]{1,0:T(8,128)(2,1)} %bitcast.17, bf16[8192,128]{1,0:T(8,128)(2,1)} %param.6), kind=kOutput, calls=%fused_computation.3 | convolution fusion | flops 268435456 | bytes 4259840 | tf_op jit(solution)/shard_map/dot_general | solution.py:246
  34.2 0.0 copy-done.2
  34.2 0.3 shard_map.56
  34.5 0.0 collective-permute-done.3.up_other_ref
  34.5 0.0 collective-permute-done.1.other_ref
  34.5 0.0 collective-permute-done.2.other_pair_ref
  34.5 0.0 all-to-all-done.received_ref
  34.5 1.0 %shard_map.57 = (bf16[8,64,128]{2,1,0:T(8,128)(2,1)S(1)}, bf16[256,128]{1,0:T(8,128)(2,1)S(1)}) custom-call(bf16[32,4,2176]{2,1,0:T(4,128)(2,1)S(1)} %all-to-all-done.received_ref, bf16[4,64,1024]{2,1,0:T(8,128)(2,1)S(1)} %bitcast.13, bf16[4,64,1024]{2,1,0:T(8,128)(2,1)S(1)} %collective-permute-done.own_pair_ref, ...), custom_call_target="tpu_custom_call" | custom-call | bytes 2654208 | tf_op jit(solution)/shard_map/pallas_call | solution.py:189
  35.5 16.2 %all_to_all.15.partial_ref = bf16[8,64,128]{2,1,0:T(8,128)(2,1)S(1)} all-to-all(bf16[8,64,128]{2,1,0:T(8,128)(2,1)S(1)} %get-tuple-element.24), channel_id=1, replica_groups=mesh['dp'=64,'tensor'=8] {'tensor'}, dimensions={0} | all-to-all | bytes 262144 | tf_op jit(solution)/shard_map/all_to_all | solution.py:258
  51.7 0.4 shard_map.58
  52.1 18.5 %all_to_all.16 = bf16[32,8,128]{2,1,0:T(8,128)(2,1)S(1)} all-to-all(bf16[32,8,128]{2,1,0:T(8,128)(2,1)S(1)} %bitcast.14), channel_id=1, replica_groups={{0,16,32,48,64,80,96,112,128,144,160,176,192,208,224,240,256,272,288,30..., dimensions={0} | all-to-all | bytes 131072 | tf_op jit(solution)/shard_map/all_to_all | solution.py:264
  70.6 0.1 fusion
  70.7 0.6 add_convert_fusion
Async XLA Ops:
  0.0 29.0 %copy-start.1 = (bf16[4,64,128]{2,1,0:T(8,128)(2,1)S(1)}, bf16[4,64,128]{2,1,0:T(8,128)(2,1)}, u32[]{:S(2)}) copy-start(bf16[4,64,128]{2,1,0:T(8,128)(2,1)} %param.8) | copy-start | bytes 196612
  0.0 15.8 %copy-start = (bf16[4,1024,64]{1,2,0:T(8,128)(2,1)S(1)}, bf16[4,1024,64]{1,2,0:T(8,128)(2,1)}, u32[]{:S(2)}) copy-start(bf16[4,1024,64]{1,2,0:T(8,128)(2,1)} %param.7) | copy-start | bytes 1572868
  2.3 32.2 %all-to-all-start = ((bf16[32,4,2176]{2,1,0:T(4,128)(2,1)}), bf16[32,4,2176]{2,1,0:T(4,128)(2,1)S(1)}, u32[]{:S(2)}, u32[]{:S(2)}) async-start(bf16[32,4,2176]{2,1,0:T(4,128)(2,1)} %shard_map.55), calls=%async_computation | async-start | bytes 1114112 | tf_op jit(solution)/shard_map/all_to_all | solution.py:225
  15.8 11.1 %collective-permute-start = (bf16[4,64,1024]{2,1,0:T(8,128)(2,1)S(1)}, bf16[4,64,1024]{2,1,0:T(8,128)(2,1)S(1)}, u32[]{:S(2)}, u32[]{:S(2)}) collective-permute-start(bf16[4,64,1024]{2,1,0:T(8,128)(2,1)S(1)} %bitcast.11), channel_id=1, source_target_pairs={{0,1},{1,0},{2,3},{3,2},{4,5},{5,4},{6,7},{7,6},{8,15},{9,10},{10,... | collective-permute-start | bytes 1572872 | tf_op jit(solution)/shard_map/ppermute | solution.py:234
  19.3 15.2 %collective-permute-start.1 = (bf16[4,64,1024]{2,1,0:T(8,128)(2,1)S(1)}, bf16[4,64,1024]{2,1,0:T(8,128)(2,1)S(1)}, u32[]{:S(2)}, u32[]{:S(2)}) collective-permute-start(bf16[4,64,1024]{2,1,0:T(8,128)(2,1)S(1)} %bitcast.12), channel_id=1, source_target_pairs={{0,8},{8,0},{16,24},{24,16},{32,40},{40,32},{48,56},{56,48},{64,72... | collective-permute-start | bytes 1572872 | tf_op jit(solution)/shard_map/ppermute | solution.py:230
  26.9 7.6 %collective-permute-start.2 = (bf16[4,64,1024]{2,1,0:T(8,128)(2,1)S(1)}, bf16[4,64,1024]{2,1,0:T(8,128)(2,1)S(1)}, u32[]{:S(2)}, u32[]{:S(2)}) collective-permute-start(bf16[4,64,1024]{2,1,0:T(8,128)(2,1)S(1)} %collective-permute-done.own_pair_ref), channel_id=1, source_target_pairs={{0,8},{8,0},{16,24},{24,16},{32,40},{40,32},{48,56},{56,48},{64,72... | collective-permute-start | bytes 1572872 | tf_op jit(solution)/shard_map/ppermute | solution.py:230
  29.0 5.5 %collective-permute-start.3 = (bf16[256,128]{1,0:T(8,128)(2,1)S(1)}, bf16[256,128]{1,0:T(8,128)(2,1)S(1)}, u32[]{:S(2)}, u32[]{:S(2)}) collective-permute-start(bf16[256,128]{1,0:T(8,128)(2,1)S(1)} %bitcast.15), channel_id=1, source_target_pairs={{0,8},{8,0},{16,24},{24,16},{32,40},{40,32},{48,56},{56,48},{64,72... | collective-permute-start | bytes 196616 | tf_op jit(solution)/shard_map/ppermute | solution.py:230
  31.3 2.9 %copy-start.2 = (s32[2,64]{1,0:T(2,128)S(1)}, s32[2,64]{1,0:T(2,128)}, u32[]{:S(2)}) copy-start(s32[2,64]{1,0:T(2,128)} %index_ref.3) | copy-start | bytes 1540

commit v10 on v9

v10 whole, which is shorter than its diff:
```python
import functools

import jax
import jax.numpy as jnp
from jax import lax
from jax.experimental import pallas as pl
from jax.experimental.pallas import tpu as pltpu
from jax.sharding import PartitionSpec as P

BF16, F32, I32 = jnp.bfloat16, jnp.float32, jnp.int32
MIB = 1024 * 1024


def iota(shape, dim):
    return lax.broadcasted_iota(I32, shape, dim)


def read_index(index_ref, owned):
    along = jnp.concatenate([index_ref[0:1, :], index_ref[1:2, :]], axis=1)
    rows = along.shape[1]
    shift = owned.bit_length() - 1
    assert owned == 1 << shift
    owner = along >> shift
    group = jnp.where(iota((1, rows), 1) >= rows // 2, 1, 0)
    wide = jnp.broadcast_to(owner * 2 + group, (rows, rows))
    line, column = iota((rows, rows), 0), iota((rows, rows), 1)
    same = jnp.sum(jnp.where(line == column, wide, 0).astype(F32), axis=1, keepdims=True)
    earlier = (wide.astype(F32) == same) & (line < column)
    place = jnp.sum(jnp.where(earlier, 1.0, 0.0), axis=0, keepdims=True).astype(I32)
    label = ((along & (owned - 1)) + 1).astype(F32)
    return (owner >> 1) * 4 + place * 2 + group, owner & 1, label


def over_lanes(values):
    share = jnp.full((128, 128), 1.0 / 64.0, BF16)
    return jnp.dot(values.astype(BF16), share, preferred_element_type=F32)


def partner(plane, core, planes):
    step = (1 - 2 * (plane % 2)) * (1 - 2 * core)
    return (plane + step + planes) % planes


def pack_kernel(owned, planes, index_ref, tokens_ref, out_ref, held, indices, sems):
    width = held.shape[2] // 2
    plane = lax.axis_index("tensor")
    core = lax.axis_index("dp") % 2
    copies = [pltpu.make_async_copy(index_ref, indices, sems.at[0])]
    for e, source in enumerate((plane, partner(plane, core, planes))):
        copies.append(
            pltpu.make_async_copy(
                tokens_ref.at[:, :, pl.ds(pl.multiple_of(source * width, width), width)],
                held.at[:, :, e * width : (e + 1) * width],
                sems.at[1 + e],
            )
        )
    for copy in copies:
        copy.start()
    copies[0].wait()
    target, owner_core, label = read_index(indices, owned)
    rows = target.shape[1]
    hit = iota((rows, rows), 0) == target
    labels = [
        jnp.sum(jnp.where(hit & (owner_core == c), label, 0.0), axis=1, keepdims=True)
        for c in range(2)
    ]
    labels = jnp.where(iota((rows, 128), 1) < 64, labels[0], labels[1]).astype(BF16)
    out_ref[:, :, 2 * width :] = labels.reshape(rows // 4, 4, 128)
    select = jnp.where(hit & (owner_core == plane % 2), 1.0, 0.0).astype(BF16)
    for copy in copies[1:]:
        copy.wait()
    tokens = held[...].reshape(rows, 2 * width)
    packed = jnp.dot(select, tokens, preferred_element_type=F32).astype(BF16)
    out_ref[:, :, : 2 * width] = packed.reshape(rows // 4, 4, 2 * width)


def shrink_kernel(
    received_ref, own_ref, first_ref, second_ref, partial_ref, label_ref, product_ref
):
    chips, per_chip, width = received_ref.shape
    width = (width - 128) // 2
    lines = chips * per_chip
    parity = lax.axis_index("tensor") % 2
    core = lax.axis_index("dp") % 2

    def multiply(weights):
        product = None
        for e in range(2):
            mine = lax.dot_general(
                received_ref[:, :, e * width : (e + 1) * width].reshape(lines, width),
                weights[e][...].reshape(256, width),
                (((1,), (1,)), ((), ())),
                preferred_element_type=F32,
            )
            product = mine if e == 0 else product + mine
        product_ref[...] = product

    @pl.when(core == parity)
    def _():
        multiply((own_ref, first_ref))

    @pl.when(core != parity)
    def _():
        multiply((first_ref, second_ref))

    label = received_ref[:, :, 2 * width :].reshape(lines, 128)
    upper = iota((lines, 128), 1) >> 6
    here = over_lanes(jnp.where(upper == parity, label.astype(F32), 0.0))
    upper = upper.astype(F32)
    total = jnp.where(here == upper + 1.0, product_ref[:, :128], 0.0)
    total = total + jnp.where(here == upper + 3.0, product_ref[:, 128:], 0.0)
    total = total + pltpu.roll(total, 64, 1)
    half = lines // 2
    packed = jnp.where(upper[:half] == 0.0, total[:half], total[half:]).astype(BF16)
    for peer in range(partial_ref.shape[0]):
        partial_ref[peer] = packed
    out_lines = label_ref.shape[0]
    line = iota((out_lines, lines), 0)
    source = (line >> 3) * 4 + (line & 3)
    take = jnp.where(iota((out_lines, lines), 1) == source, 1.0, 0.0).astype(BF16)
    label = jnp.dot(take, label, preferred_element_type=F32)
    line = iota((out_lines, 128), 0)
    label = over_lanes(jnp.where(iota((out_lines, 128), 1) >> 6 == (line >> 2) & 1, label, 0.0))
    other = (label > 0.0) & ((line >> 2) & 1 != core)
    label_ref[...] = jnp.where(other, label + 4.0, label).astype(BF16)


def expand_kernel(partial_ref, label_ref, up_own_ref, up_other_ref, out_ref):
    planes, half, _ = partial_ref.shape
    sums = []
    for p in range(2):
        total = partial_ref[p].astype(F32)
        for peer in range(p + 2, planes, 2):
            total = total + partial_ref[peer].astype(F32)
        sums.append(total.reshape(half // 8, 8, 128))
    first, second = sums
    low = iota(first.shape, 1) < 4
    by_chip = [
        jnp.where(low, first, pltpu.roll(second, 4, 1)),
        jnp.where(low, pltpu.roll(first, 4, 1), second),
    ]
    total = jnp.stack(by_chip, axis=1).reshape(half * 2, 128)
    turned = pltpu.roll(total, 64, 1)
    upper = iota(total.shape, 1) // 64
    lines = total.shape[0]
    for e in range(2):
        row = jnp.where(upper == e, total, turned)
        label = label_ref[e * lines : (e + 1) * lines].astype(F32)
        terms = None
        for up_ref, add in ((up_own_ref, 1.0), (up_other_ref, 5.0)):
            first = upper.astype(F32) + add
            left = jnp.where(label == first, row, 0.0)
            right = jnp.where(label == first + 2.0, row, 0.0)
            wide = jnp.concatenate([left, right], axis=1)
            high = wide.astype(BF16)
            for part in (high, (wide - high.astype(F32)).astype(BF16)):
                mine = jnp.dot(part, up_ref[...], preferred_element_type=F32)
                terms = mine if terms is None else terms + mine
        out_ref[e * lines : (e + 1) * lines] = terms.astype(BF16)


def place_kernel(owned, index_ref, out_ref):
    target, owner_core, _ = read_index(index_ref, owned)
    rows = target.shape[1]
    target = (target >> 2) * 8 + owner_core * 4 + (target & 3)
    line, column = iota((rows, rows), 0), iota((rows, rows), 1)
    target = jnp.broadcast_to(target, (rows, rows))
    target = jnp.sum(jnp.where(line == column, target, 0).astype(F32), axis=1, keepdims=True)
    out_ref[...] = jnp.where(iota(out_ref.shape, 1).astype(F32) == target, 1.0, 0.0).astype(BF16)


def call(kernel, shapes, ins, scratch=(), in_hbm=(), vmem=40):
    nbytes = sum(v.size * v.dtype.itemsize for v in ins)

    def spec(hbm):
        return pl.BlockSpec(memory_space=pltpu.HBM if hbm else pltpu.VMEM)

    return pl.pallas_call(
        kernel,
        out_shape=shapes,
        in_specs=[spec(i in in_hbm) for i in range(len(ins))],
        out_specs=[spec(False) for _ in shapes],
        scratch_shapes=scratch,
        compiler_params=pltpu.CompilerParams(vmem_limit_bytes=vmem * MIB),
        cost_estimate=pl.CostEstimate(flops=0, bytes_accessed=nbytes, transcendentals=0),
    )(*ins)


def on_device(tokens, value_matrix, down, up, index):
    groups, rows_local, features = tokens.shape
    owners = lax.axis_size("dp")
    planes = lax.axis_size("tensor")
    owned, width, rank = down.shape
    columns = up.shape[2]
    rows = groups * rows_local
    shape = jax.ShapeDtypeStruct

    cores = 2
    same_core = [list(range(core, owners, cores)) for core in range(cores)]

    (packed,) = call(
        functools.partial(pack_kernel, owned, planes),
        [shape((owners // cores, cores * groups, 2 * width + 128), BF16)],
        (index, tokens),
        [
            pltpu.VMEM((groups, rows_local, 2 * width), BF16),
            pltpu.VMEM(index.shape, I32),
            pltpu.SemaphoreType.DMA((3,)),
        ],
        in_hbm=(0, 1),
        vmem=62,
    )
    received = lax.all_to_all(
        packed, "dp", split_axis=0, concat_axis=0, tiled=True, axis_index_groups=same_core
    )

    down_own, up_own = down.transpose(0, 2, 1), up.reshape(owned * rank, columns)
    down_later, up_later, _ = lax.optimization_barrier((down_own, up_own, packed))
    first, second = [], []
    for i in range(owners):
        for t in range(planes):
            here, other = i * planes, (i ^ 1) * planes
            if i % cores == t % 2:
                first.append((here + t, other + t))
            else:
                first.append((here + t, here + (t - 1) % planes))
                second.append((here + t, other + (t + 1) % planes))
    down_first = lax.ppermute(down_later, ("dp", "tensor"), first)
    down_second = lax.ppermute(down_later, ("dp", "tensor"), second)
    up_other = lax.ppermute(up_later, "dp", [(i, i ^ 1) for i in range(owners)])

    base = jnp.dot(tokens.reshape(rows, features), value_matrix, preferred_element_type=F32)
    (place,) = call(
        functools.partial(place_kernel, owned), [shape((rows, owners * 4), BF16)], (index,)
    )
    received, down_first, down_second, up_other, base, place = lax.optimization_barrier(
        (received, down_first, down_second, up_other, base, place)
    )
    partial, label = call(
        shrink_kernel,
        [shape((planes, owners, 128), BF16), shape((owners * 4, 128), BF16)],
        (received, down_own, down_first, down_second),
        [pltpu.VMEM((rows, 256), F32)],
    )
    partials = lax.all_to_all(partial, "tensor", split_axis=0, concat_axis=0, tiled=True)
    (terms,) = call(
        expand_kernel,
        [shape((owners * 4, columns), BF16)],
        (partials, label, up_own, up_other),
    )
    arrived = lax.all_to_all(
        terms.reshape(owners // cores, 4 * cores, columns),
        "dp",
        split_axis=0,
        concat_axis=0,
        tiled=True,
        axis_index_groups=same_core,
    ).reshape(owners * 4, columns)
    out = (base + jnp.dot(place, arrived, preferred_element_type=F32)).astype(BF16)
    return out.reshape(groups, rows_local, columns)


def solution(mesh):
    in_specs = (
        P(None, "dp", None),
        P(None, "tensor"),
        P("dp", "tensor", None),
        P("dp", None, "tensor"),
        P(None, "dp"),
    )
    out_specs = P(None, "dp", "tensor")
    return jax.shard_map(
        on_device, mesh=mesh, in_specs=in_specs, out_specs=out_specs, check_vma=False
    )
```

time: 71.7 us -> 65.8 us (0.918)
  starting transfers between devices: 24.1 us -> 20.9 us
  blocking collectives: 34.7 us -> 31.8 us
    ppermute x4 -> x3, starting transfers between devices: 10.6 us -> 7.43 us  [the longest x1 4.82 us: on_device(): down_first = lax.ppermute(down_later, ('dp', 'tensor'), first)]
    all_to_all x1, waiting for transfers between devices: 0.01 us -> 2.95 us  [on_device(): lax.all_to_all(packed, 'dp', split_axis=0, concat_axis=0, tiled=True, axi...]
    all_to_all x1, blocking collectives: 18.5 us -> 15.8 us  [on_device(): lax.all_to_all(terms.reshape(owners // cores, 4 * cores, columns), 'dp',...]
    ppermute x4 -> x3, waiting for transfers between devices: 4.78 us -> 2.29 us  [the longest x1 2.29 us: on_device(): down_first = lax.ppermute(down_later, ('dp', 'tensor'), first)]
  transfers between devices with their start and end apart: 5 -> 4, of which waited for: 1 -> 2; matrix products, arithmetic and copies ran while one was open for 4% -> 4% of each run, Pallas kernels for 0% -> 0%
where the time goes in v10:
time: 65.8 us; the launch traced here: 65.5 us
  blocking collectives  31.8 us (48%)
  starting transfers between devices  20.9 us (32%)
  waiting for transfers between devices  5.24 us (8%)
  Pallas kernels  3.68 us (6%)
  matrix products  3.06 us (5%)
    all_to_all x1, blocking collectives, on_device(): lax.all_to_all(partial, 'tensor', split_axis=0, concat_axis=0, tiled=True)  16 us
    all_to_all x1, blocking collectives, on_device(): lax.all_to_all(terms.reshape(owners // cores, 4 * cores, columns), 'dp',...  15.8 us
    all_to_all x1, starting transfers between devices, on_device(): lax.all_to_all(packed, 'dp', split_axis=0, concat_axis=0, tiled=True, axi...  13.5 us
    ppermute x1, starting transfers between devices, on_device(): down_first = lax.ppermute(down_later, ('dp', 'tensor'), first)  4.82 us
    pallas_call x4, Pallas kernels, call(): pl.pallas_call(kernel, out_shape=shapes, in_specs=[spec(i in in_hbm) for...  3.68 us
    all_to_all x1, waiting for transfers between devices, on_device(): lax.all_to_all(packed, 'dp', split_axis=0, concat_axis=0, tiled=True, axi...  2.95 us
    dot_general x1, matrix products, on_device(): jnp.dot(tokens.reshape(rows, features), value_matrix, preferred_element_t...  2.92 us
    ppermute x1, waiting for transfers between devices, on_device(): down_first = lax.ppermute(down_later, ('dp', 'tensor'), first)  2.29 us
  transfers between devices with their start and end apart: 4, of which 2 were waited for; matrix products, arithmetic and copies ran while one was open for 4% of the time, Pallas kernels for 0%

profile of v10, /device:TPU:2, one launch (start us, length us, event | category | flops | bytes accessed | tf_op | source)
XLA Modules:
  0.0 65.5 jit_solution(12423572177586199811)
XLA Ops:
  0.0 0.0 copy-start.1
  0.0 0.0 copy-start
  0.0 2.2 %shard_map.55 = bf16[32,4,2176]{2,1,0:T(4,128)(2,1)} custom-call(s32[2,64]{1,0:T(2,128)} %index_ref.3, bf16[2,64,8192]{2,1,0:T(8,128)(2,1)} %tokens_ref.1), custom_call_target="tpu_custom_call" | custom-call | bytes 2097664 | tf_op jit(solution)/shard_map/pallas_call | solution.py:178
  2.2 13.5 %all-to-all-start = ((bf16[32,4,2176]{2,1,0:T(4,128)(2,1)}), bf16[32,4,2176]{2,1,0:T(4,128)(2,1)S(1)}, u32[]{:S(2)}, u32[]{:S(2)}) async-start(bf16[32,4,2176]{2,1,0:T(4,128)(2,1)} %shard_map.55), calls=%async_computation | async-start | bytes 1114112 | tf_op jit(solution)/shard_map/all_to_all | solution.py:213
  15.7 0.0 copy-done
  15.7 0.7 %collective-permute-start.1 = (bf16[4,64,1024]{2,1,0:T(8,128)(2,1)S(1)}, bf16[4,64,1024]{2,1,0:T(8,128)(2,1)S(1)}, u32[]{:S(2)}, u32[]{:S(2)}) collective-permute-start(bf16[4,64,1024]{2,1,0:T(8,128)(2,1)S(1)} %bitcast.11), channel_id=1, source_target_pairs={{1,10},{3,12},{5,14},{7,8},{8,1},{10,3},{12,5},{14,7},{17,26},{19,... | collective-permute-start | bytes 1572872 | tf_op jit(solution)/shard_map/ppermute | solution.py:229
  16.4 4.8 %collective-permute-start = (bf16[4,64,1024]{2,1,0:T(8,128)(2,1)S(1)}, bf16[4,64,1024]{2,1,0:T(8,128)(2,1)S(1)}, u32[]{:S(2)}, u32[]{:S(2)}) collective-permute-start(bf16[4,64,1024]{2,1,0:T(8,128)(2,1)S(1)} %bitcast.12), channel_id=1, source_target_pairs={{0,8},{1,0},{2,10},{3,2},{4,12},{5,4},{6,14},{7,6},{8,15},{9,1},{1... | collective-permute-start | bytes 1572872 | tf_op jit(solution)/shard_map/ppermute | solution.py:228
  21.3 0.0 copy-done.1
  21.3 1.9 %collective-permute-start.2 = (bf16[256,128]{1,0:T(8,128)(2,1)S(1)}, bf16[256,128]{1,0:T(8,128)(2,1)S(1)}, u32[]{:S(2)}, u32[]{:S(2)}) collective-permute-start(bf16[256,128]{1,0:T(8,128)(2,1)S(1)} %bitcast.15), channel_id=1, source_target_pairs={{0,8},{8,0},{16,24},{24,16},{32,40},{40,32},{48,56},{56,48},{64,72... | collective-permute-start | bytes 196616 | tf_op jit(solution)/shard_map/ppermute | solution.py:230
  23.2 0.0 copy-start.2
  23.2 2.9 %fusion.2 = f32[128,128]{1,0:T(8,128)S(1)} fusion(bf16[128,8192]{1,0:T(8,128)(2,1)} %bitcast.17, bf16[8192,128]{1,0:T(8,128)(2,1)} %param.6), kind=kOutput, calls=%fused_computation.3 | convolution fusion | flops 268435456 | bytes 4259840 | tf_op jit(solution)/shard_map/dot_general | solution.py:232
  26.1 0.0 copy-done.2
  26.2 0.3 shard_map.56
  26.4 0.0 collective-permute-done.2.up_other_ref
  26.5 0.0 collective-permute-done.1.second_ref
  26.5 2.3 %collective-permute-done.first_ref = bf16[4,64,1024]{2,1,0:T(8,128)(2,1)S(1)} collective-permute-done((bf16[4,64,1024]{2,1,0:T(8,128)(2,1)S(1)}, bf16[4,64,1024]{2,1,0:T(8,128)(2,1)S(1)}, u32[]{:S(2)}, u32[]{:S(2)}) %collective-permute-start) | collective-permute-done | bytes 524320 | tf_op jit(solution)/shard_map/ppermute | solution.py:228
  28.8 3.0 %all-to-all-done.received_ref = bf16[32,4,2176]{2,1,0:T(4,128)(2,1)S(1)} async-done(((bf16[32,4,2176]{2,1,0:T(4,128)(2,1)}), bf16[32,4,2176]{2,1,0:T(4,128)(2,1)S(1)}, u32[]{:S(2)}, u32[]{:S(2)}) %all-to-all-start) | async-done | bytes 557088 | tf_op jit(solution)/shard_map/all_to_all | solution.py:213
  31.7 0.8 %shard_map.57 = (bf16[8,64,128]{2,1,0:T(8,128)(2,1)S(1)}, bf16[256,128]{1,0:T(8,128)(2,1)S(1)}) custom-call(bf16[32,4,2176]{2,1,0:T(4,128)(2,1)S(1)} %all-to-all-done.received_ref, bf16[4,64,1024]{2,1,0:T(8,128)(2,1)S(1)} %bitcast.13, bf16[4,64,1024]{2,1,0:T(8,128)(2,1)S(1)} %collective-permute-done.first_ref, ...), custom_call_target="tpu_custom_call" | custom-call | bytes 2129920 | tf_op jit(solution)/shard_map/pallas_call | solution.py:178
  32.5 16.0 %all_to_all.15.partial_ref = bf16[8,64,128]{2,1,0:T(8,128)(2,1)S(1)} all-to-all(bf16[8,64,128]{2,1,0:T(8,128)(2,1)S(1)} %get-tuple-element.22), channel_id=1, replica_groups=mesh['dp'=64,'tensor'=8] {'tensor'}, dimensions={0} | all-to-all | bytes 262144 | tf_op jit(solution)/shard_map/all_to_all | solution.py:245
  48.5 0.4 shard_map.58
  48.8 15.8 %all_to_all.16 = bf16[32,8,128]{2,1,0:T(8,128)(2,1)S(1)} all-to-all(bf16[32,8,128]{2,1,0:T(8,128)(2,1)S(1)} %bitcast.14), channel_id=1, replica_groups={{0,16,32,48,64,80,96,112,128,144,160,176,192,208,224,240,256,272,288,30..., dimensions={0} | all-to-all | bytes 131072 | tf_op jit(solution)/shard_map/all_to_all | solution.py:251
  64.7 0.1 fusion
  64.8 0.6 add_convert_fusion
Async XLA Ops:
  0.0 21.3 %copy-start.1 = (bf16[4,64,128]{2,1,0:T(8,128)(2,1)S(1)}, bf16[4,64,128]{2,1,0:T(8,128)(2,1)}, u32[]{:S(2)}) copy-start(bf16[4,64,128]{2,1,0:T(8,128)(2,1)} %param.8) | copy-start | bytes 196612
  0.0 15.7 %copy-start = (bf16[4,1024,64]{1,2,0:T(8,128)(2,1)S(1)}, bf16[4,1024,64]{1,2,0:T(8,128)(2,1)}, u32[]{:S(2)}) copy-start(bf16[4,1024,64]{1,2,0:T(8,128)(2,1)} %param.7) | copy-start | bytes 1572868
  2.2 29.5 %all-to-all-start = ((bf16[32,4,2176]{2,1,0:T(4,128)(2,1)}), bf16[32,4,2176]{2,1,0:T(4,128)(2,1)S(1)}, u32[]{:S(2)}, u32[]{:S(2)}) async-start(bf16[32,4,2176]{2,1,0:T(4,128)(2,1)} %shard_map.55), calls=%async_computation | async-start | bytes 1114112 | tf_op jit(solution)/shard_map/all_to_all | solution.py:213
  15.7 10.7 %collective-permute-start.1 = (bf16[4,64,1024]{2,1,0:T(8,128)(2,1)S(1)}, bf16[4,64,1024]{2,1,0:T(8,128)(2,1)S(1)}, u32[]{:S(2)}, u32[]{:S(2)}) collective-permute-start(bf16[4,64,1024]{2,1,0:T(8,128)(2,1)S(1)} %bitcast.11), channel_id=1, source_target_pairs={{1,10},{3,12},{5,14},{7,8},{8,1},{10,3},{12,5},{14,7},{17,26},{19,... | collective-permute-start | bytes 1572872 | tf_op jit(solution)/shard_map/ppermute | solution.py:229
  16.4 12.3 %collective-permute-start = (bf16[4,64,1024]{2,1,0:T(8,128)(2,1)S(1)}, bf16[4,64,1024]{2,1,0:T(8,128)(2,1)S(1)}, u32[]{:S(2)}, u32[]{:S(2)}) collective-permute-start(bf16[4,64,1024]{2,1,0:T(8,128)(2,1)S(1)} %bitcast.12), channel_id=1, source_target_pairs={{0,8},{1,0},{2,10},{3,2},{4,12},{5,4},{6,14},{7,6},{8,15},{9,1},{1... | collective-permute-start | bytes 1572872 | tf_op jit(solution)/shard_map/ppermute | solution.py:228
  21.3 5.2 %collective-permute-start.2 = (bf16[256,128]{1,0:T(8,128)(2,1)S(1)}, bf16[256,128]{1,0:T(8,128)(2,1)S(1)}, u32[]{:S(2)}, u32[]{:S(2)}) collective-permute-start(bf16[256,128]{1,0:T(8,128)(2,1)S(1)} %bitcast.15), channel_id=1, source_target_pairs={{0,8},{8,0},{16,24},{24,16},{32,40},{40,32},{48,56},{56,48},{64,72... | collective-permute-start | bytes 196616 | tf_op jit(solution)/shard_map/ppermute | solution.py:230
  23.2 2.9 %copy-start.2 = (s32[2,64]{1,0:T(2,128)S(1)}, s32[2,64]{1,0:T(2,128)}, u32[]{:S(2)}) copy-start(s32[2,64]{1,0:T(2,128)} %index_ref.3) | copy-start | bytes 1540

commit v11 on v10

--- a/solution.py
+++ b/solution.py
@@ -28,11 +28,11 @@
     earlier = (wide.astype(F32) == same) & (line < column)
     place = jnp.sum(jnp.where(earlier, 1.0, 0.0), axis=0, keepdims=True).astype(I32)
     label = ((along & (owned - 1)) + 1).astype(F32)
-    return (owner >> 1) * 4 + place * 2 + group, owner & 1, label
+    return (owner >> 1) * 2 + group, place, owner & 1, label
 
 
 def over_lanes(values):
-    share = jnp.full((128, 128), 1.0 / 64.0, BF16)
+    share = jnp.full((128, 128), 1.0 / 32.0, BF16)
     return jnp.dot(values.astype(BF16), share, preferred_element_type=F32)
 
 
@@ -57,112 +57,124 @@
     for copy in copies:
         copy.start()
     copies[0].wait()
-    target, owner_core, label = read_index(indices, owned)
-    rows = target.shape[1]
-    hit = iota((rows, rows), 0) == target
-    labels = [
-        jnp.sum(jnp.where(hit & (owner_core == c), label, 0.0), axis=1, keepdims=True)
-        for c in range(2)
-    ]
-    labels = jnp.where(iota((rows, 128), 1) < 64, labels[0], labels[1]).astype(BF16)
-    out_ref[:, :, 2 * width :] = labels.reshape(rows // 4, 4, 128)
+    key, place, owner_core, label = read_index(indices, owned)
+    rows, lines = key.shape[1], out_ref.shape[0] * out_ref.shape[1]
+    hit = iota((2 * lines, rows), 0) == place * lines + key
+    labels = None
+    field = iota((lines, 128), 1) >> 5
+    for c in range(2):
+        found = jnp.where(hit & (owner_core == c), label, 0.0)
+        found = jnp.sum(found, axis=1, keepdims=True)
+        for p in range(2):
+            mine = found[p * lines : (p + 1) * lines]
+            labels = mine if labels is None else jnp.where(field == 2 * c + p, mine, labels)
+    labels = jnp.broadcast_to(labels, (lines, 128)).astype(BF16)
+    out_ref[:, :, 4 * width :] = labels.reshape(lines // 2, 2, 128)
     select = jnp.where(hit & (owner_core == plane % 2), 1.0, 0.0).astype(BF16)
     for copy in copies[1:]:
         copy.wait()
     tokens = held[...].reshape(rows, 2 * width)
     packed = jnp.dot(select, tokens, preferred_element_type=F32).astype(BF16)
-    out_ref[:, :, : 2 * width] = packed.reshape(rows // 4, 4, 2 * width)
-
-
-def shrink_kernel(
-    received_ref, own_ref, first_ref, second_ref, partial_ref, label_ref, product_ref
-):
-    chips, per_chip, width = received_ref.shape
-    width = (width - 128) // 2
-    lines = chips * per_chip
+    for p in range(2):
+        out_ref[:, :, 2 * p * width : 2 * (p + 1) * width] = packed[
+            p * lines : (p + 1) * lines
+        ].reshape(lines // 2, 2, 2 * width)
+
+
+def shrink(received_ref, weights, partial_ref, label_ref):
+    chips, groups, width = received_ref.shape
+    width = (width - 128) // 4
+    lines = chips * groups
     parity = lax.axis_index("tensor") % 2
     core = lax.axis_index("dp") % 2
 
-    def multiply(weights):
-        product = None
-        for e in range(2):
-            mine = lax.dot_general(
-                received_ref[:, :, e * width : (e + 1) * width].reshape(lines, width),
-                weights[e][...].reshape(256, width),
-                (((1,), (1,)), ((), ())),
-                preferred_element_type=F32,
-            )
-            product = mine if e == 0 else product + mine
-        product_ref[...] = product
-
-    @pl.when(core == parity)
-    def _():
-        multiply((own_ref, first_ref))
-
-    @pl.when(core != parity)
-    def _():
-        multiply((first_ref, second_ref))
-
-    label = received_ref[:, :, 2 * width :].reshape(lines, 128)
-    upper = iota((lines, 128), 1) >> 6
-    here = over_lanes(jnp.where(upper == parity, label.astype(F32), 0.0))
-    upper = upper.astype(F32)
-    total = jnp.where(here == upper + 1.0, product_ref[:, :128], 0.0)
-    total = total + jnp.where(here == upper + 3.0, product_ref[:, 128:], 0.0)
+    def part(at):
+        return received_ref[:, :, at * width : (at + 1) * width].reshape(lines, width)
+
+    product = None
+    for e in range(2):
+        mine = lax.dot_general(
+            jnp.concatenate([part(e), part(2 + e)], axis=0),
+            weights[e][...].reshape(256, width),
+            (((1,), (1,)), ((), ())),
+            preferred_element_type=F32,
+        )
+        product = mine if e == 0 else product + mine
+    label = received_ref[:, :, 4 * width :].reshape(lines, 128)
+    field = iota((lines, 128), 1) >> 5
+    here = [
+        jnp.where(field == 2 * parity + p, label.astype(F32), 0.0) for p in range(2)
+    ]
+    here = over_lanes(jnp.concatenate(here, axis=0))
+    upper = (iota((2 * lines, 128), 1) >> 6).astype(F32)
+    total = jnp.where(here == upper + 1.0, product[:, :128], 0.0)
+    total = total + jnp.where(here == upper + 3.0, product[:, 128:], 0.0)
     total = total + pltpu.roll(total, 64, 1)
-    half = lines // 2
-    packed = jnp.where(upper[:half] == 0.0, total[:half], total[half:]).astype(BF16)
+    packed = jnp.where(upper[:lines] == 0.0, total[:lines], total[lines:]).astype(BF16)
     for peer in range(partial_ref.shape[0]):
         partial_ref[peer] = packed
     out_lines = label_ref.shape[0]
     line = iota((out_lines, lines), 0)
-    source = (line >> 3) * 4 + (line & 3)
+    source = (line >> 3) * 2 + (line & 1)
     take = jnp.where(iota((out_lines, lines), 1) == source, 1.0, 0.0).astype(BF16)
     label = jnp.dot(take, label, preferred_element_type=F32)
     line = iota((out_lines, 128), 0)
-    label = over_lanes(jnp.where(iota((out_lines, 128), 1) >> 6 == (line >> 2) & 1, label, 0.0))
+    label = over_lanes(jnp.where(iota((out_lines, 128), 1) >> 5 == (line >> 1) & 3, label, 0.0))
     other = (label > 0.0) & ((line >> 2) & 1 != core)
     label_ref[...] = jnp.where(other, label + 4.0, label).astype(BF16)
 
 
+def shrink_kernel(received_ref, own_ref, first_ref, second_ref, partial_ref, label_ref):
+    at_home = lax.axis_index("tensor") % 2 == lax.axis_index("dp") % 2
+
+    @pl.when(at_home)
+    def _():
+        shrink(received_ref, (own_ref, first_ref), partial_ref, label_ref)
+
+    @pl.when(jnp.logical_not(at_home))
+    def _():
+        shrink(received_ref, (first_ref, second_ref), partial_ref, label_ref)
+
+
 def expand_kernel(partial_ref, label_ref, up_own_ref, up_other_ref, out_ref):
-    planes, half, _ = partial_ref.shape
+    planes, lines, _ = partial_ref.shape
     sums = []
-    for p in range(2):
-        total = partial_ref[p].astype(F32)
-        for peer in range(p + 2, planes, 2):
+    for q in range(2):
+        total = partial_ref[q].astype(F32)
+        for peer in range(q + 2, planes, 2):
             total = total + partial_ref[peer].astype(F32)
-        sums.append(total.reshape(half // 8, 8, 128))
-    first, second = sums
-    low = iota(first.shape, 1) < 4
-    by_chip = [
-        jnp.where(low, first, pltpu.roll(second, 4, 1)),
-        jnp.where(low, pltpu.roll(first, 4, 1), second),
-    ]
-    total = jnp.stack(by_chip, axis=1).reshape(half * 2, 128)
-    turned = pltpu.roll(total, 64, 1)
-    upper = iota(total.shape, 1) // 64
-    lines = total.shape[0]
-    for e in range(2):
-        row = jnp.where(upper == e, total, turned)
-        label = label_ref[e * lines : (e + 1) * lines].astype(F32)
-        terms = None
-        for up_ref, add in ((up_own_ref, 1.0), (up_other_ref, 5.0)):
-            first = upper.astype(F32) + add
-            left = jnp.where(label == first, row, 0.0)
-            right = jnp.where(label == first + 2.0, row, 0.0)
-            wide = jnp.concatenate([left, right], axis=1)
-            high = wide.astype(BF16)
-            for part in (high, (wide - high.astype(F32)).astype(BF16)):
-                mine = jnp.dot(part, up_ref[...], preferred_element_type=F32)
-                terms = mine if terms is None else terms + mine
-        out_ref[e * lines : (e + 1) * lines] = terms.astype(BF16)
+        sums.append(total.reshape(lines // 8, 8, 128))
+    spot = iota(sums[0].shape, 1) >> 1
+    by_chip = []
+    for chip in range(4):
+        out = None
+        for field in range(4):
+            by = 2 * (field - chip) % 8
+            piece = pltpu.roll(sums[field // 2], by, 1) if by else sums[field // 2]
+            out = piece if field == 0 else jnp.where(spot == field, piece, out)
+        by_chip.append(out)
+    total = jnp.stack(by_chip, axis=1).reshape(lines * 4, 128)
+    upper = iota(total.shape, 1) >> 6
+    place = (iota(total.shape, 0) >> 1) & 1
+    row = jnp.where(upper == place, total, pltpu.roll(total, 64, 1))
+    label = label_ref[...].astype(F32)
+    terms = None
+    for up_ref, add in ((up_own_ref, 1.0), (up_other_ref, 5.0)):
+        at = upper.astype(F32) + add
+        left = jnp.where(label == at, row, 0.0)
+        right = jnp.where(label == at + 2.0, row, 0.0)
+        wide = jnp.concatenate([left, right], axis=1)
+        high = wide.astype(BF16)
+        for part in (high, (wide - high.astype(F32)).astype(BF16)):
+            mine = jnp.dot(part, up_ref[...], preferred_element_type=F32)
+            terms = mine if terms is None else terms + mine
+    out_ref[...] = terms.astype(BF16)
 
 
 def place_kernel(owned, index_ref, out_ref):
-    target, owner_core, _ = read_index(index_ref, owned)
-    rows = target.shape[1]
-    target = (target >> 2) * 8 + owner_core * 4 + (target & 3)
+    key, place, owner_core, _ = read_index(index_ref, owned)
+    rows = key.shape[1]
+    target = (key >> 1) * 8 + owner_core * 4 + place * 2 + (key & 1)
     line, column = iota((rows, rows), 0), iota((rows, rows), 1)
     target = jnp.broadcast_to(target, (rows, rows))
     target = jnp.sum(jnp.where(line == column, target, 0).astype(F32), axis=1, keepdims=True)
@@ -200,7 +212,7 @@
 
     (packed,) = call(
         functools.partial(pack_kernel, owned, planes),
-        [shape((owners // cores, cores * groups, 2 * width + 128), BF16)],
+        [shape((owners // cores, groups, 4 * width + 128), BF16)],
         (index, tokens),
         [
             pltpu.VMEM((groups, rows_local, 2 * width), BF16),
@@ -240,7 +252,6 @@
         shrink_kernel,
         [shape((planes, owners, 128), BF16), shape((owners * 4, 128), BF16)],
         (received, down_own, down_first, down_second),
-        [pltpu.VMEM((rows, 256), F32)],
     )
     partials = lax.all_to_all(partial, "tensor", split_axis=0, concat_axis=0, tiled=True)
     (terms,) = call(

time: 65.8 us -> 65.3 us (level)
  no operation moved by 1% of the time
where the time goes in v11:
time: 65.3 us; the launch traced here: 65 us
  blocking collectives  31.7 us (49%)
  starting transfers between devices  20.9 us (32%)
  waiting for transfers between devices  5 us (8%)
  Pallas kernels  3.5 us (5%)
  matrix products  3.06 us (5%)
    all_to_all x1, blocking collectives, on_device(): lax.all_to_all(partial, 'tensor', split_axis=0, concat_axis=0, tiled=True)  16 us
    all_to_all x1, blocking collectives, on_device(): lax.all_to_all(terms.reshape(owners // cores, 4 * cores, columns), 'dp',...  15.7 us
    all_to_all x1, starting transfers between devices, on_device(): lax.all_to_all(packed, 'dp', split_axis=0, concat_axis=0, tiled=True, axi...  13.5 us
    ppermute x1, starting transfers between devices, on_device(): down_first = lax.ppermute(down_later, ('dp', 'tensor'), first)  4.82 us
    pallas_call x4, Pallas kernels, call(): pl.pallas_call(kernel, out_shape=shapes, in_specs=[spec(i in in_hbm) for...  3.5 us
    dot_general x1, matrix products, on_device(): jnp.dot(tokens.reshape(rows, features), value_matrix, preferred_element_t...  2.92 us
    all_to_all x1, waiting for transfers between devices, on_device(): lax.all_to_all(packed, 'dp', split_axis=0, concat_axis=0, tiled=True, axi...  2.7 us
    ppermute x1, waiting for transfers between devices, on_device(): down_first = lax.ppermute(down_later, ('dp', 'tensor'), first)  2.29 us
  transfers between devices with their start and end apart: 4, of which 2 were waited for; matrix products, arithmetic and copies ran while one was open for 4% of the time, Pallas kernels for 0%

profile of v11, /device:TPU:2, one launch (start us, length us, event | category | flops | bytes accessed | tf_op | source)
XLA Modules:
  0.0 65.0 jit_solution(12445539218198691456)
XLA Ops:
  0.0 0.0 copy-start.1
  0.0 0.0 copy-start
  0.0 2.2 %shard_map.55 = bf16[32,2,4224]{2,1,0:T(2,128)(2,1)} custom-call(s32[2,64]{1,0:T(2,128)} %index_ref.3, bf16[2,64,8192]{2,1,0:T(8,128)(2,1)} %tokens_ref.1), custom_call_target="tpu_custom_call" | custom-call | bytes 2097664 | tf_op jit(solution)/shard_map/pallas_call | solution.py:190
  2.2 13.5 %all-to-all-start = ((bf16[32,2,4224]{2,1,0:T(2,128)(2,1)}), bf16[32,2,4224]{2,1,0:T(2,128)(2,1)S(1)}, u32[]{:S(2)}, u32[]{:S(2)}) async-start(bf16[32,2,4224]{2,1,0:T(2,128)(2,1)} %shard_map.55), calls=%async_computation | async-start | bytes 1081344 | tf_op jit(solution)/shard_map/all_to_all | solution.py:225
  15.7 0.0 copy-done
  15.7 0.7 %collective-permute-start.1 = (bf16[4,64,1024]{2,1,0:T(8,128)(2,1)S(1)}, bf16[4,64,1024]{2,1,0:T(8,128)(2,1)S(1)}, u32[]{:S(2)}, u32[]{:S(2)}) collective-permute-start(bf16[4,64,1024]{2,1,0:T(8,128)(2,1)S(1)} %bitcast.11), channel_id=1, source_target_pairs={{1,10},{3,12},{5,14},{7,8},{8,1},{10,3},{12,5},{14,7},{17,26},{19,... | collective-permute-start | bytes 1572872 | tf_op jit(solution)/shard_map/ppermute | solution.py:241
  16.4 4.8 %collective-permute-start = (bf16[4,64,1024]{2,1,0:T(8,128)(2,1)S(1)}, bf16[4,64,1024]{2,1,0:T(8,128)(2,1)S(1)}, u32[]{:S(2)}, u32[]{:S(2)}) collective-permute-start(bf16[4,64,1024]{2,1,0:T(8,128)(2,1)S(1)} %bitcast.12), channel_id=1, source_target_pairs={{0,8},{1,0},{2,10},{3,2},{4,12},{5,4},{6,14},{7,6},{8,15},{9,1},{1... | collective-permute-start | bytes 1572872 | tf_op jit(solution)/shard_map/ppermute | solution.py:240
  21.3 0.0 copy-done.1
  21.3 1.9 %collective-permute-start.2 = (bf16[256,128]{1,0:T(8,128)(2,1)S(1)}, bf16[256,128]{1,0:T(8,128)(2,1)S(1)}, u32[]{:S(2)}, u32[]{:S(2)}) collective-permute-start(bf16[256,128]{1,0:T(8,128)(2,1)S(1)} %bitcast.15), channel_id=1, source_target_pairs={{0,8},{8,0},{16,24},{24,16},{32,40},{40,32},{48,56},{56,48},{64,72... | collective-permute-start | bytes 196616 | tf_op jit(solution)/shard_map/ppermute | solution.py:242
  23.2 0.0 copy-start.2
  23.2 2.9 %fusion.2 = f32[128,128]{1,0:T(8,128)S(1)} fusion(bf16[128,8192]{1,0:T(8,128)(2,1)} %bitcast.17, bf16[8192,128]{1,0:T(8,128)(2,1)} %param.6), kind=kOutput, calls=%fused_computation.3 | convolution fusion | flops 268435456 | bytes 4259840 | tf_op jit(solution)/shard_map/dot_general | solution.py:244
  26.1 0.0 copy-done.2
  26.2 0.3 shard_map.56
  26.4 0.0 collective-permute-done.2.up_other_ref
  26.5 0.0 collective-permute-done.1.second_ref
  26.5 2.3 %collective-permute-done.first_ref = bf16[4,64,1024]{2,1,0:T(8,128)(2,1)S(1)} collective-permute-done((bf16[4,64,1024]{2,1,0:T(8,128)(2,1)S(1)}, bf16[4,64,1024]{2,1,0:T(8,128)(2,1)S(1)}, u32[]{:S(2)}, u32[]{:S(2)}) %collective-permute-start) | collective-permute-done | bytes 524320 | tf_op jit(solution)/shard_map/ppermute | solution.py:240
  28.8 2.7 %all-to-all-done.received_ref = bf16[32,2,4224]{2,1,0:T(2,128)(2,1)S(1)} async-done(((bf16[32,2,4224]{2,1,0:T(2,128)(2,1)}), bf16[32,2,4224]{2,1,0:T(2,128)(2,1)S(1)}, u32[]{:S(2)}, u32[]{:S(2)}) %all-to-all-start) | async-done | bytes 540704 | tf_op jit(solution)/shard_map/all_to_all | solution.py:225
  31.5 0.6 shard_map.57
  32.1 16.0 %all_to_all.15.partial_ref = bf16[8,64,128]{2,1,0:T(8,128)(2,1)S(1)} all-to-all(bf16[8,64,128]{2,1,0:T(8,128)(2,1)S(1)} %get-tuple-element.22), channel_id=1, replica_groups=mesh['dp'=64,'tensor'=8] {'tensor'}, dimensions={0} | all-to-all | bytes 262144 | tf_op jit(solution)/shard_map/all_to_all | solution.py:256
  48.1 0.4 shard_map.58
  48.4 15.7 %all_to_all.16 = bf16[32,8,128]{2,1,0:T(8,128)(2,1)S(1)} all-to-all(bf16[32,8,128]{2,1,0:T(8,128)(2,1)S(1)} %bitcast.14), channel_id=1, replica_groups={{0,16,32,48,64,80,96,112,128,144,160,176,192,208,224,240,256,272,288,30..., dimensions={0} | all-to-all | bytes 131072 | tf_op jit(solution)/shard_map/all_to_all | solution.py:262
  64.2 0.1 fusion
  64.3 0.6 add_convert_fusion
Async XLA Ops:
  0.0 21.3 %copy-start.1 = (bf16[4,64,128]{2,1,0:T(8,128)(2,1)S(1)}, bf16[4,64,128]{2,1,0:T(8,128)(2,1)}, u32[]{:S(2)}) copy-start(bf16[4,64,128]{2,1,0:T(8,128)(2,1)} %param.8) | copy-start | bytes 196612
  0.0 15.7 %copy-start = (bf16[4,1024,64]{1,2,0:T(8,128)(2,1)S(1)}, bf16[4,1024,64]{1,2,0:T(8,128)(2,1)}, u32[]{:S(2)}) copy-start(bf16[4,1024,64]{1,2,0:T(8,128)(2,1)} %param.7) | copy-start | bytes 1572868
  2.2 29.2 %all-to-all-start = ((bf16[32,2,4224]{2,1,0:T(2,128)(2,1)}), bf16[32,2,4224]{2,1,0:T(2,128)(2,1)S(1)}, u32[]{:S(2)}, u32[]{:S(2)}) async-start(bf16[32,2,4224]{2,1,0:T(2,128)(2,1)} %shard_map.55), calls=%async_computation | async-start | bytes 1081344 | tf_op jit(solution)/shard_map/all_to_all | solution.py:225
  15.7 10.7 %collective-permute-start.1 = (bf16[4,64,1024]{2,1,0:T(8,128)(2,1)S(1)}, bf16[4,64,1024]{2,1,0:T(8,128)(2,1)S(1)}, u32[]{:S(2)}, u32[]{:S(2)}) collective-permute-start(bf16[4,64,1024]{2,1,0:T(8,128)(2,1)S(1)} %bitcast.11), channel_id=1, source_target_pairs={{1,10},{3,12},{5,14},{7,8},{8,1},{10,3},{12,5},{14,7},{17,26},{19,... | collective-permute-start | bytes 1572872 | tf_op jit(solution)/shard_map/ppermute | solution.py:241
  16.4 12.3 %collective-permute-start = (bf16[4,64,1024]{2,1,0:T(8,128)(2,1)S(1)}, bf16[4,64,1024]{2,1,0:T(8,128)(2,1)S(1)}, u32[]{:S(2)}, u32[]{:S(2)}) collective-permute-start(bf16[4,64,1024]{2,1,0:T(8,128)(2,1)S(1)} %bitcast.12), channel_id=1, source_target_pairs={{0,8},{1,0},{2,10},{3,2},{4,12},{5,4},{6,14},{7,6},{8,15},{9,1},{1... | collective-permute-start | bytes 1572872 | tf_op jit(solution)/shard_map/ppermute | solution.py:240
  21.3 5.2 %collective-permute-start.2 = (bf16[256,128]{1,0:T(8,128)(2,1)S(1)}, bf16[256,128]{1,0:T(8,128)(2,1)S(1)}, u32[]{:S(2)}, u32[]{:S(2)}) collective-permute-start(bf16[256,128]{1,0:T(8,128)(2,1)S(1)} %bitcast.15), channel_id=1, source_target_pairs={{0,8},{8,0},{16,24},{24,16},{32,40},{40,32},{48,56},{56,48},{64,72... | collective-permute-start | bytes 196616 | tf_op jit(solution)/shard_map/ppermute | solution.py:242
  23.2 2.9 %copy-start.2 = (s32[2,64]{1,0:T(2,128)S(1)}, s32[2,64]{1,0:T(2,128)}, u32[]{:S(2)}) copy-start(s32[2,64]{1,0:T(2,128)} %index_ref.3) | copy-start | bytes 1540

commit v12 on v11

--- a/solution.py
+++ b/solution.py
@@ -74,11 +74,14 @@
     for copy in copies[1:]:
         copy.wait()
     tokens = held[...].reshape(rows, 2 * width)
-    packed = jnp.dot(select, tokens, preferred_element_type=F32).astype(BF16)
-    for p in range(2):
-        out_ref[:, :, 2 * p * width : 2 * (p + 1) * width] = packed[
-            p * lines : (p + 1) * lines
-        ].reshape(lines // 2, 2, 2 * width)
+    for e in range(2):
+        part = tokens[:, e * width : (e + 1) * width]
+        packed = jnp.dot(select, part, preferred_element_type=F32).astype(BF16)
+        for p in range(2):
+            at = (2 * p + e) * width
+            out_ref[:, :, at : at + width] = packed[p * lines : (p + 1) * lines].reshape(
+                lines // 2, 2, width
+            )
 
 
 def shrink(received_ref, weights, partial_ref, label_ref):
@@ -95,8 +98,8 @@
     for e in range(2):
         mine = lax.dot_general(
             jnp.concatenate([part(e), part(2 + e)], axis=0),
-            weights[e][...].reshape(256, width),
-            (((1,), (1,)), ((), ())),
+            weights[e][...],
+            (((1,), (0,)), ((), ())),
             preferred_element_type=F32,
         )
         product = mine if e == 0 else product + mine
@@ -226,8 +229,9 @@
         packed, "dp", split_axis=0, concat_axis=0, tiled=True, axis_index_groups=same_core
     )
 
-    down_own, up_own = down.transpose(0, 2, 1), up.reshape(owned * rank, columns)
-    down_later, up_later, _ = lax.optimization_barrier((down_own, up_own, packed))
+    up_own = up.reshape(owned * rank, columns)
+    down_later, up_later, _ = lax.optimization_barrier((down, up_own, packed))
+    down_own = down_later.transpose(1, 0, 2).reshape(width, owned * rank)
     first, second = [], []
     for i in range(owners):
         for t in range(planes):
@@ -237,8 +241,8 @@
             else:
                 first.append((here + t, here + (t - 1) % planes))
                 second.append((here + t, other + (t + 1) % planes))
-    down_first = lax.ppermute(down_later, ("dp", "tensor"), first)
-    down_second = lax.ppermute(down_later, ("dp", "tensor"), second)
+    down_first = lax.ppermute(down_own, ("dp", "tensor"), first)
+    down_second = lax.ppermute(down_own, ("dp", "tensor"), second)
     up_other = lax.ppermute(up_later, "dp", [(i, i ^ 1) for i in range(owners)])
 
     base = jnp.dot(tokens.reshape(rows, features), value_matrix, preferred_element_type=F32)

time: 65.3 us -> 65.1 us (level)
  transfers between devices with their start and end apart: 4 -> 4, of which waited for: 2 -> 2; matrix products, arithmetic and copies ran while one was open for 4% -> 5% of each run, Pallas kernels for 0% -> 0%
where the time goes in v12:
time: 65.1 us; the launch traced here: 64.8 us
  blocking collectives  31.7 us (49%)
  starting transfers between devices  20.9 us (32%)
  waiting for transfers between devices  4.79 us (7%)
  Pallas kernels  3.33 us (5%)
  matrix products  3.06 us (5%)
    all_to_all x1, blocking collectives, on_device(): lax.all_to_all(partial, 'tensor', split_axis=0, concat_axis=0, tiled=True)  16 us
    all_to_all x1, blocking collectives, on_device(): lax.all_to_all(terms.reshape(owners // cores, 4 * cores, columns), 'dp',...  15.7 us
    all_to_all x1, starting transfers between devices, on_device(): lax.all_to_all(packed, 'dp', split_axis=0, concat_axis=0, tiled=True, axi...  13.5 us
    ppermute x1, starting transfers between devices, on_device(): down_first = lax.ppermute(down_own, ('dp', 'tensor'), first)  4.82 us
    pallas_call x4, Pallas kernels, call(): pl.pallas_call(kernel, out_shape=shapes, in_specs=[spec(i in in_hbm) for...  3.33 us
    dot_general x1, matrix products, on_device(): jnp.dot(tokens.reshape(rows, features), value_matrix, preferred_element_t...  2.92 us
    all_to_all x1, waiting for transfers between devices, on_device(): lax.all_to_all(packed, 'dp', split_axis=0, concat_axis=0, tiled=True, axi...  2.49 us
    ppermute x1, waiting for transfers between devices, on_device(): down_first = lax.ppermute(down_own, ('dp', 'tensor'), first)  2.29 us
  transfers between devices with their start and end apart: 4, of which 2 were waited for; matrix products, arithmetic and copies ran while one was open for 5% of the time, Pallas kernels for 0%

profile of v12, /device:TPU:2, one launch (start us, length us, event | category | flops | bytes accessed | tf_op | source)
XLA Modules:
  0.0 64.8 jit_solution(15178310798312838903)
XLA Ops:
  0.0 0.0 copy-start
  0.0 0.0 copy-start.2
  0.0 2.2 %shard_map.55 = bf16[32,2,4224]{2,1,0:T(2,128)(2,1)} custom-call(s32[2,64]{1,0:T(2,128)} %index_ref.3, bf16[2,64,8192]{2,1,0:T(8,128)(2,1)} %tokens_ref.1), custom_call_target="tpu_custom_call" | custom-call | bytes 2097664 | tf_op jit(solution)/shard_map/pallas_call | solution.py:193
  2.2 13.5 %all-to-all-start = ((bf16[32,2,4224]{2,1,0:T(2,128)(2,1)}), bf16[32,2,4224]{2,1,0:T(2,128)(2,1)S(1)}, u32[]{:S(2)}, u32[]{:S(2)}) async-start(bf16[32,2,4224]{2,1,0:T(2,128)(2,1)} %shard_map.55), calls=%async_computation | async-start | bytes 1081344 | tf_op jit(solution)/shard_map/all_to_all | solution.py:228
  15.7 0.0 copy-done.2
  15.7 0.2 copy.7.own_ref
  15.9 0.7 %collective-permute-start.1 = (bf16[1024,256]{1,0:T(8,128)(2,1)S(1)}, bf16[1024,256]{1,0:T(8,128)(2,1)S(1)}, u32[]{:S(2)}, u32[]{:S(2)}) collective-permute-start(bf16[1024,256]{1,0:T(8,128)(2,1)S(1)} %copy.7.own_ref), channel_id=1, source_target_pairs={{1,10},{3,12},{5,14},{7,8},{8,1},{10,3},{12,5},{14,7},{17,26},{19,... | collective-permute-start | bytes 1572872 | tf_op jit(solution)/shard_map/ppermute | solution.py:245
  16.6 4.8 %collective-permute-start = (bf16[1024,256]{1,0:T(8,128)(2,1)S(1)}, bf16[1024,256]{1,0:T(8,128)(2,1)S(1)}, u32[]{:S(2)}, u32[]{:S(2)}) collective-permute-start(bf16[1024,256]{1,0:T(8,128)(2,1)S(1)} %copy.7.own_ref), channel_id=1, source_target_pairs={{0,8},{1,0},{2,10},{3,2},{4,12},{5,4},{6,14},{7,6},{8,15},{9,1},{1... | collective-permute-start | bytes 1572872 | tf_op jit(solution)/shard_map/ppermute | solution.py:244
  21.5 0.0 copy-done
  21.5 1.9 %collective-permute-start.2 = (bf16[256,128]{1,0:T(8,128)(2,1)S(1)}, bf16[256,128]{1,0:T(8,128)(2,1)S(1)}, u32[]{:S(2)}, u32[]{:S(2)}) collective-permute-start(bf16[256,128]{1,0:T(8,128)(2,1)S(1)} %bitcast.14), channel_id=1, source_target_pairs={{0,8},{8,0},{16,24},{24,16},{32,40},{40,32},{48,56},{56,48},{64,72... | collective-permute-start | bytes 196616 | tf_op jit(solution)/shard_map/ppermute | solution.py:246
  23.4 0.0 copy-start.1
  23.4 2.9 %fusion.2 = f32[128,128]{1,0:T(8,128)S(1)} fusion(bf16[128,8192]{1,0:T(8,128)(2,1)} %bitcast.16, bf16[8192,128]{1,0:T(8,128)(2,1)} %param.6), kind=kOutput, calls=%fused_computation.3 | convolution fusion | flops 268435456 | bytes 4259840 | tf_op jit(solution)/shard_map/dot_general | solution.py:248
  26.4 0.0 copy-done.1
  26.4 0.3 shard_map.56
  26.6 0.0 collective-permute-done.2.up_other_ref
  26.7 0.0 collective-permute-done.1.second_ref
  26.7 2.3 %collective-permute-done.first_ref = bf16[1024,256]{1,0:T(8,128)(2,1)S(1)} collective-permute-done((bf16[1024,256]{1,0:T(8,128)(2,1)S(1)}, bf16[1024,256]{1,0:T(8,128)(2,1)S(1)}, u32[]{:S(2)}, u32[]{:S(2)}) %collective-permute-start) | collective-permute-done | bytes 524320 | tf_op jit(solution)/shard_map/ppermute | solution.py:244
  29.0 2.5 %all-to-all-done.received_ref = bf16[32,2,4224]{2,1,0:T(2,128)(2,1)S(1)} async-done(((bf16[32,2,4224]{2,1,0:T(2,128)(2,1)}), bf16[32,2,4224]{2,1,0:T(2,128)(2,1)S(1)}, u32[]{:S(2)}, u32[]{:S(2)}) %all-to-all-start) | async-done | bytes 540704 | tf_op jit(solution)/shard_map/all_to_all | solution.py:228
  31.5 0.5 shard_map.57
  31.9 16.0 %all_to_all.15.partial_ref = bf16[8,64,128]{2,1,0:T(8,128)(2,1)S(1)} all-to-all(bf16[8,64,128]{2,1,0:T(8,128)(2,1)S(1)} %get-tuple-element.22), channel_id=1, replica_groups=mesh['dp'=64,'tensor'=8] {'tensor'}, dimensions={0} | all-to-all | bytes 262144 | tf_op jit(solution)/shard_map/all_to_all | solution.py:260
  47.9 0.4 shard_map.58
  48.3 15.7 %all_to_all.16 = bf16[32,8,128]{2,1,0:T(8,128)(2,1)S(1)} all-to-all(bf16[32,8,128]{2,1,0:T(8,128)(2,1)S(1)} %bitcast.13), channel_id=1, replica_groups={{0,16,32,48,64,80,96,112,128,144,160,176,192,208,224,240,256,272,288,30..., dimensions={0} | all-to-all | bytes 131072 | tf_op jit(solution)/shard_map/all_to_all | solution.py:266
  64.0 0.1 fusion
  64.2 0.6 add_convert_fusion
Async XLA Ops:
  0.0 21.5 %copy-start = (bf16[4,64,128]{2,1,0:T(8,128)(2,1)S(1)}, bf16[4,64,128]{2,1,0:T(8,128)(2,1)}, u32[]{:S(2)}) copy-start(bf16[4,64,128]{2,1,0:T(8,128)(2,1)} %param.8) | copy-start | bytes 196612
  0.0 15.7 %copy-start.2 = (bf16[4,1024,64]{1,2,0:T(8,128)(2,1)S(1)}, bf16[4,1024,64]{1,2,0:T(8,128)(2,1)}, u32[]{:S(2)}) copy-start(bf16[4,1024,64]{1,2,0:T(8,128)(2,1)} %param.7) | copy-start | bytes 1572868
  2.2 29.2 %all-to-all-start = ((bf16[32,2,4224]{2,1,0:T(2,128)(2,1)}), bf16[32,2,4224]{2,1,0:T(2,128)(2,1)S(1)}, u32[]{:S(2)}, u32[]{:S(2)}) async-start(bf16[32,2,4224]{2,1,0:T(2,128)(2,1)} %shard_map.55), calls=%async_computation | async-start | bytes 1081344 | tf_op jit(solution)/shard_map/all_to_all | solution.py:228
  15.9 10.7 %collective-permute-start.1 = (bf16[1024,256]{1,0:T(8,128)(2,1)S(1)}, bf16[1024,256]{1,0:T(8,128)(2,1)S(1)}, u32[]{:S(2)}, u32[]{:S(2)}) collective-permute-start(bf16[1024,256]{1,0:T(8,128)(2,1)S(1)} %copy.7.own_ref), channel_id=1, source_target_pairs={{1,10},{3,12},{5,14},{7,8},{8,1},{10,3},{12,5},{14,7},{17,26},{19,... | collective-permute-start | bytes 1572872 | tf_op jit(solution)/shard_map/ppermute | solution.py:245
  16.6 12.3 %collective-permute-start = (bf16[1024,256]{1,0:T(8,128)(2,1)S(1)}, bf16[1024,256]{1,0:T(8,128)(2,1)S(1)}, u32[]{:S(2)}, u32[]{:S(2)}) collective-permute-start(bf16[1024,256]{1,0:T(8,128)(2,1)S(1)} %copy.7.own_ref), channel_id=1, source_target_pairs={{0,8},{1,0},{2,10},{3,2},{4,12},{5,4},{6,14},{7,6},{8,15},{9,1},{1... | collective-permute-start | bytes 1572872 | tf_op jit(solution)/shard_map/ppermute | solution.py:244
  21.5 5.2 %collective-permute-start.2 = (bf16[256,128]{1,0:T(8,128)(2,1)S(1)}, bf16[256,128]{1,0:T(8,128)(2,1)S(1)}, u32[]{:S(2)}, u32[]{:S(2)}) collective-permute-start(bf16[256,128]{1,0:T(8,128)(2,1)S(1)} %bitcast.14), channel_id=1, source_target_pairs={{0,8},{8,0},{16,24},{24,16},{32,40},{40,32},{48,56},{56,48},{64,72... | collective-permute-start | bytes 196616 | tf_op jit(solution)/shard_map/ppermute | solution.py:246
  23.4 2.9 %copy-start.1 = (s32[2,64]{1,0:T(2,128)S(1)}, s32[2,64]{1,0:T(2,128)}, u32[]{:S(2)}) copy-start(s32[2,64]{1,0:T(2,128)} %index_ref.3) | copy-start | bytes 1540

commit v13 on v12

--- a/solution.py
+++ b/solution.py
@@ -108,7 +108,9 @@
     here = [
         jnp.where(field == 2 * parity + p, label.astype(F32), 0.0) for p in range(2)
     ]
-    here = over_lanes(jnp.concatenate(here, axis=0))
+    here = jnp.concatenate(here, axis=0)
+    here = here + pltpu.roll(here, 64, 1)
+    here = here + pltpu.roll(here, 32, 1)
     upper = (iota((2 * lines, 128), 1) >> 6).astype(F32)
     total = jnp.where(here == upper + 1.0, product[:, :128], 0.0)
     total = total + jnp.where(here == upper + 3.0, product[:, 128:], 0.0)
@@ -166,11 +168,9 @@
         at = upper.astype(F32) + add
         left = jnp.where(label == at, row, 0.0)
         right = jnp.where(label == at + 2.0, row, 0.0)
-        wide = jnp.concatenate([left, right], axis=1)
-        high = wide.astype(BF16)
-        for part in (high, (wide - high.astype(F32)).astype(BF16)):
-            mine = jnp.dot(part, up_ref[...], preferred_element_type=F32)
-            terms = mine if terms is None else terms + mine
+        wide = jnp.concatenate([left, right], axis=1).astype(BF16)
+        mine = jnp.dot(wide, up_ref[...], preferred_element_type=F32)
+        terms = mine if terms is None else terms + mine
     out_ref[...] = terms.astype(BF16)
 
 

time: 65.1 us -> 65 us (level)
  no operation moved by 1% of the time
where the time goes in v13:
time: 65 us; the launch traced here: 64.7 us
  blocking collectives  31.7 us (49%)
  starting transfers between devices  20.9 us (32%)
  waiting for transfers between devices  4.79 us (7%)
  Pallas kernels  3.23 us (5%)
  matrix products  3.06 us (5%)
    all_to_all x1, blocking collectives, on_device(): lax.all_to_all(partial, 'tensor', split_axis=0, concat_axis=0, tiled=True)  16 us
    all_to_all x1, blocking collectives, on_device(): lax.all_to_all(terms.reshape(owners // cores, 4 * cores, columns), 'dp',...  15.7 us
    all_to_all x1, starting transfers between devices, on_device(): lax.all_to_all(packed, 'dp', split_axis=0, concat_axis=0, tiled=True, axi...  13.5 us
    ppermute x1, starting transfers between devices, on_device(): down_first = lax.ppermute(down_own, ('dp', 'tensor'), first)  4.82 us
    pallas_call x4, Pallas kernels, call(): pl.pallas_call(kernel, out_shape=shapes, in_specs=[spec(i in in_hbm) for...  3.23 us
    dot_general x1, matrix products, on_device(): jnp.dot(tokens.reshape(rows, features), value_matrix, preferred_element_t...  2.92 us
    all_to_all x1, waiting for transfers between devices, on_device(): lax.all_to_all(packed, 'dp', split_axis=0, concat_axis=0, tiled=True, axi...  2.49 us
    ppermute x1, waiting for transfers between devices, on_device(): down_first = lax.ppermute(down_own, ('dp', 'tensor'), first)  2.29 us
  transfers between devices with their start and end apart: 4, of which 2 were waited for; matrix products, arithmetic and copies ran while one was open for 5% of the time, Pallas kernels for 0%

profile of v13, /device:TPU:2, one launch (start us, length us, event | category | flops | bytes accessed | tf_op | source)
XLA Modules:
  0.0 64.7 jit_solution(5086121761887296815)
XLA Ops:
  0.0 0.0 copy-start
  0.0 0.0 copy-start.2
  0.0 2.2 %shard_map.55 = bf16[32,2,4224]{2,1,0:T(2,128)(2,1)} custom-call(s32[2,64]{1,0:T(2,128)} %index_ref.3, bf16[2,64,8192]{2,1,0:T(8,128)(2,1)} %tokens_ref.1), custom_call_target="tpu_custom_call" | custom-call | bytes 2097664 | tf_op jit(solution)/shard_map/pallas_call | solution.py:193
  2.2 13.5 %all-to-all-start = ((bf16[32,2,4224]{2,1,0:T(2,128)(2,1)}), bf16[32,2,4224]{2,1,0:T(2,128)(2,1)S(1)}, u32[]{:S(2)}, u32[]{:S(2)}) async-start(bf16[32,2,4224]{2,1,0:T(2,128)(2,1)} %shard_map.55), calls=%async_computation | async-start | bytes 1081344 | tf_op jit(solution)/shard_map/all_to_all | solution.py:228
  15.7 0.0 copy-done.2
  15.7 0.2 copy.7.own_ref
  15.9 0.7 %collective-permute-start.1 = (bf16[1024,256]{1,0:T(8,128)(2,1)S(1)}, bf16[1024,256]{1,0:T(8,128)(2,1)S(1)}, u32[]{:S(2)}, u32[]{:S(2)}) collective-permute-start(bf16[1024,256]{1,0:T(8,128)(2,1)S(1)} %copy.7.own_ref), channel_id=1, source_target_pairs={{1,10},{3,12},{5,14},{7,8},{8,1},{10,3},{12,5},{14,7},{17,26},{19,... | collective-permute-start | bytes 1572872 | tf_op jit(solution)/shard_map/ppermute | solution.py:245
  16.6 4.8 %collective-permute-start = (bf16[1024,256]{1,0:T(8,128)(2,1)S(1)}, bf16[1024,256]{1,0:T(8,128)(2,1)S(1)}, u32[]{:S(2)}, u32[]{:S(2)}) collective-permute-start(bf16[1024,256]{1,0:T(8,128)(2,1)S(1)} %copy.7.own_ref), channel_id=1, source_target_pairs={{0,8},{1,0},{2,10},{3,2},{4,12},{5,4},{6,14},{7,6},{8,15},{9,1},{1... | collective-permute-start | bytes 1572872 | tf_op jit(solution)/shard_map/ppermute | solution.py:244
  21.5 0.0 copy-done
  21.5 1.9 %collective-permute-start.2 = (bf16[256,128]{1,0:T(8,128)(2,1)S(1)}, bf16[256,128]{1,0:T(8,128)(2,1)S(1)}, u32[]{:S(2)}, u32[]{:S(2)}) collective-permute-start(bf16[256,128]{1,0:T(8,128)(2,1)S(1)} %bitcast.14), channel_id=1, source_target_pairs={{0,8},{8,0},{16,24},{24,16},{32,40},{40,32},{48,56},{56,48},{64,72... | collective-permute-start | bytes 196616 | tf_op jit(solution)/shard_map/ppermute | solution.py:246
  23.4 0.0 copy-start.1
  23.4 2.9 %fusion.2 = f32[128,128]{1,0:T(8,128)S(1)} fusion(bf16[128,8192]{1,0:T(8,128)(2,1)} %bitcast.16, bf16[8192,128]{1,0:T(8,128)(2,1)} %param.6), kind=kOutput, calls=%fused_computation.3 | convolution fusion | flops 268435456 | bytes 4259840 | tf_op jit(solution)/shard_map/dot_general | solution.py:248
  26.4 0.0 copy-done.1
  26.4 0.3 shard_map.56
  26.6 0.0 collective-permute-done.2.up_other_ref
  26.7 0.0 collective-permute-done.1.second_ref
  26.7 2.3 %collective-permute-done.first_ref = bf16[1024,256]{1,0:T(8,128)(2,1)S(1)} collective-permute-done((bf16[1024,256]{1,0:T(8,128)(2,1)S(1)}, bf16[1024,256]{1,0:T(8,128)(2,1)S(1)}, u32[]{:S(2)}, u32[]{:S(2)}) %collective-permute-start) | collective-permute-done | bytes 524320 | tf_op jit(solution)/shard_map/ppermute | solution.py:244
  29.0 2.5 %all-to-all-done.received_ref = bf16[32,2,4224]{2,1,0:T(2,128)(2,1)S(1)} async-done(((bf16[32,2,4224]{2,1,0:T(2,128)(2,1)}), bf16[32,2,4224]{2,1,0:T(2,128)(2,1)S(1)}, u32[]{:S(2)}, u32[]{:S(2)}) %all-to-all-start) | async-done | bytes 540704 | tf_op jit(solution)/shard_map/all_to_all | solution.py:228
  31.5 0.4 shard_map.57
  31.9 16.0 %all_to_all.15.partial_ref = bf16[8,64,128]{2,1,0:T(8,128)(2,1)S(1)} all-to-all(bf16[8,64,128]{2,1,0:T(8,128)(2,1)S(1)} %get-tuple-element.22), channel_id=1, replica_groups=mesh['dp'=64,'tensor'=8] {'tensor'}, dimensions={0} | all-to-all | bytes 262144 | tf_op jit(solution)/shard_map/all_to_all | solution.py:260
  47.9 0.3 shard_map.58
  48.2 15.7 %all_to_all.16 = bf16[32,8,128]{2,1,0:T(8,128)(2,1)S(1)} all-to-all(bf16[32,8,128]{2,1,0:T(8,128)(2,1)S(1)} %bitcast.13), channel_id=1, replica_groups={{0,16,32,48,64,80,96,112,128,144,160,176,192,208,224,240,256,272,288,30..., dimensions={0} | all-to-all | bytes 131072 | tf_op jit(solution)/shard_map/all_to_all | solution.py:266
  63.9 0.1 fusion
  64.1 0.6 add_convert_fusion
Async XLA Ops:
  0.0 21.5 %copy-start = (bf16[4,64,128]{2,1,0:T(8,128)(2,1)S(1)}, bf16[4,64,128]{2,1,0:T(8,128)(2,1)}, u32[]{:S(2)}) copy-start(bf16[4,64,128]{2,1,0:T(8,128)(2,1)} %param.8) | copy-start | bytes 196612
  0.0 15.7 %copy-start.2 = (bf16[4,1024,64]{1,2,0:T(8,128)(2,1)S(1)}, bf16[4,1024,64]{1,2,0:T(8,128)(2,1)}, u32[]{:S(2)}) copy-start(bf16[4,1024,64]{1,2,0:T(8,128)(2,1)} %param.7) | copy-start | bytes 1572868
  2.2 29.2 %all-to-all-start = ((bf16[32,2,4224]{2,1,0:T(2,128)(2,1)}), bf16[32,2,4224]{2,1,0:T(2,128)(2,1)S(1)}, u32[]{:S(2)}, u32[]{:S(2)}) async-start(bf16[32,2,4224]{2,1,0:T(2,128)(2,1)} %shard_map.55), calls=%async_computation | async-start | bytes 1081344 | tf_op jit(solution)/shard_map/all_to_all | solution.py:228
  15.9 10.7 %collective-permute-start.1 = (bf16[1024,256]{1,0:T(8,128)(2,1)S(1)}, bf16[1024,256]{1,0:T(8,128)(2,1)S(1)}, u32[]{:S(2)}, u32[]{:S(2)}) collective-permute-start(bf16[1024,256]{1,0:T(8,128)(2,1)S(1)} %copy.7.own_ref), channel_id=1, source_target_pairs={{1,10},{3,12},{5,14},{7,8},{8,1},{10,3},{12,5},{14,7},{17,26},{19,... | collective-permute-start | bytes 1572872 | tf_op jit(solution)/shard_map/ppermute | solution.py:245
  16.6 12.3 %collective-permute-start = (bf16[1024,256]{1,0:T(8,128)(2,1)S(1)}, bf16[1024,256]{1,0:T(8,128)(2,1)S(1)}, u32[]{:S(2)}, u32[]{:S(2)}) collective-permute-start(bf16[1024,256]{1,0:T(8,128)(2,1)S(1)} %copy.7.own_ref), channel_id=1, source_target_pairs={{0,8},{1,0},{2,10},{3,2},{4,12},{5,4},{6,14},{7,6},{8,15},{9,1},{1... | collective-permute-start | bytes 1572872 | tf_op jit(solution)/shard_map/ppermute | solution.py:244
  21.5 5.2 %collective-permute-start.2 = (bf16[256,128]{1,0:T(8,128)(2,1)S(1)}, bf16[256,128]{1,0:T(8,128)(2,1)S(1)}, u32[]{:S(2)}, u32[]{:S(2)}) collective-permute-start(bf16[256,128]{1,0:T(8,128)(2,1)S(1)} %bitcast.14), channel_id=1, source_target_pairs={{0,8},{8,0},{16,24},{24,16},{32,40},{40,32},{48,56},{56,48},{64,72... | collective-permute-start | bytes 196616 | tf_op jit(solution)/shard_map/ppermute | solution.py:246
  23.4 2.9 %copy-start.1 = (s32[2,64]{1,0:T(2,128)S(1)}, s32[2,64]{1,0:T(2,128)}, u32[]{:S(2)}) copy-start(s32[2,64]{1,0:T(2,128)} %index_ref.3) | copy-start | bytes 1540

commit v14 on v13

--- a/solution.py
+++ b/solution.py
@@ -55,7 +55,7 @@
             )
         )
     for copy in copies:
-        copy.start()
+        copy.start(priority=1)
     copies[0].wait()
     key, place, owner_core, label = read_index(indices, owned)
     rows, lines = key.shape[1], out_ref.shape[0] * out_ref.shape[1]

time: 65 us -> 65 us (level)
  no operation moved by 1% of the time
where the time goes in v14:
time: 65 us; the launch traced here: 64.7 us
  blocking collectives  31.7 us (49%)
  starting transfers between devices  20.9 us (32%)
  waiting for transfers between devices  4.79 us (7%)
  Pallas kernels  3.23 us (5%)
  matrix products  3.06 us (5%)
    all_to_all x1, blocking collectives, on_device(): lax.all_to_all(partial, 'tensor', split_axis=0, concat_axis=0, tiled=True)  16 us
    all_to_all x1, blocking collectives, on_device(): lax.all_to_all(terms.reshape(owners // cores, 4 * cores, columns), 'dp',...  15.7 us
    all_to_all x1, starting transfers between devices, on_device(): lax.all_to_all(packed, 'dp', split_axis=0, concat_axis=0, tiled=True, axi...  13.5 us
    ppermute x1, starting transfers between devices, on_device(): down_first = lax.ppermute(down_own, ('dp', 'tensor'), first)  4.82 us
    pallas_call x4, Pallas kernels, call(): pl.pallas_call(kernel, out_shape=shapes, in_specs=[spec(i in in_hbm) for...  3.23 us
    dot_general x1, matrix products, on_device(): jnp.dot(tokens.reshape(rows, features), value_matrix, preferred_element_t...  2.92 us
    all_to_all x1, waiting for transfers between devices, on_device(): lax.all_to_all(packed, 'dp', split_axis=0, concat_axis=0, tiled=True, axi...  2.49 us
    ppermute x1, waiting for transfers between devices, on_device(): down_first = lax.ppermute(down_own, ('dp', 'tensor'), first)  2.29 us
  transfers between devices with their start and end apart: 4, of which 2 were waited for; matrix products, arithmetic and copies ran while one was open for 5% of the time, Pallas kernels for 0%

profile of v14, /device:TPU:2, one launch (start us, length us, event | category | flops | bytes accessed | tf_op | source)
XLA Modules:
  0.0 64.7 jit_solution(12600733848710768539)
XLA Ops:
  0.0 0.0 copy-start
  0.0 0.0 copy-start.2
  0.0 2.2 %shard_map.55 = bf16[32,2,4224]{2,1,0:T(2,128)(2,1)} custom-call(s32[2,64]{1,0:T(2,128)} %index_ref.3, bf16[2,64,8192]{2,1,0:T(8,128)(2,1)} %tokens_ref.1), custom_call_target="tpu_custom_call" | custom-call | bytes 2097664 | tf_op jit(solution)/shard_map/pallas_call | solution.py:193
  2.2 13.5 %all-to-all-start = ((bf16[32,2,4224]{2,1,0:T(2,128)(2,1)}), bf16[32,2,4224]{2,1,0:T(2,128)(2,1)S(1)}, u32[]{:S(2)}, u32[]{:S(2)}) async-start(bf16[32,2,4224]{2,1,0:T(2,128)(2,1)} %shard_map.55), calls=%async_computation | async-start | bytes 1081344 | tf_op jit(solution)/shard_map/all_to_all | solution.py:228
  15.7 0.0 copy-done.2
  15.7 0.2 copy.7.own_ref
  15.9 0.7 %collective-permute-start.1 = (bf16[1024,256]{1,0:T(8,128)(2,1)S(1)}, bf16[1024,256]{1,0:T(8,128)(2,1)S(1)}, u32[]{:S(2)}, u32[]{:S(2)}) collective-permute-start(bf16[1024,256]{1,0:T(8,128)(2,1)S(1)} %copy.7.own_ref), channel_id=1, source_target_pairs={{1,10},{3,12},{5,14},{7,8},{8,1},{10,3},{12,5},{14,7},{17,26},{19,... | collective-permute-start | bytes 1572872 | tf_op jit(solution)/shard_map/ppermute | solution.py:245
  16.6 4.8 %collective-permute-start = (bf16[1024,256]{1,0:T(8,128)(2,1)S(1)}, bf16[1024,256]{1,0:T(8,128)(2,1)S(1)}, u32[]{:S(2)}, u32[]{:S(2)}) collective-permute-start(bf16[1024,256]{1,0:T(8,128)(2,1)S(1)} %copy.7.own_ref), channel_id=1, source_target_pairs={{0,8},{1,0},{2,10},{3,2},{4,12},{5,4},{6,14},{7,6},{8,15},{9,1},{1... | collective-permute-start | bytes 1572872 | tf_op jit(solution)/shard_map/ppermute | solution.py:244
  21.5 0.0 copy-done
  21.5 1.9 %collective-permute-start.2 = (bf16[256,128]{1,0:T(8,128)(2,1)S(1)}, bf16[256,128]{1,0:T(8,128)(2,1)S(1)}, u32[]{:S(2)}, u32[]{:S(2)}) collective-permute-start(bf16[256,128]{1,0:T(8,128)(2,1)S(1)} %bitcast.14), channel_id=1, source_target_pairs={{0,8},{8,0},{16,24},{24,16},{32,40},{40,32},{48,56},{56,48},{64,72... | collective-permute-start | bytes 196616 | tf_op jit(solution)/shard_map/ppermute | solution.py:246
  23.4 0.0 copy-start.1
  23.4 2.9 %fusion.2 = f32[128,128]{1,0:T(8,128)S(1)} fusion(bf16[128,8192]{1,0:T(8,128)(2,1)} %bitcast.16, bf16[8192,128]{1,0:T(8,128)(2,1)} %param.6), kind=kOutput, calls=%fused_computation.3 | convolution fusion | flops 268435456 | bytes 4259840 | tf_op jit(solution)/shard_map/dot_general | solution.py:248
  26.4 0.0 copy-done.1
  26.4 0.3 shard_map.56
  26.6 0.0 collective-permute-done.2.up_other_ref
  26.7 0.0 collective-permute-done.1.second_ref
  26.7 2.3 %collective-permute-done.first_ref = bf16[1024,256]{1,0:T(8,128)(2,1)S(1)} collective-permute-done((bf16[1024,256]{1,0:T(8,128)(2,1)S(1)}, bf16[1024,256]{1,0:T(8,128)(2,1)S(1)}, u32[]{:S(2)}, u32[]{:S(2)}) %collective-permute-start) | collective-permute-done | bytes 524320 | tf_op jit(solution)/shard_map/ppermute | solution.py:244
  29.0 2.5 %all-to-all-done.received_ref = bf16[32,2,4224]{2,1,0:T(2,128)(2,1)S(1)} async-done(((bf16[32,2,4224]{2,1,0:T(2,128)(2,1)}), bf16[32,2,4224]{2,1,0:T(2,128)(2,1)S(1)}, u32[]{:S(2)}, u32[]{:S(2)}) %all-to-all-start) | async-done | bytes 540704 | tf_op jit(solution)/shard_map/all_to_all | solution.py:228
  31.5 0.4 shard_map.57
  31.9 16.0 %all_to_all.15.partial_ref = bf16[8,64,128]{2,1,0:T(8,128)(2,1)S(1)} all-to-all(bf16[8,64,128]{2,1,0:T(8,128)(2,1)S(1)} %get-tuple-element.22), channel_id=1, replica_groups=mesh['dp'=64,'tensor'=8] {'tensor'}, dimensions={0} | all-to-all | bytes 262144 | tf_op jit(solution)/shard_map/all_to_all | solution.py:260
  47.9 0.3 shard_map.58
  48.2 15.7 %all_to_all.16 = bf16[32,8,128]{2,1,0:T(8,128)(2,1)S(1)} all-to-all(bf16[32,8,128]{2,1,0:T(8,128)(2,1)S(1)} %bitcast.13), channel_id=1, replica_groups={{0,16,32,48,64,80,96,112,128,144,160,176,192,208,224,240,256,272,288,30..., dimensions={0} | all-to-all | bytes 131072 | tf_op jit(solution)/shard_map/all_to_all | solution.py:266
  63.9 0.1 fusion
  64.1 0.6 add_convert_fusion
Async XLA Ops:
  0.0 21.5 %copy-start = (bf16[4,64,128]{2,1,0:T(8,128)(2,1)S(1)}, bf16[4,64,128]{2,1,0:T(8,128)(2,1)}, u32[]{:S(2)}) copy-start(bf16[4,64,128]{2,1,0:T(8,128)(2,1)} %param.8) | copy-start | bytes 196612
  0.0 15.7 %copy-start.2 = (bf16[4,1024,64]{1,2,0:T(8,128)(2,1)S(1)}, bf16[4,1024,64]{1,2,0:T(8,128)(2,1)}, u32[]{:S(2)}) copy-start(bf16[4,1024,64]{1,2,0:T(8,128)(2,1)} %param.7) | copy-start | bytes 1572868
  2.2 29.2 %all-to-all-start = ((bf16[32,2,4224]{2,1,0:T(2,128)(2,1)}), bf16[32,2,4224]{2,1,0:T(2,128)(2,1)S(1)}, u32[]{:S(2)}, u32[]{:S(2)}) async-start(bf16[32,2,4224]{2,1,0:T(2,128)(2,1)} %shard_map.55), calls=%async_computation | async-start | bytes 1081344 | tf_op jit(solution)/shard_map/all_to_all | solution.py:228
  15.9 10.7 %collective-permute-start.1 = (bf16[1024,256]{1,0:T(8,128)(2,1)S(1)}, bf16[1024,256]{1,0:T(8,128)(2,1)S(1)}, u32[]{:S(2)}, u32[]{:S(2)}) collective-permute-start(bf16[1024,256]{1,0:T(8,128)(2,1)S(1)} %copy.7.own_ref), channel_id=1, source_target_pairs={{1,10},{3,12},{5,14},{7,8},{8,1},{10,3},{12,5},{14,7},{17,26},{19,... | collective-permute-start | bytes 1572872 | tf_op jit(solution)/shard_map/ppermute | solution.py:245
  16.6 12.3 %collective-permute-start = (bf16[1024,256]{1,0:T(8,128)(2,1)S(1)}, bf16[1024,256]{1,0:T(8,128)(2,1)S(1)}, u32[]{:S(2)}, u32[]{:S(2)}) collective-permute-start(bf16[1024,256]{1,0:T(8,128)(2,1)S(1)} %copy.7.own_ref), channel_id=1, source_target_pairs={{0,8},{1,0},{2,10},{3,2},{4,12},{5,4},{6,14},{7,6},{8,15},{9,1},{1... | collective-permute-start | bytes 1572872 | tf_op jit(solution)/shard_map/ppermute | solution.py:244
  21.5 5.2 %collective-permute-start.2 = (bf16[256,128]{1,0:T(8,128)(2,1)S(1)}, bf16[256,128]{1,0:T(8,128)(2,1)S(1)}, u32[]{:S(2)}, u32[]{:S(2)}) collective-permute-start(bf16[256,128]{1,0:T(8,128)(2,1)S(1)} %bitcast.14), channel_id=1, source_target_pairs={{0,8},{8,0},{16,24},{24,16},{32,40},{40,32},{48,56},{56,48},{64,72... | collective-permute-start | bytes 196616 | tf_op jit(solution)/shard_map/ppermute | solution.py:246
  23.4 2.9 %copy-start.1 = (s32[2,64]{1,0:T(2,128)S(1)}, s32[2,64]{1,0:T(2,128)}, u32[]{:S(2)}) copy-start(s32[2,64]{1,0:T(2,128)} %index_ref.3) | copy-start | bytes 1540

commit v15 on v14

--- a/solution.py
+++ b/solution.py
@@ -184,6 +184,11 @@
     out_ref[...] = jnp.where(iota(out_ref.shape, 1).astype(F32) == target, 1.0, 0.0).astype(BF16)
 
 
+def add_kernel(place_ref, arrived_ref, base_ref, out_ref):
+    terms = jnp.dot(place_ref[...], arrived_ref[...], preferred_element_type=F32)
+    out_ref[...] = (base_ref[...] + terms).astype(BF16)
+
+
 def call(kernel, shapes, ins, scratch=(), in_hbm=(), vmem=40):
     nbytes = sum(v.size * v.dtype.itemsize for v in ins)
 
@@ -271,7 +276,7 @@
         tiled=True,
         axis_index_groups=same_core,
     ).reshape(owners * 4, columns)
-    out = (base + jnp.dot(place, arrived, preferred_element_type=F32)).astype(BF16)
+    (out,) = call(add_kernel, [shape((rows, columns), BF16)], (place, arrived, base))
     return out.reshape(groups, rows_local, columns)
 
 

time: 65 us -> 65 us (level)
  Pallas kernels: 3.23 us -> 4 us
    pallas_call x4 -> x5, Pallas kernels: 3.23 us -> 4 us  [call(): pl.pallas_call(kernel, out_shape=shapes, in_specs=[spec(i in in_hbm) for...]
where the time goes in v15:
time: 65 us; the launch traced here: 64.7 us
  blocking collectives  31.7 us (49%)
  starting transfers between devices  20.9 us (32%)
  waiting for transfers between devices  4.79 us (7%)
  Pallas kernels  4 us (6%)
  matrix products  2.92 us (4%)
    all_to_all x1, blocking collectives, on_device(): lax.all_to_all(partial, 'tensor', split_axis=0, concat_axis=0, tiled=True)  16 us
    all_to_all x1, blocking collectives, on_device(): lax.all_to_all(terms.reshape(owners // cores, 4 * cores, columns), 'dp',...  15.7 us
    all_to_all x1, starting transfers between devices, on_device(): lax.all_to_all(packed, 'dp', split_axis=0, concat_axis=0, tiled=True, axi...  13.5 us
    ppermute x1, starting transfers between devices, on_device(): down_first = lax.ppermute(down_own, ('dp', 'tensor'), first)  4.82 us
    pallas_call x5, Pallas kernels, call(): pl.pallas_call(kernel, out_shape=shapes, in_specs=[spec(i in in_hbm) for...  4 us
    dot_general x1, matrix products, on_device(): jnp.dot(tokens.reshape(rows, features), value_matrix, preferred_element_t...  2.92 us
    all_to_all x1, waiting for transfers between devices, on_device(): lax.all_to_all(packed, 'dp', split_axis=0, concat_axis=0, tiled=True, axi...  2.49 us
    ppermute x1, waiting for transfers between devices, on_device(): down_first = lax.ppermute(down_own, ('dp', 'tensor'), first)  2.29 us
  transfers between devices with their start and end apart: 4, of which 2 were waited for; matrix products, arithmetic and copies ran while one was open for 5% of the time, Pallas kernels for 0%

profile of v15, /device:TPU:2, one launch (start us, length us, event | category | flops | bytes accessed | tf_op | source)
XLA Modules:
  0.0 64.7 jit_solution(16392546890774866125)
XLA Ops:
  0.0 0.0 copy-start
  0.0 0.0 copy-start.2
  0.0 2.2 %shard_map.55 = bf16[32,2,4224]{2,1,0:T(2,128)(2,1)} custom-call(s32[2,64]{1,0:T(2,128)} %index_ref.3, bf16[2,64,8192]{2,1,0:T(8,128)(2,1)} %tokens_ref.1), custom_call_target="tpu_custom_call" | custom-call | bytes 2097664 | tf_op jit(solution)/shard_map/pallas_call | solution.py:198
  2.2 13.5 %all-to-all-start = ((bf16[32,2,4224]{2,1,0:T(2,128)(2,1)}), bf16[32,2,4224]{2,1,0:T(2,128)(2,1)S(1)}, u32[]{:S(2)}, u32[]{:S(2)}) async-start(bf16[32,2,4224]{2,1,0:T(2,128)(2,1)} %shard_map.55), calls=%async_computation | async-start | bytes 1081344 | tf_op jit(solution)/shard_map/all_to_all | solution.py:233
  15.7 0.0 copy-done.2
  15.7 0.2 copy.7.own_ref
  15.9 0.7 %collective-permute-start.1 = (bf16[1024,256]{1,0:T(8,128)(2,1)S(1)}, bf16[1024,256]{1,0:T(8,128)(2,1)S(1)}, u32[]{:S(2)}, u32[]{:S(2)}) collective-permute-start(bf16[1024,256]{1,0:T(8,128)(2,1)S(1)} %copy.7.own_ref), channel_id=1, source_target_pairs={{1,10},{3,12},{5,14},{7,8},{8,1},{10,3},{12,5},{14,7},{17,26},{19,... | collective-permute-start | bytes 1572872 | tf_op jit(solution)/shard_map/ppermute | solution.py:250
  16.6 4.8 %collective-permute-start = (bf16[1024,256]{1,0:T(8,128)(2,1)S(1)}, bf16[1024,256]{1,0:T(8,128)(2,1)S(1)}, u32[]{:S(2)}, u32[]{:S(2)}) collective-permute-start(bf16[1024,256]{1,0:T(8,128)(2,1)S(1)} %copy.7.own_ref), channel_id=1, source_target_pairs={{0,8},{1,0},{2,10},{3,2},{4,12},{5,4},{6,14},{7,6},{8,15},{9,1},{1... | collective-permute-start | bytes 1572872 | tf_op jit(solution)/shard_map/ppermute | solution.py:249
  21.5 0.0 copy-done
  21.5 1.9 %collective-permute-start.2 = (bf16[256,128]{1,0:T(8,128)(2,1)S(1)}, bf16[256,128]{1,0:T(8,128)(2,1)S(1)}, u32[]{:S(2)}, u32[]{:S(2)}) collective-permute-start(bf16[256,128]{1,0:T(8,128)(2,1)S(1)} %bitcast.12), channel_id=1, source_target_pairs={{0,8},{8,0},{16,24},{24,16},{32,40},{40,32},{48,56},{56,48},{64,72... | collective-permute-start | bytes 196616 | tf_op jit(solution)/shard_map/ppermute | solution.py:251
  23.4 0.0 copy-start.1
  23.4 2.9 %fusion.base_ref = f32[128,128]{1,0:T(8,128)S(1)} fusion(bf16[128,8192]{1,0:T(8,128)(2,1)} %bitcast.14, bf16[8192,128]{1,0:T(8,128)(2,1)} %param.6), kind=kOutput, calls=%fused_computation | convolution fusion | flops 268435456 | bytes 4259840 | tf_op jit(solution)/shard_map/dot_general | solution.py:253
  26.4 0.0 copy-done.1
  26.4 0.3 shard_map.56.place_ref
  26.6 0.0 collective-permute-done.2.up_other_ref
  26.7 0.0 collective-permute-done.1.second_ref
  26.7 2.3 %collective-permute-done.first_ref = bf16[1024,256]{1,0:T(8,128)(2,1)S(1)} collective-permute-done((bf16[1024,256]{1,0:T(8,128)(2,1)S(1)}, bf16[1024,256]{1,0:T(8,128)(2,1)S(1)}, u32[]{:S(2)}, u32[]{:S(2)}) %collective-permute-start) | collective-permute-done | bytes 524320 | tf_op jit(solution)/shard_map/ppermute | solution.py:249
  29.0 2.5 %all-to-all-done.received_ref = bf16[32,2,4224]{2,1,0:T(2,128)(2,1)S(1)} async-done(((bf16[32,2,4224]{2,1,0:T(2,128)(2,1)}), bf16[32,2,4224]{2,1,0:T(2,128)(2,1)S(1)}, u32[]{:S(2)}, u32[]{:S(2)}) %all-to-all-start) | async-done | bytes 540704 | tf_op jit(solution)/shard_map/all_to_all | solution.py:233
  31.5 0.4 shard_map.57
  31.9 16.0 %all_to_all.15.partial_ref = bf16[8,64,128]{2,1,0:T(8,128)(2,1)S(1)} all-to-all(bf16[8,64,128]{2,1,0:T(8,128)(2,1)S(1)} %get-tuple-element.21), channel_id=1, replica_groups=mesh['dp'=64,'tensor'=8] {'tensor'}, dimensions={0} | all-to-all | bytes 262144 | tf_op jit(solution)/shard_map/all_to_all | solution.py:265
  47.9 0.3 shard_map.58
  48.2 15.7 %all_to_all.16 = bf16[32,8,128]{2,1,0:T(8,128)(2,1)S(1)} all-to-all(bf16[32,8,128]{2,1,0:T(8,128)(2,1)S(1)} %bitcast.11), channel_id=1, replica_groups={{0,16,32,48,64,80,96,112,128,144,160,176,192,208,224,240,256,272,288,30..., dimensions={0} | all-to-all | bytes 131072 | tf_op jit(solution)/shard_map/all_to_all | solution.py:271
  63.9 0.8 %shard_map.59 = bf16[128,128]{1,0:T(8,128)(2,1)} custom-call(bf16[128,256]{1,0:T(8,128)(2,1)S(1)} %shard_map.56.place_ref, bf16[256,128]{1,0:T(8,128)(2,1)S(1)} %bitcast.10, f32[128,128]{1,0:T(8,128)S(1)} %fusion.base_ref), custom_call_target="tpu_custom_call" | custom-call | bytes 196608 | tf_op jit(solution)/shard_map/pallas_call | solution.py:198
Async XLA Ops:
  0.0 21.5 %copy-start = (bf16[4,64,128]{2,1,0:T(8,128)(2,1)S(1)}, bf16[4,64,128]{2,1,0:T(8,128)(2,1)}, u32[]{:S(2)}) copy-start(bf16[4,64,128]{2,1,0:T(8,128)(2,1)} %param.8) | copy-start | bytes 196612
  0.0 15.7 %copy-start.2 = (bf16[4,1024,64]{1,2,0:T(8,128)(2,1)S(1)}, bf16[4,1024,64]{1,2,0:T(8,128)(2,1)}, u32[]{:S(2)}) copy-start(bf16[4,1024,64]{1,2,0:T(8,128)(2,1)} %param.7) | copy-start | bytes 1572868
  2.2 29.2 %all-to-all-start = ((bf16[32,2,4224]{2,1,0:T(2,128)(2,1)}), bf16[32,2,4224]{2,1,0:T(2,128)(2,1)S(1)}, u32[]{:S(2)}, u32[]{:S(2)}) async-start(bf16[32,2,4224]{2,1,0:T(2,128)(2,1)} %shard_map.55), calls=%async_computation | async-start | bytes 1081344 | tf_op jit(solution)/shard_map/all_to_all | solution.py:233
  15.9 10.7 %collective-permute-start.1 = (bf16[1024,256]{1,0:T(8,128)(2,1)S(1)}, bf16[1024,256]{1,0:T(8,128)(2,1)S(1)}, u32[]{:S(2)}, u32[]{:S(2)}) collective-permute-start(bf16[1024,256]{1,0:T(8,128)(2,1)S(1)} %copy.7.own_ref), channel_id=1, source_target_pairs={{1,10},{3,12},{5,14},{7,8},{8,1},{10,3},{12,5},{14,7},{17,26},{19,... | collective-permute-start | bytes 1572872 | tf_op jit(solution)/shard_map/ppermute | solution.py:250
  16.6 12.3 %collective-permute-start = (bf16[1024,256]{1,0:T(8,128)(2,1)S(1)}, bf16[1024,256]{1,0:T(8,128)(2,1)S(1)}, u32[]{:S(2)}, u32[]{:S(2)}) collective-permute-start(bf16[1024,256]{1,0:T(8,128)(2,1)S(1)} %copy.7.own_ref), channel_id=1, source_target_pairs={{0,8},{1,0},{2,10},{3,2},{4,12},{5,4},{6,14},{7,6},{8,15},{9,1},{1... | collective-permute-start | bytes 1572872 | tf_op jit(solution)/shard_map/ppermute | solution.py:249
  21.5 5.2 %collective-permute-start.2 = (bf16[256,128]{1,0:T(8,128)(2,1)S(1)}, bf16[256,128]{1,0:T(8,128)(2,1)S(1)}, u32[]{:S(2)}, u32[]{:S(2)}) collective-permute-start(bf16[256,128]{1,0:T(8,128)(2,1)S(1)} %bitcast.12), channel_id=1, source_target_pairs={{0,8},{8,0},{16,24},{24,16},{32,40},{40,32},{48,56},{56,48},{64,72... | collective-permute-start | bytes 196616 | tf_op jit(solution)/shard_map/ppermute | solution.py:251
  23.4 2.9 %copy-start.1 = (s32[2,64]{1,0:T(2,128)S(1)}, s32[2,64]{1,0:T(2,128)}, u32[]{:S(2)}) copy-start(s32[2,64]{1,0:T(2,128)} %index_ref.3) | copy-start | bytes 1540
